TPU v7x, 128 devices: a whole 4x4x4 slice. The times are simulated.
128 devices in a mesh: seq: 4 (over y_lo, core), res: 32 (over y_hi, z, x).
Axes of the slice: x: 4, y: 4 (y_hi: 2, y_lo: 2; y = y_hi * 2 + y_lo), z: 4, core: 2. Of those that a mesh axis runs over, the one named last changes fastest.
Arguments:
- lineup_state: bfloat16 [16, 2048, 256], P('seq', 'res'), may hold values from -6 to 6
- couple_state: bfloat16 [2048, 2048, 128], P('seq', 'res'), may hold values from -6 to 6
- lineup_filled: int32 [16, 2048], P('seq', 'res'), may hold values 0 or 1
- observed_amino_flag: int32 [2048], replicated, may hold values 0 or 1
- horizontal_query_matrix: bfloat16 [256, 1024], replicated, may hold values from -0.375 to 0.375
- horizontal_final_matrix: bfloat16 [256, 256], replicated, may hold values from -0.375 to 0.375
- couple_offset_matrix: bfloat16 [128, 8], replicated, as said below
- vertical_query_matrix: bfloat16 [256, 1024], replicated, as said below
- vertical_final_matrix: bfloat16 [256, 256], replicated, may hold values from -0.375 to 0.375
- tensor_mean_side_matrix: bfloat16 [256, 64], replicated, may hold values from -0.375 to 0.375
- tensor_mean_final_matrix: bfloat16 [1024, 128], replicated, may hold values from -0.1875 to 0.1875
Outputs:
- alignment_output: bfloat16 [16, 2048, 256], P('seq', 'res')
- pair_output: bfloat16 [2048, 2048, 128], P('seq', 'res')
Inputs may be any that keep to these rules, and one draw needn't show every extreme that they name: `couple_offset_matrix`: pair-bias projection of pair features, one column a head. `vertical_query_matrix`: column attention projections: query, key, value and gate blocks of 256 columns each, heads in order within a block.
All inputs are finite; a program needn't handle non-finite values. No bound on the sum of `lineup_filled` on one device may be relied on, other than what follows from the above.
Results may differ from a plain program's by a relative error of at most 0.038.
The roundings to bfloat16 on the way count: a program that leaves them out, or rounds other values in their place, can miss the bound.
Values may be sent and summed in bfloat16 or wider, within the bound.
No kernel may reach another device: no remote copies, remote signals or barrier semaphores. Data moves between devices by JAX's collectives and lax.ppermute only.
A program may use at most 128 MiB of HBM per device.

v0:
```python
import math

import jax
import jax.numpy as jnp
from jax import lax
from jax.sharding import PartitionSpec as P


def standardize_features(values):
    data = values.astype(jnp.float32)
    centered = data - jnp.mean(data, axis=-1, keepdims=True)
    variance = jnp.mean(centered * centered, axis=-1, keepdims=True)
    return centered * lax.rsqrt(variance + 1e-05)


def column_core(queries, gating, key_vals, key_mask, head_count):
    feature_span = gating.shape[-1]
    head_dim = feature_span // head_count
    seq_keys, res_count = (key_vals.shape[0], key_vals.shape[1])
    seq_queries = queries.shape[0]
    keys = key_vals[..., :feature_span].reshape(seq_keys, res_count, head_count, head_dim)
    value_all = key_vals[..., feature_span:].reshape(seq_keys, res_count, head_count, head_dim)
    scores = jnp.einsum("qrhc,krhc->rhqk", queries, keys, preferred_element_type=jnp.float32)
    scores = jnp.where(key_mask.T[:, None, None, :] > 0, scores, -1000000000.0)
    highest = jnp.max(scores, axis=-1, keepdims=True)
    expo = jnp.exp(scores - highest)
    mixed = jnp.einsum(
        "rhqk,krhc->qrhc", expo.astype(jnp.bfloat16), value_all, preferred_element_type=jnp.float32
    )
    mixed = mixed / jnp.sum(expo, axis=-1).transpose(2, 0, 1)[..., None]
    return (gating * mixed.reshape(seq_queries, res_count, feature_span)).astype(jnp.bfloat16)


def split_projection(linear_map, feature_span, head_count, score_scale):
    lead = linear_map.shape[:2]
    queries = (
        (linear_map[..., :feature_span] * score_scale)
        .astype(jnp.bfloat16)
        .reshape(lead + (head_count, feature_span // head_count))
    )
    key_vals = linear_map[..., feature_span : 3 * feature_span].astype(jnp.bfloat16)
    gating = jax.nn.sigmoid(linear_map[..., 3 * feature_span :])
    return (queries, key_vals, gating)


def per_device(
    lineup_state,
    couple_state,
    lineup_filled,
    observed_amino_flag,
    horizontal_query_matrix,
    horizontal_final_matrix,
    couple_offset_matrix,
    vertical_query_matrix,
    vertical_final_matrix,
    tensor_mean_side_matrix,
    tensor_mean_final_matrix,
):
    homologs_each_device, amino_each_device, lineup_feature_count = lineup_state.shape
    pair_local_rows, pair_channel_width = (couple_state.shape[0], couple_state.shape[2])
    head_count = couple_offset_matrix.shape[1]
    feature_span = horizontal_final_matrix.shape[0]
    head_dim = feature_span // head_count
    outer_width = tensor_mean_side_matrix.shape[1] // 2
    score_scale = 1.0 / math.sqrt(head_dim)
    seq_index = lax.axis_index("seq")
    res_index = lax.axis_index("res")
    local_residues = lax.dynamic_slice_in_dim(
        observed_amino_flag, res_index * amino_each_device, amino_each_device
    )
    present_entries = (lineup_filled * local_residues[None, :]).astype(jnp.bfloat16)
    pair_normed = standardize_features(couple_state).astype(jnp.bfloat16)
    bias_local = jnp.dot(
        pair_normed.reshape(-1, pair_channel_width),
        couple_offset_matrix,
        preferred_element_type=jnp.float32,
    )
    bias_local = (
        bias_local.reshape(pair_local_rows, amino_each_device, head_count)
        .astype(jnp.bfloat16)
        .transpose(2, 0, 1)
    )
    bias_all = lax.all_gather(bias_local, "seq", axis=1, tiled=True)
    bias_mine = lax.all_to_all(bias_all, "res", split_axis=1, concat_axis=2, tiled=True)
    standardized_source = standardize_features(lineup_state).astype(jnp.bfloat16)
    linear_map = jnp.dot(
        standardized_source.reshape(-1, lineup_feature_count),
        horizontal_query_matrix,
        preferred_element_type=jnp.float32,
    ).reshape(homologs_each_device, amino_each_device, 4 * feature_span)
    queries, key_vals, gating = split_projection(linear_map, feature_span, head_count, score_scale)
    kv_part = lax.all_gather(key_vals, "res", axis=1, tiled=True)
    key_mask = lax.all_gather(present_entries, "res", axis=1, tiled=True)
    n_keys = kv_part.shape[1]
    keys = kv_part[..., :feature_span].reshape(homologs_each_device, n_keys, head_count, head_dim)
    value_part = kv_part[..., feature_span:].reshape(
        homologs_each_device, n_keys, head_count, head_dim
    )
    scores = jnp.einsum("sqhc,skhc->shqk", queries, keys, preferred_element_type=jnp.float32)
    scores = scores + bias_mine.astype(jnp.float32)[None]
    scores = jnp.where(key_mask[:, None, None, :] > 0, scores, -1000000000.0)
    running_max = jnp.full(
        (homologs_each_device, head_count, amino_each_device), -1e30, jnp.float32
    )
    new_max = jnp.maximum(running_max, jnp.max(scores, axis=-1))
    expo = jnp.exp(scores - new_max[..., None])
    running_sum = jnp.sum(expo, axis=-1)
    weighted = jnp.einsum(
        "shqk,skhc->shqc", expo.astype(jnp.bfloat16), value_part, preferred_element_type=jnp.float32
    )
    attended = (
        (weighted / running_sum[..., None])
        .transpose(0, 2, 1, 3)
        .reshape(homologs_each_device, amino_each_device, feature_span)
    )
    sigmoid_scaled = (gating * attended).astype(jnp.bfloat16)
    horizontal_increment = jnp.dot(
        sigmoid_scaled.reshape(-1, feature_span),
        horizontal_final_matrix,
        preferred_element_type=jnp.float32,
    ).reshape(homologs_each_device, amino_each_device, lineup_feature_count)
    single_homolog = (lineup_state.astype(jnp.float32) + horizontal_increment).astype(jnp.bfloat16)
    standardized_source = standardize_features(single_homolog).astype(jnp.bfloat16)
    column_entry_mask = lineup_filled.astype(jnp.bfloat16)
    linear_map = jnp.dot(
        standardized_source.reshape(-1, lineup_feature_count),
        vertical_query_matrix,
        preferred_element_type=jnp.float32,
    ).reshape(homologs_each_device, amino_each_device, 4 * feature_span)
    queries, key_vals, gating = split_projection(linear_map, feature_span, head_count, score_scale)
    all_kv, all_mask = (
        lax.all_gather(key_vals, "seq", axis=0, tiled=True),
        lax.all_gather(column_entry_mask, "seq", axis=0, tiled=True),
    )
    sigmoid_scaled = column_core(queries, gating, all_kv, all_mask, head_count)
    vertical_increment = jnp.dot(
        sigmoid_scaled.reshape(-1, feature_span),
        vertical_final_matrix,
        preferred_element_type=jnp.float32,
    ).reshape(homologs_each_device, amino_each_device, lineup_feature_count)
    alignment_output = (single_homolog.astype(jnp.float32) + vertical_increment).astype(
        jnp.bfloat16
    )
    standardized_source = standardize_features(alignment_output).astype(jnp.bfloat16)
    coupled_result = jnp.dot(
        standardized_source.reshape(-1, lineup_feature_count),
        tensor_mean_side_matrix,
        preferred_element_type=jnp.float32,
    ).reshape(homologs_each_device, amino_each_device, 2 * outer_width)
    coupled_result = (coupled_result * present_entries.astype(jnp.float32)[..., None]).astype(
        jnp.bfloat16
    )
    paired_all, live_all = (
        lax.all_gather(coupled_result, "seq", axis=0, tiled=True),
        lax.all_gather(present_entries, "seq", axis=0, tiled=True),
    )
    left_full, live_full = (
        lax.all_gather(paired_all[..., :outer_width], "res", axis=1, tiled=True),
        lax.all_gather(live_all, "res", axis=1, tiled=True),
    )
    seq_total = paired_all.shape[0]
    left_rows = lax.dynamic_slice_in_dim(left_full, seq_index * pair_local_rows, pair_local_rows, 1)
    live_rows = lax.dynamic_slice_in_dim(live_full, seq_index * pair_local_rows, pair_local_rows, 1)
    right_cols = paired_all[..., outer_width:]
    pair_count = jnp.dot(live_rows.T, live_all, preferred_element_type=jnp.float32)
    block_len = math.gcd(pair_local_rows, 128)
    n_blocks = pair_local_rows // block_len

    def outer_block(inputs):
        left_part, pair_part, count_part = inputs
        outer_sum = jnp.einsum(
            "sic,sjd->ijcd", left_part, right_cols, preferred_element_type=jnp.float32
        )
        outer_sum = outer_sum.reshape(
            block_len * amino_each_device, outer_width * outer_width
        ).astype(jnp.bfloat16)
        update = jnp.dot(
            outer_sum, tensor_mean_final_matrix, preferred_element_type=jnp.float32
        ).reshape(block_len, amino_each_device, pair_channel_width)
        update = update / jnp.maximum(count_part, 1.0)[..., None]
        return (pair_part.astype(jnp.float32) + update).astype(jnp.bfloat16)

    left_blocks = left_rows.reshape(seq_total, n_blocks, block_len, outer_width).transpose(
        1, 0, 2, 3
    )
    pair_output = lax.map(
        outer_block,
        (
            left_blocks,
            couple_state.reshape(n_blocks, block_len, amino_each_device, pair_channel_width),
            pair_count.reshape(n_blocks, block_len, amino_each_device),
        ),
    )
    return (
        alignment_output,
        pair_output.reshape(pair_local_rows, amino_each_device, pair_channel_width),
    )


def solution(mesh):
    return jax.shard_map(
        per_device,
        mesh=mesh,
        in_specs=(
            P("seq", "res", None),
            P("seq", "res", None),
            P("seq", "res"),
            P(),
            P(),
            P(),
            P(),
            P(),
            P(),
            P(),
            P(),
        ),
        out_specs=(P("seq", "res", None), P("seq", "res", None)),
        check_vma=False,
    )
```

profile of v0, /device:TPU:1, one launch (start us, length us, event | category | flops | bytes accessed | tf_op | source)
XLA Modules:
  0.0 559.4 jit_solution(10079175198850157705)
XLA Ops:
  7.2 7.9 %convert_reduce_fusion = f32[512,64]{1,0:T(8,128)S(1)} fusion(bf16[512,64,128]{2,1,0:T(8,128)(2,1)} %param.14), kind=kLoop, calls=%fused_computation.17 | loop fusion | flops 8355840 | bytes 8519680 | tf_op jit(solution)/shard_map/reduce_sum | solution.py:11
  15.2 12.1 %fusion.13 = f32[512,64]{1,0:T(8,128)S(1)} fusion(bf16[512,64,128]{2,1,0:T(8,128)(2,1)} %param.14, f32[512,64]{1,0:T(8,128)S(1)} %broadcast_multiply_fusion), kind=kLoop, calls=%fused_computation.20 | loop fusion | flops 16744448 | bytes 8650752 | tf_op jit(solution)/shard_map/reduce_sum | solution.py:12
  27.4 11.7 %fusion.28 = bf16[8,512,64]{2,0,1:T(8,128)(2,1)S(1)} fusion(bf16[512,64,128]{2,1,0:T(8,128)(2,1)S(1)} %bitcast.127, f32[512,64]{1,0:T(8,128)S(1)} %add_rsqrt_fusion, f32[512,64]{1,0:T(8,128)S(1)} %broadcast_multiply_fusion, bf16[128,8]{0,1:T(8,128)(2,1)S(1)} %copy-done.13), kind=kOutput, calls=%fused_computation.35 | convolution fusion | flops 84148224 | bytes 9177088 | tf_op jit(solution)/shard_map/dot_general | solution.py:73
  39.1 1.5 copy.102
  41.4 1.0 copy-done.4
  42.4 0.7 slice.95
  43.2 30.4 %all-gather.11.cloned.1.call-done = bf16[8,2048,64]{1,2,0:T(8,128)(2,1)} async-done(((bf16[8,512,64]{1,2,0:T(8,128)(2,1)}), bf16[8,2048,64]{1,2,0:T(8,128)(2,1)}) %all-gather.11.cloned.1.call-update) | async-done | bytes 2097168 | tf_op jit(solution)/shard_map/all_gather | solution.py:83
  73.5 5.6 %copy.103 = bf16[8,2048,64]{2,0,1:T(8,128)(2,1)} copy(bf16[8,2048,64]{1,2,0:T(8,128)(2,1)} %all-gather.11.cloned.1.call-done) | data formatting | bytes 4194304 | tf_op jit(solution)/shard_map/all_gather | solution.py:83
  79.2 7.9 %reshape.183 = bf16[32,2,16384]{2,1,0:T(2,128)(2,1)} reshape(bf16[2048,8,64]{2,1,0:T(8,128)(2,1)} %bitcast.129) | data formatting | bytes 4194304
  87.0 9.1 %all-to-all-start = ((bf16[32,2,16384]{2,1,0:T(2,128)(2,1)}), bf16[32,2,16384]{2,1,0:T(2,128)(2,1)S(1)}, u32[]{:S(2)}, u32[]{:S(2)}) async-start(bf16[32,2,16384]{2,1,0:T(2,128)(2,1)} %reshape.183), calls=%async_computation | async-start | bytes 4194304 | tf_op jit(solution)/shard_map/all_to_all | solution.py:84
  96.2 0.8 dynamic_slice.21
  97.0 95.2 %all-gather = bf16[32,64,4]{1,2,0:T(4,128)(2,1)S(1)} all-gather(bf16[1,64,4]{1,2,0:T(4,128)(2,1)S(1)} %bitcast.149), channel_id=1, replica_groups=mesh['seq'=4,'res'=32] {'res'}, dimensions={0}, use_global_device_ids=true | all-gather | bytes 16896 | tf_op jit(solution)/shard_map/all_gather | solution.py:93
  192.3 1.0 fusion.63
  193.5 4.0 reshape.184
  197.4 3.2 convert_bitcast_fusion
  200.6 8.3 %copy.104 = f32[8,64,32,64]{3,2,1,0:T(8,128)} copy(f32[8,64,32,64]{3,0,1,2:T(8,128)S(1)} %convert_bitcast_fusion) | data formatting | bytes 8388608 | tf_op jit(solution)/shard_map/convert_element_type | solution.py:100
  208.9 7.8 %reshape.160 = f32[8,64,2048]{2,1,0:T(8,128)} reshape(f32[8,64,32,64]{3,2,1,0:T(8,128)} %copy.104) | data formatting | bytes 8388608 | tf_op jit(solution)/shard_map/convert_element_type | solution.py:100
  216.7 5.8 %fusion.93 = (bf16[4,2048,256]{2,1,0:T(8,128)(2,1)}, bf16[4,2048,256]{2,1,0:T(8,128)(2,1)}) fusion(bf16[4,2048,512]{2,1,0:T(8,128)(2,1)} %all-gather.9.cloned.1.call-done), kind=kLoop, calls=%fused_computation.120 | loop fusion | bytes 16777216 | tf_op jit(solution)/shard_map/slice | solution.py:95
  222.5 6.3 %copy.105 = bf16[4,2048,256]{1,2,0:T(8,128)(2,1)} copy(bf16[4,2048,256]{2,1,0:T(8,128)(2,1)} %get-tuple-element.92) | data formatting | bytes 8388608 | tf_op jit(solution)/shard_map/slice | solution.py:96
  228.8 6.4 %copy.101 = bf16[4,2048,256]{1,2,0:T(8,128)(2,1)} copy(bf16[4,2048,256]{2,1,0:T(8,128)(2,1)} %get-tuple-element.91) | data formatting | bytes 8388608 | tf_op jit(solution)/shard_map/slice | solution.py:95
  235.2 5.2 fusion.15
  240.4 4.5 fusion.16
  245.0 7.4 %fusion.39 = f32[4,64,8,32]{1,3,2,0:T(8,128)} fusion(bf16[4,2048,8,32]{1,3,2,0:T(8,128)(2,1)} %bitcast.134, f32[4,8,64,2048]{3,2,1,0:T(8,128)S(1)} %get-tuple-element.99, f32[4,8,64]{2,1,0:T(8,128)S(1)} %broadcast_maximum_fusion, f32[8,64,2048]{2,1,0:T(8,128)} %reshape.160, pred[4,2048]{1,0:T(4,128)(4,1)S(1)} %bitcast.143, f32[4,64,8]{1,2,0:T(8,128)S(1)} %bitcast.148), kind=kOutput, calls=%fused_computation.47 | convolution fusion | flops 285278208 | bytes 25452544 | tf_op jit(solution)/shard_map/shqk,skhc->shqc/dot_general | solution.py:108
  252.3 1.2 copy.106
  253.6 1.2 fusion.96
  255.4 0.8 slice.94
  256.3 18.7 %all-gather.1 = bf16[4,4,64]{2,1,0:T(4,128)(2,1)S(1)} all-gather(bf16[1,4,64]{2,1,0:T(4,128)(2,1)S(1)} %get-tuple-element.97), channel_id=1, replica_groups=mesh['seq'=4,'res'=32] {'seq'}, dimensions={0}, use_global_device_ids=true | all-gather | bytes 2560 | tf_op jit(solution)/shard_map/all_gather | solution.py:133
  275.3 0.8 copy.111
  276.1 11.2 %all-gather.13.cloned.1.call-done = bf16[16,64,512]{2,1,0:T(8,128)(2,1)} async-done(((bf16[4,64,512]{2,1,0:T(8,128)(2,1)}), bf16[16,64,512]{2,1,0:T(8,128)(2,1)}) %all-gather.13.cloned.1.call-update) | async-done | bytes 1048592 | tf_op jit(solution)/shard_map/all_gather | solution.py:132
  287.3 1.3 fusion.94
  288.6 0.5 copy.129
  289.1 3.9 copy.113
  293.0 1.4 copy.130
  294.4 4.2 copy.112
  298.6 1.3 fusion.97
  299.9 1.3 fusion.42
  301.2 2.6 fusion.31
  303.9 0.7 copy.114
  304.7 1.2 convert_reduce_fusion.2
  306.5 5.9 %all_gather.32 = bf16[16,64,64]{2,1,0:T(8,128)(2,1)S(1)} all-gather(bf16[4,64,64]{2,1,0:T(8,128)(2,1)S(1)} %fusion.38), channel_id=1, replica_groups=mesh['seq'=4,'res'=32] {'seq'}, dimensions={0}, use_global_device_ids=true | all-gather | bytes 163840 | tf_op jit(solution)/shard_map/all_gather | solution.py:154
  312.3 0.8 fusion.95
  313.2 5.0 all-gather.2
  318.2 82.4 %all-gather.3 = bf16[32,64,16]{1,2,0:T(8,128)(2,1)S(1)} all-gather(bf16[1,64,16]{1,2,0:T(8,128)(2,1)S(1)} %bitcast.145), channel_id=1, replica_groups=mesh['seq'=4,'res'=32] {'res'}, dimensions={0}, use_global_device_ids=true | all-gather | bytes 67584 | tf_op jit(solution)/shard_map/all_gather | solution.py:159
  401.3 16.5 %all-gather.15.cloned.1.call-done = bf16[16,2048,32]{2,1,0:T(8,128)(2,1)} async-done(((bf16[16,64,32]{2,1,0:T(8,128)(2,1)}), bf16[16,2048,32]{2,1,0:T(8,128)(2,1)}) %all-gather.15.cloned.1.call-update) | async-done | bytes 2097168 | tf_op jit(solution)/shard_map/all_gather | solution.py:158
  417.8 1.7 constant_dynamic-slice_fusion.2
  419.5 0.9 copy.124
  420.8 130.8 %while.10 = (s32[]{:T(128)}, bf16[4,128,64,128]{3,2,1,0:T(8,128)(2,1)}, bf16[4,128,64,128]{3,2,1,0:T(8,128)(2,1)}, bf16[4,16,128,32]{2,1,3,0:T(8,128)(2,1)S(1)},...) while((s32[]{:T(128)}, ...), condition=%wide.region_13.14_spmd, body=%wide.region_12.13_spmd.sunk | while | flops 2428510208 | bytes 46825580 | solution.py:186
  421.1 1.8 constant_dynamic-slice_fusion.6
  422.9 8.1 %convolution_convert_fusion.2 = bf16[128,32,64,32]{0,2,3,1:T(8,128)(2,1)} fusion(bf16[16,64,32]{1,0,2:T(8,128)(2,1)S(1)} %get-tuple-element.169, bf16[4,16,128,32]{2,1,3,0:T(8,128)(2,1)S(1)} %get-tuple-element.168, s32[]{:T(128)S(6)} %copy.150), kind=kOutput, calls=%fused_computation.2.clone.1 | convolution fusion | flops 276824064 | bytes 17039364 | tf_op jit(solution)/shard_map/while/body/eval_jaxpr/sic,sjd->ijcd/dot_general | solution.py:171
  431.0 20.0 %fusion.114 = bf16[1,128,64,128]{3,1,2,0:T(8,128)(2,1)S(1)} fusion(f32[128,64]{0,1:T(8,128)S(1)} %maximum_bitcast_fusion.2, bf16[1,128,64,128]{3,2,1,0:T(8,128)(2,1)S(1)} %constant_dynamic-slice_fusion.6, bf16[128,64,1024]{0,1,2:T(8,128)(2,1)} %bitcast.124, bf16[1024,128]{1,0:T(8,128)(2,1)S(1)} %get-tuple-element.170), kind=kOutput, calls=%fused_computation.7.clone.1 | convolution fusion | flops 2151677952 | bytes 21266432 | tf_op jit(solution)/shard_map/while/body/eval_jaxpr/dot_general | solution.py:177
  451.0 2.7 copy_dynamic-update-slice_fusion.2
  453.7 1.8 constant_dynamic-slice_fusion.6
  455.5 8.1 %convolution_convert_fusion.2 = bf16[128,32,64,32]{0,2,3,1:T(8,128)(2,1)} fusion(bf16[16,64,32]{1,0,2:T(8,128)(2,1)S(1)} %get-tuple-element.169, bf16[4,16,128,32]{2,1,3,0:T(8,128)(2,1)S(1)} %get-tuple-element.168, s32[]{:T(128)S(6)} %copy.150), kind=kOutput, calls=%fused_computation.2.clone.1 | convolution fusion | flops 276824064 | bytes 17039364 | tf_op jit(solution)/shard_map/while/body/eval_jaxpr/sic,sjd->ijcd/dot_general | solution.py:171
  463.6 20.0 %fusion.114 = bf16[1,128,64,128]{3,1,2,0:T(8,128)(2,1)S(1)} fusion(f32[128,64]{0,1:T(8,128)S(1)} %maximum_bitcast_fusion.2, bf16[1,128,64,128]{3,2,1,0:T(8,128)(2,1)S(1)} %constant_dynamic-slice_fusion.6, bf16[128,64,1024]{0,1,2:T(8,128)(2,1)} %bitcast.124, bf16[1024,128]{1,0:T(8,128)(2,1)S(1)} %get-tuple-element.170), kind=kOutput, calls=%fused_computation.7.clone.1 | convolution fusion | flops 2151677952 | bytes 21266432 | tf_op jit(solution)/shard_map/while/body/eval_jaxpr/dot_general | solution.py:177
  483.6 2.7 copy_dynamic-update-slice_fusion.2
  486.3 1.8 constant_dynamic-slice_fusion.6
  488.1 8.1 %convolution_convert_fusion.2 = bf16[128,32,64,32]{0,2,3,1:T(8,128)(2,1)} fusion(bf16[16,64,32]{1,0,2:T(8,128)(2,1)S(1)} %get-tuple-element.169, bf16[4,16,128,32]{2,1,3,0:T(8,128)(2,1)S(1)} %get-tuple-element.168, s32[]{:T(128)S(6)} %copy.150), kind=kOutput, calls=%fused_computation.2.clone.1 | convolution fusion | flops 276824064 | bytes 17039364 | tf_op jit(solution)/shard_map/while/body/eval_jaxpr/sic,sjd->ijcd/dot_general | solution.py:171
  496.2 20.0 %fusion.114 = bf16[1,128,64,128]{3,1,2,0:T(8,128)(2,1)S(1)} fusion(f32[128,64]{0,1:T(8,128)S(1)} %maximum_bitcast_fusion.2, bf16[1,128,64,128]{3,2,1,0:T(8,128)(2,1)S(1)} %constant_dynamic-slice_fusion.6, bf16[128,64,1024]{0,1,2:T(8,128)(2,1)} %bitcast.124, bf16[1024,128]{1,0:T(8,128)(2,1)S(1)} %get-tuple-element.170), kind=kOutput, calls=%fused_computation.7.clone.1 | convolution fusion | flops 2151677952 | bytes 21266432 | tf_op jit(solution)/shard_map/while/body/eval_jaxpr/dot_general | solution.py:177
  516.2 2.7 copy_dynamic-update-slice_fusion.2
  519.0 1.8 constant_dynamic-slice_fusion.6
  520.7 8.1 %convolution_convert_fusion.2 = bf16[128,32,64,32]{0,2,3,1:T(8,128)(2,1)} fusion(bf16[16,64,32]{1,0,2:T(8,128)(2,1)S(1)} %get-tuple-element.169, bf16[4,16,128,32]{2,1,3,0:T(8,128)(2,1)S(1)} %get-tuple-element.168, s32[]{:T(128)S(6)} %copy.150), kind=kOutput, calls=%fused_computation.2.clone.1 | convolution fusion | flops 276824064 | bytes 17039364 | tf_op jit(solution)/shard_map/while/body/eval_jaxpr/sic,sjd->ijcd/dot_general | solution.py:171
  528.9 20.0 %fusion.114 = bf16[1,128,64,128]{3,1,2,0:T(8,128)(2,1)S(1)} fusion(f32[128,64]{0,1:T(8,128)S(1)} %maximum_bitcast_fusion.2, bf16[1,128,64,128]{3,2,1,0:T(8,128)(2,1)S(1)} %constant_dynamic-slice_fusion.6, bf16[128,64,1024]{0,1,2:T(8,128)(2,1)} %bitcast.124, bf16[1024,128]{1,0:T(8,128)(2,1)S(1)} %get-tuple-element.170), kind=kOutput, calls=%fused_computation.7.clone.1 | convolution fusion | flops 2151677952 | bytes 21266432 | tf_op jit(solution)/shard_map/while/body/eval_jaxpr/dot_general | solution.py:177
  548.9 2.7 copy_dynamic-update-slice_fusion.2
  551.6 1.0 copy-done.1
  (82 shorter events, 4.0 us)
Async XLA Ops:
  7.2 33.9 %copy-start = (bf16[256,1024]{1,0:T(8,128)(2,1)S(1)}, bf16[256,1024]{1,0:T(8,128)(2,1)}, u32[]{:S(2)}) copy-start(bf16[256,1024]{1,0:T(8,128)(2,1)} %param.17) | copy-start | bytes 1572868
  7.2 20.2 %copy-start.13 = (bf16[128,8]{0,1:T(8,128)(2,1)S(1)}, bf16[128,8]{0,1:T(8,128)(2,1)}, u32[]{:S(2)}) copy-start(bf16[128,8]{0,1:T(8,128)(2,1)} %param.19) | copy-start | bytes 6148
  7.2 66.4 %all-gather.11.cloned.1.call-start = ((), (), s32[]{:S(2)}) async-start(), calls=%async_computation.2 | async-start | bytes 2621440 | tf_op jit(solution)/shard_map/all_gather | solution.py:83
  7.2 20.1 %slice-start = ((s8[8388608]{0:T(1024)(128)(4,1)}), s8[4194304]{0:T(1024)(128)(4,1)S(1)}, s32[]{:S(2)}) async-start(s8[8388608]{0:T(1024)(128)(4,1)} %bitcast.126), calls=%async_computation.5 | async-start | bytes 8388608
  15.2 12.2 %slice-start.1 = ((s8[8388608]{0:T(1024)(128)(4,1)}), s8[4194304]{0:T(1024)(128)(4,1)S(1)}, s32[]{:S(2)}) async-start(s8[8388608]{0:T(1024)(128)(4,1)} %bitcast.126), calls=%async_computation.6 | async-start | bytes 8388608
  27.4 13.3 %copy-start.5 = (bf16[4,64,256]{2,1,0:T(8,128)(2,1)S(1)}, bf16[4,64,256]{2,1,0:T(8,128)(2,1)}, u32[]{:S(2)}) copy-start(bf16[4,64,256]{2,1,0:T(8,128)(2,1)} %param.13) | copy-start | bytes 393220
  40.7 176.0 %all-gather.9.cloned.1.call-start = ((), (), s32[]{:S(2)}) async-start(), calls=%async_computation.1 | async-start | bytes 8650752 | tf_op jit(solution)/shard_map/all_gather | solution.py:92
  41.4 1.0 copy-start.4
  43.2 53.8 %copy-start.8 = (s32[4,64]{1,0:T(4,128)S(1)}, s32[4,64]{1,0:T(4,128)}, u32[]{:S(2)}) copy-start(s32[4,64]{1,0:T(4,128)} %param.15) | copy-start | bytes 3076
  87.0 106.4 %all-to-all-start = ((bf16[32,2,16384]{2,1,0:T(2,128)(2,1)}), bf16[32,2,16384]{2,1,0:T(2,128)(2,1)S(1)}, u32[]{:S(2)}, u32[]{:S(2)}) async-start(bf16[32,2,16384]{2,1,0:T(2,128)(2,1)} %reshape.183), calls=%async_computation | async-start | bytes 4194304 | tf_op jit(solution)/shard_map/all_to_all | solution.py:84
  96.2 191.2 %all-gather.13.cloned.1.call-start = ((), (), s32[]{:S(2)}) async-start(), calls=%async_computation.3 | async-start | bytes 1310720 | tf_op jit(solution)/shard_map/all_gather | solution.py:132
  235.2 5.2 copy-start.2
  245.0 8.6 %copy-start.10 = (bf16[256,256]{1,0:T(8,128)(2,1)S(1)}, bf16[256,256]{1,0:T(8,128)(2,1)}, u32[]{:S(2)}) copy-start(bf16[256,256]{1,0:T(8,128)(2,1)} %param.18) | copy-start | bytes 393220
  245.0 10.1 %copy-start.6 = (bf16[256,1024]{1,0:T(8,128)(2,1)S(1)}, bf16[256,1024]{1,0:T(8,128)(2,1)}, u32[]{:S(2)}) copy-start(bf16[256,1024]{1,0:T(8,128)(2,1)} %param.20) | copy-start | bytes 1572868
  255.4 33.2 %copy-start.3 = (f32[4,64,1024]{2,1,0:T(8,128)}, f32[4,64,1024]{2,1,0:T(8,128)S(1)}, u32[]{:S(2)}) copy-start(f32[4,64,1024]{2,1,0:T(8,128)S(1)} %fusion.45) | copy-start | bytes 3145732
  256.3 161.5 %all-gather.15.cloned.1.call-start = ((), (), s32[]{:S(2)}) async-start(), calls=%async_computation.4 | async-start | bytes 8650752 | tf_op jit(solution)/shard_map/all_gather | solution.py:158
  299.8 4.9 copy-start.11
  299.8 6.4 %copy-start.12 = (bf16[256,64]{0,1:T(8,128)(2,1)S(1)}, bf16[256,64]{0,1:T(8,128)(2,1)}, u32[]{:S(2)}) copy-start(bf16[256,64]{0,1:T(8,128)(2,1)} %param.22) | copy-start | bytes 98308
  303.8 116.9 %copy-start.9 = (bf16[1024,128]{1,0:T(8,128)(2,1)S(1)}, bf16[1024,128]{1,0:T(8,128)(2,1)}, u32[]{:S(2)}) copy-start(bf16[1024,128]{1,0:T(8,128)(2,1)} %param.23) | copy-start | bytes 786436
  306.0 114.8 %copy-start.7 = (bf16[4,64,256]{2,1,0:T(8,128)(2,1)}, bf16[4,64,256]{2,1,0:T(8,128)(2,1)S(1)}, u32[]{:S(2)}) copy-start(bf16[4,64,256]{2,1,0:T(8,128)(2,1)S(1)} %get-tuple-element.105) | copy-start | bytes 393220
  551.6 1.0 copy-start.1
Sparse Core Ops, SparseCore 0:
  40.8 32.7 all-gather.10
  76.6 121.4 all-gather.8
  256.4 30.9 all-gather.12
  313.3 104.4 all-gather.14
where the time goes:
time: 568 us; the launch traced here: 559 us
  blocking collectives  207 us (36%)
  matrix products  144 us (25%)
  local copies, waits for them, and re-layouts  94.7 us (17%)
  waiting for transfers between devices  58.2 us (10%)
  other arithmetic  30.9 us (5%)
  between operations  14.5 us (3%)
  starting transfers between devices  9.28 us (2%)
    all_gather x1, blocking collectives, per_device(): key_mask = lax.all_gather(present_entries, 'res', axis=1, tiled=True)  95.2 us
    all_gather x1, blocking collectives, per_device(): lax.all_gather(live_all, 'res', axis=1, tiled=True)  82.4 us
    dot_general x4, matrix products, outer_block(): jnp.dot(outer_sum, tensor_mean_final_matrix, preferred_element_type=jnp.f...  80 us
    dot_general x4, matrix products, outer_block(): jnp.einsum('sic,sjd->ijcd', left_part, right_cols, preferred_element_type...  32.5 us
    all_gather x1, waiting for transfers between devices, per_device(): bias_all = lax.all_gather(bias_local, 'seq', axis=1, tiled=True)  30.4 us
    all_gather x1, blocking collectives, per_device(): lax.all_gather(column_entry_mask, 'seq', axis=0, tiled=True)  18.7 us
    all_gather x1, waiting for transfers between devices, per_device(): lax.all_gather(paired_all[..., :outer_width], 'res', axis=1, tiled=True)  16.5 us
    convert_element_type x2, local copies, waits for them, and re-layouts, per_device(): scores = scores + bias_mine.astype(jnp.float32)[None]  16.1 us
  transfers between devices with their start and end apart: 5, of which 3 were waited for; matrix products, arithmetic and copies ran while one was open for 7% of the time, Pallas kernels for 0%

commit v1 on v0

v1 whole, which is shorter than its diff:
```python
import math

import jax
import jax.numpy as jnp
import numpy as np
from jax import lax
from jax.experimental import pallas as pl
from jax.experimental.pallas import tpu as pltpu
from jax.sharding import Mesh, PartitionSpec as P

F32 = jnp.float32
BF16 = jnp.bfloat16

AXES = ("yl", "co", "yh", "zh", "zl", "x")
SIZES = (2, 2, 2, 2, 2, 4)
SEQ = ("yl", "co")
RES = ("yh", "zh", "zl", "x")
SWAPPED = ("yl", "co", "yh", "zh")
COLUMN = ("yh", "zh")
NEAR = ("zl", "x")

SEQS = 4
BLOCK = 64
ROWS = 512
WIDTH = 256
HEADS = 8
HEAD_DIM = 32
ALL_SEQS = 16
OUTER = 32
PAIR = 128
LEFT = ALL_SEQS * OUTER
CHUNK = SEQS * BLOCK + 8
MASKED = -1000000000.0
OTHER = -2000000000.0

NT = (((1,), (1,)), ((), ()))


def swap_pairs():
    pairs = []
    for spot in np.ndindex(2, 2, 2, 2):
        target = (spot[2], spot[3], spot[0], spot[1])
        pairs.append(
            (int(np.ravel_multi_index(spot, (2, 2, 2, 2))), int(np.ravel_multi_index(target, (2, 2, 2, 2))))
        )
    return pairs


def swap(array):
    return lax.ppermute(array, SWAPPED, swap_pairs())


def shift(array, axis, size, step):
    return lax.ppermute(array, axis, [(i, (i + step) % size) for i in range(size)])


def dot(a, b, dims=(((1,), (0,)), ((), ()))):
    return lax.dot_general(a, b, dims, preferred_element_type=F32)


def norm(data):
    centered = data - jnp.mean(data, axis=-1, keepdims=True)
    variance = jnp.mean(centered * centered, axis=-1, keepdims=True)
    return centered * lax.rsqrt(variance + 1e-05)


def iota(shape, dim):
    return lax.broadcasted_iota(jnp.int32, shape, dim)


def pack_body(block_ref, x_ref, filled_ref, flag_ref, out_ref):
    rows = SEQS * BLOCK
    out_ref[:rows, :] = x_ref[...]
    filled = filled_ref[...].astype(F32)
    live = filled * flag_ref[pl.ds(block_ref[0], 1), :].astype(F32)
    lines = [jnp.concatenate([part[i : i + 1] for i in range(SEQS)], axis=1) for part in (filled, live)]
    lines.append(jnp.zeros((6, WIDTH), F32))
    out_ref[rows:, :] = jnp.concatenate(lines, axis=0).astype(BF16)


def pack_chunk(block, lineup_state, lineup_filled, flags):
    vmem = pl.BlockSpec(memory_space=pltpu.VMEM)
    return pl.pallas_call(
        pack_body,
        in_specs=[pl.BlockSpec(memory_space=pltpu.SMEM), vmem, vmem, vmem],
        out_specs=vmem,
        out_shape=jax.ShapeDtypeStruct((CHUNK, WIDTH), BF16),
        name="pack_lineup",
    )(block, lineup_state.reshape(SEQS * BLOCK, WIDTH), lineup_filled, flags.reshape(-1, BLOCK))


GATHERED = 16


def norm_body(x_ref, out_ref, *send_refs):
    rows = SEQS * BLOCK
    normed = norm(x_ref[:rows, :].astype(F32)).astype(BF16)
    for r, part in ((slice(0, rows), normed), (slice(rows, CHUNK), x_ref[rows:, :])):
        out_ref[r, :] = part
        for half, send in enumerate(send_refs):
            for k in range(GATHERED):
                send[k, r, :] = part[:, half * 128 : (half + 1) * 128]


def norm_chunk(chunk):
    send = jax.ShapeDtypeStruct((GATHERED, CHUNK, 128), BF16)
    return pl.pallas_call(
        norm_body,
        out_shape=[jax.ShapeDtypeStruct((CHUNK, WIDTH), BF16), send, send],
        name="norm_lineup",
    )(chunk)


BIAS_STEP = 256
BIAS_PARTS = 2
GROUP = 32
COPIES = 4


def bias_body(pair_ref, weight_ref, out_ref, spread, normed):
    @pl.when(pl.program_id(0) == 0)
    def _():
        wide = weight_ref[...]
        owner = iota((PAIR, WIDTH), 1) // HEADS

        def place(i, carry):
            spread[pl.ds(pl.multiple_of(i * PAIR, PAIR), PAIR), :] = jnp.where(
                owner == i, wide, jnp.zeros_like(wide)
            )
            return carry

        lax.fori_loop(0, GROUP, place, 0)

    groups = BIAS_STEP // GROUP
    cols = BLOCK // BIAS_PARTS
    ones = jnp.ones((PAIR, PAIR), BF16)

    def one(i, carry):
        for g in range(groups):
            raw = pair_ref[g * GROUP + i]
            centered = raw.astype(F32) - dot(raw, ones) * (1.0 / PAIR)
            variance = jnp.mean(centered * centered, axis=-1, keepdims=True)
            normed[g * cols : (g + 1) * cols, pl.ds(pl.multiple_of(i * PAIR, PAIR), PAIR)] = (
                centered * lax.rsqrt(variance + 1e-05)
            ).astype(BF16)
        return carry

    lax.fori_loop(0, GROUP, one, 0, unroll=8)
    result = dot(normed[...], spread[...]).astype(BF16)
    for g in range(groups):
        for c in range(COPIES):
            out_ref[c, g // 2, :, (g % 2) * WIDTH : (g % 2 + 1) * WIDTH] = result[g * cols : (g + 1) * cols]


def bias_blocks(couple_state, couple_offset_matrix, part):
    wide = jnp.tile(couple_offset_matrix, (1, GROUP))
    per_step = BIAS_STEP // BLOCK
    cols = BLOCK // BIAS_PARTS
    return pl.pallas_call(
        bias_body,
        grid=(ROWS // BIAS_STEP,),
        in_specs=[
            pl.BlockSpec((BIAS_STEP, cols, PAIR), lambda i: (i, part, 0)),
            pl.BlockSpec((PAIR, WIDTH), lambda i: (0, 0)),
        ],
        out_specs=pl.BlockSpec((COPIES, per_step, cols, BLOCK * HEADS), lambda i: (0, i, 0, 0)),
        out_shape=jax.ShapeDtypeStruct((COPIES, ROWS // BLOCK, cols, BLOCK * HEADS), BF16),
        scratch_shapes=[
            pltpu.VMEM((GROUP * PAIR, WIDTH), BF16),
            pltpu.VMEM((BIAS_STEP // GROUP * cols, GROUP * PAIR), BF16),
        ],
        compiler_params=pltpu.CompilerParams(vmem_limit_bytes=56 << 20),
        cost_estimate=pl.CostEstimate(flops=8 << 30, bytes_accessed=6 << 20, transcendentals=0),
        name="pair_bias",
    )(couple_state, wide)


KEY_TILE = 256
KEYS = 2048
QH = BLOCK * HEADS


def row_body(
    core_ref, own_ref, x_ref, n0_ref, n1_ref, f0_ref, f1_ref, m0_ref, m1_ref, m2_ref, m3_ref, *refs
):
    bias_refs = refs[:BIAS_PARTS]
    wq_ref, wk_ref, wvt_ref, wg_ref, wo_ref, out_ref, scores, values, live = refs[BIAS_PARTS:]
    s = pl.program_id(0)
    core = core_ref[0]

    @pl.when(s == 0)
    def _():
        out_ref[SEQS * BLOCK :, :] = x_ref[SEQS * BLOCK :, :]
        for side, half, ref in ((0, 0, m0_ref), (0, 1, m1_ref), (1, 0, m2_ref), (1, 1, m3_ref)):
            lanes = ref[...].astype(F32)[:, 1, :]
            live[half * 128 : (half + 1) * 128, side * 128 : side * 128 + 16] = lanes.T

    rows = pl.ds(pl.multiple_of(s * BLOCK, BLOCK), BLOCK)
    mine = own_ref[rows, :]
    queries = (dot(mine, wq_ref[...]) * (1.0 / math.sqrt(HEAD_DIM))).astype(BF16).astype(F32)
    head_rows = (iota((BLOCK, HEADS, WIDTH), 2) // HEAD_DIM) == iota((BLOCK, HEADS, WIDTH), 1)
    spread = (
        jnp.where(head_rows, jnp.broadcast_to(queries[:, None, :], (BLOCK, HEADS, WIDTH)), 0.0)
        .reshape(QH, WIDTH)
        .astype(BF16)
    )
    top = jnp.full((8, QH), -3e38, F32)
    per_tile = KEY_TILE // BLOCK
    cols = BLOCK // BIAS_PARTS
    for side, halves in enumerate(((n0_ref, n1_ref), (f0_ref, f1_ref))):
        owner = core if side == 0 else 1 - core
        mask_rows = live[pl.ds(pl.multiple_of(s * BLOCK, BLOCK), BLOCK), side * 128 : side * 128 + 16]
        for t in range(16 // per_tile):
            first = t * per_tile
            tile = jnp.concatenate(
                [ref[first : first + per_tile].reshape(KEY_TILE, 128) for ref in halves], axis=1
            )
            keys = dot(tile, wk_ref[...]).astype(BF16)
            spot = side * (KEYS // 2) + first * BLOCK
            values[:, spot : spot + KEY_TILE] = dot(wvt_ref[...], tile, NT).astype(BF16)
            start = (first // 8) * 16 + owner * 8 + first % 8
            bias = jnp.concatenate(
                [ref[start + b] for b in range(per_tile) for ref in bias_refs], axis=0
            ).astype(F32)
            product = dot(keys, spread, NT) + bias
            alive = jnp.concatenate(
                [mask_rows[:, first + b : first + b + 1] for b in range(per_tile)], axis=0
            )
            product = jnp.where(alive > 0.0, product, MASKED)
            scores[spot : spot + KEY_TILE, :] = product
            top = jnp.maximum(top, jnp.max(product.reshape(KEY_TILE // 8, 8, QH), axis=0))
    highest = jnp.max(top, axis=0, keepdims=True)
    total = jnp.zeros((8, QH), F32)
    mixed = jnp.zeros((WIDTH, QH), F32)
    for t in range(KEYS // KEY_TILE):
        expo = jnp.exp(scores[t * KEY_TILE : (t + 1) * KEY_TILE, :] - highest)
        total = total + jnp.sum(expo.reshape(KEY_TILE // 8, 8, QH), axis=0)
        mixed = mixed + dot(values[:, t * KEY_TILE : (t + 1) * KEY_TILE], expo.astype(BF16))
    mixed = mixed / jnp.sum(total, axis=0, keepdims=True)
    picked = jnp.where(head_rows, mixed.T.reshape(BLOCK, HEADS, WIDTH), 0.0)
    attended = jnp.sum(picked, axis=1)
    gate = jax.nn.sigmoid(dot(mine, wg_ref[...]))
    added = dot((gate * attended).astype(BF16), wo_ref[...])
    out_ref[rows, :] = (x_ref[rows, :].astype(F32) + added).astype(BF16)


def row_attention(core, own, x, near, far, biases, query_matrix, final_matrix):
    wq, wk, wv, wg = (query_matrix[:, i * WIDTH : (i + 1) * WIDTH] for i in range(4))
    whole = lambda shape: pl.BlockSpec(shape, lambda s: (0,) * len(shape))
    gathered = pl.BlockSpec((GATHERED, BLOCK, 128), lambda s: (0, s, 0))
    masks = pl.BlockSpec((GATHERED, 8, 128), lambda s: (0, SEQS * BLOCK // 8, 0))
    square = whole((WIDTH, WIDTH))
    return pl.pallas_call(
        row_body,
        grid=(SEQS,),
        in_specs=[
            pl.BlockSpec(memory_space=pltpu.SMEM),
            whole((CHUNK, WIDTH)),
            whole((CHUNK, WIDTH)),
            *([gathered] * 4),
            *([masks] * 4),
            *([whole((KEYS // BLOCK, BLOCK // BIAS_PARTS, QH))] * BIAS_PARTS),
            square,
            square,
            square,
            square,
            square,
        ],
        out_specs=whole((CHUNK, WIDTH)),
        out_shape=jax.ShapeDtypeStruct((CHUNK, WIDTH), BF16),
        scratch_shapes=[
            pltpu.VMEM((KEYS, QH), F32),
            pltpu.VMEM((WIDTH, KEYS), BF16),
            pltpu.VMEM((WIDTH, 256), F32),
        ],
        compiler_params=pltpu.CompilerParams(vmem_limit_bytes=48 << 20),
        cost_estimate=pl.CostEstimate(flops=16 << 30, bytes_accessed=8 << 20, transcendentals=4 << 20),
        name="row_attention",
    )(core, own, x, *near, *far, *near, *far, *biases, wq, wk, wv.T, wg, final_matrix)


PART = 16
PART_ROWS = ALL_SEQS * PART
SIDE = LEFT + 128


def column_body(
    mine_ref, x0_ref, x1_ref, x2_ref, x3_ref, w_ref, wo_ref, left_ref, right_ref, out_ref, a_ref, b_ref, masks,
):
    x_refs = (x0_ref, x1_ref, x2_ref, x3_ref)
    mine = mine_ref[0]
    for b in range(4):
        lanes = x_refs[b][SEQS * BLOCK :, :].astype(F32)
        masks[:, b * 128 : b * 128 + 8] = lanes.T
    one_row = iota((PART_ROWS, PART_ROWS), 0)
    one_col = iota((PART_ROWS, PART_ROWS), 1)
    same = (one_row % PART) == (one_col % PART)

    def sequence(shape):
        slot = iota(shape, 0) // PART
        return ((slot // SEQS) ^ mine) * SEQS + slot % SEQS

    keep = iota((PART_ROWS, LEFT), 1) % ALL_SEQS == sequence((PART_ROWS, LEFT))
    keep_flag = iota((PART_ROWS, 128), 1) == sequence((PART_ROWS, 128))
    lane_head = iota((PART_ROWS, WIDTH), 1) // HEAD_DIM
    for g in range(BLOCK // PART):
        spots = [(s // SEQS, (s % SEQS) * BLOCK + g * PART) for s in range(ALL_SEQS)]
        data = jnp.concatenate([x_refs[b][r : r + PART, :] for b, r in spots], axis=0).astype(F32)
        filled = jnp.concatenate([masks[r : r + PART, b * 128 : b * 128 + 1] for b, r in spots], axis=0)
        live = jnp.concatenate([masks[r : r + PART, b * 128 + 1 : b * 128 + 2] for b, r in spots], axis=0)
        filled_lane = jnp.broadcast_to(filled, (PART_ROWS, 128)).T[0:1, :]
        fill = jnp.where(same, MASKED, OTHER)
        use = jnp.logical_and(same, jnp.broadcast_to(filled_lane, (PART_ROWS, PART_ROWS)) > 0.0)
        line = dot(norm(data).astype(BF16), w_ref[...])
        queries = (line[:, :WIDTH] * (1.0 / math.sqrt(HEAD_DIM))).astype(BF16)
        keys = line[:, WIDTH : 2 * WIDTH].astype(BF16)
        value = line[:, 2 * WIDTH : 3 * WIDTH].astype(BF16)
        gate = jax.nn.sigmoid(line[:, 3 * WIDTH :])
        mixed = jnp.zeros((PART_ROWS, WIDTH), F32)
        for h in range(HEADS):
            head = lane_head == h
            product = dot(jnp.where(head, queries, jnp.zeros_like(queries)), keys, NT)
            product = jnp.where(use, product, fill)
            expo = jnp.exp(product - jnp.max(product, axis=1, keepdims=True))
            total = jnp.sum(expo, axis=1, keepdims=True)
            mixed = mixed + jnp.where(head, dot(expo.astype(BF16), value) / total, 0.0)
        result = (data + dot((gate * mixed).astype(BF16), wo_ref[...])).astype(BF16)
        for s in range(SEQS):
            out_ref[s * BLOCK + g * PART : s * BLOCK + (g + 1) * PART, :] = result[s * PART : (s + 1) * PART]
        normed = norm(result.astype(F32)).astype(BF16)
        flags = jnp.where(keep_flag, jnp.broadcast_to(live, (PART_ROWS, 128)), 0.0)
        flags = jnp.sum(flags.reshape(ALL_SEQS, PART, 128), axis=0).astype(BF16)
        for weight_ref, out in ((left_ref, a_ref), (right_ref, b_ref)):
            wide = (dot(normed, weight_ref[...]) * live).astype(BF16).astype(F32)
            wide = jnp.where(keep, wide, 0.0)
            wide = jnp.sum(wide.reshape(ALL_SEQS, PART, LEFT), axis=0).astype(BF16)
            for k in range(out.shape[0]):
                out[k, g * PART : (g + 1) * PART, :LEFT] = wide
                out[k, g * PART : (g + 1) * PART, LEFT:] = flags


def column_attention(mine, rows, query_matrix, final_matrix, side_matrix):
    left = jnp.repeat(side_matrix[:, :OUTER], ALL_SEQS, axis=1)
    right = jnp.repeat(side_matrix[:, OUTER:], ALL_SEQS, axis=1)
    vmem = pl.BlockSpec(memory_space=pltpu.VMEM)
    return pl.pallas_call(
        column_body,
        in_specs=[pl.BlockSpec(memory_space=pltpu.SMEM)] + [vmem] * 8,
        out_specs=[vmem] * 3,
        out_shape=[
            jax.ShapeDtypeStruct((SEQS * BLOCK, WIDTH), BF16),
            jax.ShapeDtypeStruct((8, BLOCK, SIDE), BF16),
            jax.ShapeDtypeStruct((1, BLOCK, SIDE), BF16),
        ],
        scratch_shapes=[pltpu.VMEM((WIDTH, 512), F32)],
        compiler_params=pltpu.CompilerParams(vmem_limit_bytes=48 << 20),
        cost_estimate=pl.CostEstimate(flops=4 << 30, bytes_accessed=3 << 20, transcendentals=2 << 20),
        name="column_attention",
    )(mine, *rows, query_matrix, final_matrix, left, right)


PAIR_STEP = 128
WIDE = BLOCK * PAIR
STRIDE = BLOCK + 8


def pair_body(a_ref, b_ref, w_ref, pair_ref, out_ref, table, update):
    @pl.when(pl.program_id(0) == 0)
    def _():
        keep = (iota((16 * ALL_SEQS, LEFT), 1) % ALL_SEQS) == (iota((16 * ALL_SEQS, LEFT), 0) % ALL_SEQS)
        fold = (iota((LEFT, 128), 0) // ALL_SEQS == iota((LEFT, 128), 1)).astype(BF16)

        def build(q, carry):
            rows = b_ref[pl.ds(pl.multiple_of(q * 16, 16), 16), :LEFT].astype(F32)
            rows = jnp.broadcast_to(rows[:, None, :], (16, ALL_SEQS, LEFT)).reshape(16 * ALL_SEQS, LEFT)
            right = dot(jnp.where(keep, rows, 0.0).astype(BF16), fold).astype(BF16)
            for c in range(OUTER // 2):
                part = dot(right, w_ref[:, c * 256 : (c + 1) * 256]).astype(BF16)
                for j in range(16):
                    lanes = pl.ds(pl.multiple_of((q * 16 + j) * PAIR, PAIR), PAIR)
                    for d in range(2):
                        table[(2 * c + d) * 16 : (2 * c + d + 1) * 16, lanes] = part[
                            j * 16 : (j + 1) * 16, d * PAIR : (d + 1) * PAIR
                        ]
            return carry

        lax.fori_loop(0, BLOCK // 16, build, 0)

    left = a_ref[:, :LEFT]
    count = dot(a_ref[:, LEFT:], b_ref[:, LEFT:], NT)
    scale = 1.0 / jnp.maximum(count, 1.0)
    per_dot = 4
    for j in range(0, BLOCK, per_dot):
        part = dot(left, table[:, j * PAIR : (j + per_dot) * PAIR])
        for d in range(per_dot):
            update[pl.ds(j + d, PAIR_STEP, stride=STRIDE), :] = (
                part[:, d * PAIR : (d + 1) * PAIR] * scale[:, j + d : j + d + 1]
            )

    def finish(i, carry):
        rows = update[pl.ds(pl.multiple_of(i * STRIDE, 8), BLOCK), :]
        out_ref[i] = (pair_ref[i].astype(F32) + rows).astype(BF16)
        return carry

    lax.fori_loop(0, PAIR_STEP, finish, 0, unroll=4)


def pair_update(left, right, final_matrix, couple_state):
    wide = final_matrix.reshape(OUTER, OUTER, PAIR).transpose(1, 0, 2).reshape(OUTER, OUTER * PAIR)
    wide = jnp.pad(wide, ((0, 128 - OUTER), (0, 0)))
    block = pl.BlockSpec((PAIR_STEP, BLOCK, PAIR), lambda i: (i, 0, 0))
    return pl.pallas_call(
        pair_body,
        grid=(ROWS // PAIR_STEP,),
        in_specs=[
            pl.BlockSpec((PAIR_STEP, SIDE), lambda i: (i, 0)),
            pl.BlockSpec((BLOCK, SIDE), lambda i: (0, 0)),
            pl.BlockSpec((128, OUTER * PAIR), lambda i: (0, 0)),
            block,
        ],
        out_specs=block,
        out_shape=jax.ShapeDtypeStruct(couple_state.shape, BF16),
        scratch_shapes=[
            pltpu.VMEM((LEFT, WIDE), BF16),
            pltpu.VMEM((STRIDE * PAIR_STEP, PAIR), F32),
        ],
        compiler_params=pltpu.CompilerParams(vmem_limit_bytes=56 << 20),
        cost_estimate=pl.CostEstimate(flops=8 << 30, bytes_accessed=18 << 20, transcendentals=0),
        name="pair_update",
    )(left, right, wide, couple_state)


def per_device(
    lineup_state,
    couple_state,
    lineup_filled,
    observed_amino_flag,
    horizontal_query_matrix,
    horizontal_final_matrix,
    couple_offset_matrix,
    vertical_query_matrix,
    vertical_final_matrix,
    tensor_mean_side_matrix,
    tensor_mean_final_matrix,
):
    core = lax.axis_index("co").astype(jnp.int32).reshape(1)
    block = lax.axis_index(RES).astype(jnp.int32).reshape(1)
    mine = (lax.axis_index("yh") * 2 + lax.axis_index("zh")).astype(jnp.int32).reshape(1)
    chunk = swap(pack_chunk(block, lineup_state, lineup_filled, observed_amino_flag))
    normed, *sends = norm_chunk(chunk)
    near = [lax.all_to_all(send, ("yl", "zl", "x"), 0, 0) for send in sends]
    far = [lax.ppermute(part, "co", [(0, 1), (1, 0)]) for part in near]
    biases = []
    for part in range(BIAS_PARTS):
        send = bias_blocks(couple_state, couple_offset_matrix, part)
        send = send.reshape((32,) + send.shape[2:])
        biases.append(lax.all_to_all(send, RES, 0, 0))
    rows = row_attention(
        core, normed, chunk, near, far, biases, horizontal_query_matrix, horizontal_final_matrix
    )
    rows = [rows] + [lax.ppermute(rows, COLUMN, [(i, i ^ k) for i in range(4)]) for k in (1, 2, 3)]
    aligned, left, right = column_attention(
        mine, rows, vertical_query_matrix, vertical_final_matrix, tensor_mean_side_matrix
    )
    right = swap(right[0])
    aligned = swap(aligned)
    left = lax.all_to_all(left, NEAR, 0, 0)
    pair = pair_update(left.reshape(ROWS, SIDE), right, tensor_mean_final_matrix, couple_state)
    return aligned.reshape(SEQS, BLOCK, WIDTH), pair


def solution(mesh):
    fine = Mesh(mesh.devices.reshape(SIZES), AXES)
    return jax.shard_map(
        per_device,
        mesh=fine,
        in_specs=(
            P(SEQ, RES, None),
            P(SEQ, RES, None),
            P(SEQ, RES),
            P(),
            P(),
            P(),
            P(),
            P(),
            P(),
            P(),
            P(),
        ),
        out_specs=(P(SEQ, RES, None), P(SEQ, RES, None)),
        check_vma=False,
    )
```

time: 568 us -> 183 us (0.32); the launches traced: 559 us -> 183 us
  blocking collectives: 207 us -> 23.5 us
  matrix products: 144 us -> 0 us
  local copies, waits for them, and re-layouts: 94.7 us -> 13.4 us
  Pallas kernels: 0 us -> 66.1 us
  other arithmetic: 30.9 us -> 0 us
  starting transfers between devices: 9.28 us -> 39.3 us
  waiting for transfers between devices: 58.2 us -> 39.4 us
  between operations: 14.5 us -> 0.83 us
    all_gather x5 -> x0, blocking collectives: 207 us -> none  [the longest x1 95.2 us: per_device(): key_mask = lax.all_gather(present_entries, 'res', axis=1, tiled=True)]
    dot_general x19 -> x0, matrix products: 144 us -> none  [the longest x4 80 us: outer_block(): jnp.dot(outer_sum, tensor_mean_final_matrix, preferred_element_type=jnp.f...]
    pallas_call x0 -> x7, Pallas kernels: none -> 66.1 us  [the longest x2 20.3 us: bias_blocks(): pl.pallas_call(bias_body, grid=(ROWS // BIAS_STEP,), in_specs=[pl.BlockSp...]
    all_gather x4 -> x0, waiting for transfers between devices: 58.1 us -> none  [the longest x1 30.4 us: per_device(): bias_all = lax.all_gather(bias_local, 'seq', axis=1, tiled=True)]
    all_to_all x1 -> x4, waiting for transfers between devices: 0.01 us -> 29.1 us  [the longest x2 20.2 us: per_device(): biases.append(lax.all_to_all(send, RES, 0, 0))]
    reduce_sum x8 -> x0, other arithmetic: 26.5 us -> none  [the longest x4 12.6 us: standardize_features(): variance = jnp.mean(centered * centered, axis=-1, keepdims=True)]
    all_to_all x0 -> x1, blocking collectives: none -> 23.5 us  [per_device(): near = [lax.all_to_all(send, ('yl', 'zl', 'x'), 0, 0) for send in sends]]
    ppermute x0 -> x8, starting transfers between devices: none -> 21.8 us  [the longest x3 15.5 us: swap(): return lax.ppermute(array, SWAPPED, swap_pairs())]
  transfers between devices with their start and end apart: 5 -> 12, of which waited for: 3 -> 8; matrix products, arithmetic and copies ran while one was open for 7% -> 3% of each run, Pallas kernels for 0% -> 11%
where the time goes in v1:
time: 183 us
  Pallas kernels  66.1 us (36%)
  waiting for transfers between devices  39.4 us (22%)
  starting transfers between devices  39.3 us (21%)
  blocking collectives  23.5 us (13%)
  local copies, waits for them, and re-layouts  13.4 us (7%)
    all_to_all x1, blocking collectives, per_device(): near = [lax.all_to_all(send, ('yl', 'zl', 'x'), 0, 0) for send in sends]  23.5 us
    pallas_call x2, Pallas kernels, bias_blocks(): pl.pallas_call(bias_body, grid=(ROWS // BIAS_STEP,), in_specs=[pl.BlockSp...  20.3 us
    all_to_all x2, waiting for transfers between devices, per_device(): biases.append(lax.all_to_all(send, RES, 0, 0))  20.2 us
    pallas_call x1, Pallas kernels, row_attention(): pl.pallas_call(row_body, grid=(SEQS,), in_specs=[pl.BlockSpec(memory_spac...  17 us
    ppermute x3, starting transfers between devices, swap(): return lax.ppermute(array, SWAPPED, swap_pairs())  15.5 us
    pallas_call x1, Pallas kernels, pair_update(): pl.pallas_call(pair_body, grid=(ROWS // PAIR_STEP,), in_specs=[pl.BlockSp...  15.3 us
    pallas_call x1, Pallas kernels, column_attention(): pl.pallas_call(column_body, in_specs=[pl.BlockSpec(memory_space=pltpu.SME...  9.23 us
    all_to_all x1, waiting for transfers between devices, per_device(): near = [lax.all_to_all(send, ('yl', 'zl', 'x'), 0, 0) for send in sends]  8.91 us
  transfers between devices with their start and end apart: 12, of which 8 were waited for; matrix products, arithmetic and copies ran while one was open for 3% of the time, Pallas kernels for 11%

profile of v1, /device:TPU:1, one launch (start us, length us, event | category | flops | bytes accessed | tf_op | source)
XLA Modules:
  0.0 182.5 jit_solution(16564751033567154479)
XLA Ops:
  0.6 0.0 copy-start
  0.7 1.4 reshape.51.flag_ref
  2.0 1.7 pack_lineup.1
  3.7 6.9 %collective-permute-start = (bf16[264,256]{1,0:T(8,128)(2,1)}, bf16[264,256]{1,0:T(8,128)(2,1)S(1)}, u32[]{:S(2)}, u32[]{:S(2)}) collective-permute-start(bf16[264,256]{1,0:T(8,128)(2,1)} %pack_lineup.1), channel_id=1, source_target_pairs={{0,0},{8,32},{16,64},{24,96},{32,8},{40,40},{48,72},{56,104},{64,1... | collective-permute-start | bytes 405512 | tf_op jit(solution)/shard_map/ppermute | solution.py:50
  10.6 2.9 %collective-permute-done.x_ref = bf16[264,256]{1,0:T(8,128)(2,1)S(1)} collective-permute-done((bf16[264,256]{1,0:T(8,128)(2,1)}, bf16[264,256]{1,0:T(8,128)(2,1)S(1)}, u32[]{:S(2)}, u32[]{:S(2)}) %collective-permute-start) | collective-permute-done | bytes 135200 | tf_op jit(solution)/shard_map/ppermute | solution.py:50
  13.5 0.0 copy-start.1
  13.5 0.6 copy-done.1
  14.1 2.6 %norm_lineup.1 = (bf16[264,256]{1,0:T(8,128)(2,1)}, bf16[16,264,128]{2,1,0:T(8,128)(2,1)}, bf16[16,264,128]{2,1,0:T(8,128)(2,1)}) custom-call(bf16[264,256]{1,0:T(8,128)(2,1)} %copy-done.1), custom_call_target="tpu_custom_call" | custom-call | tf_op jit(solution)/shard_map/norm_lineup/pallas_call | solution.py:107
  16.7 23.5 %all_to_all.25.n0_ref.m0_ref = bf16[16,264,128]{2,1,0:T(8,128)(2,1)S(1)} all-to-all(bf16[16,264,128]{2,1,0:T(8,128)(2,1)} %get-tuple-element.9), channel_id=1, replica_groups=mesh['yl'=2,'co'=2,'yh'=2,'zh'=2,'zl'=2,'x'=4] {'yl','zl','x'}, dimensions={0} | all-to-all | bytes 2162688 | tf_op jit(solution)/shard_map/all_to_all | solution.py:451
  40.2 3.7 %all-to-all-start.1 = ((bf16[16,264,128]{2,1,0:T(8,128)(2,1)}), bf16[16,264,128]{2,1,0:T(8,128)(2,1)S(1)}, u32[]{:S(2)}, u32[]{:S(2)}) async-start(bf16[16,264,128]{2,1,0:T(8,128)(2,1)} %get-tuple-element.10), calls=%async_computation.1 | async-start | bytes 2162688 | tf_op jit(solution)/shard_map/all_to_all | solution.py:451
  43.9 0.0 copy-done
  44.0 0.7 copy.18.weight_ref
  44.7 10.1 %pair_bias.3 = bf16[4,8,32,512]{3,2,1,0:T(8,128)(2,1)} custom-call(bf16[512,64,128]{2,1,0:T(8,128)(2,1)} %pair_ref.5, bf16[128,256]{1,0:T(8,128)(2,1)} %copy.18.weight_ref), custom_call_target="tpu_custom_call" | custom-call | flops 8589934592 | bytes 6291456 | tf_op jit(solution)/shard_map/pair_bias/pallas_call | solution.py:159
  54.9 8.9 %all-to-all-done.1.n1_ref.m1_ref = bf16[16,264,128]{2,1,0:T(8,128)(2,1)S(1)} async-done(((bf16[16,264,128]{2,1,0:T(8,128)(2,1)}), bf16[16,264,128]{2,1,0:T(8,128)(2,1)S(1)}, u32[]{:S(2)}, u32[]{:S(2)}) %all-to-all-start.1) | async-done | bytes 1081376 | tf_op jit(solution)/shard_map/all_to_all | solution.py:451
  63.8 3.9 %all-to-all-start.3 = ((bf16[32,32,512]{2,1,0:T(8,128)(2,1)}), bf16[32,32,512]{2,1,0:T(8,128)(2,1)S(1)}, u32[]{:S(2)}, u32[]{:S(2)}) async-start(bf16[32,32,512]{2,1,0:T(8,128)(2,1)} %bitcast.24), calls=%async_computation.3 | async-start | bytes 2097152 | tf_op jit(solution)/shard_map/all_to_all | solution.py:457
  67.7 0.5 collective-permute-start.2
  68.2 0.1 collective-permute-start.1
  68.3 10.1 %pair_bias.2 = bf16[4,8,32,512]{3,2,1,0:T(8,128)(2,1)} custom-call(bf16[512,64,128]{2,1,0:T(8,128)(2,1)} %pair_ref.5, bf16[128,256]{1,0:T(8,128)(2,1)} %copy.18.weight_ref), custom_call_target="tpu_custom_call" | custom-call | flops 8589934592 | bytes 6291456 | tf_op jit(solution)/shard_map/pair_bias/pallas_call | solution.py:159
  78.4 6.8 %all-to-all-done.3.refs_1_ = bf16[32,32,512]{2,1,0:T(8,128)(2,1)S(1)} async-done(((bf16[32,32,512]{2,1,0:T(8,128)(2,1)}), bf16[32,32,512]{2,1,0:T(8,128)(2,1)S(1)}, u32[]{:S(2)}, u32[]{:S(2)}) %all-to-all-start.3) | async-done | bytes 1048608 | tf_op jit(solution)/shard_map/all_to_all | solution.py:457
  85.3 4.7 %all-to-all-start.2 = ((bf16[32,32,512]{2,1,0:T(8,128)(2,1)}), bf16[32,32,512]{2,1,0:T(8,128)(2,1)}, u32[]{:S(2)}, u32[]{:S(2)}) async-start(bf16[32,32,512]{2,1,0:T(8,128)(2,1)} %bitcast.23), calls=%async_computation.2 | async-start | bytes 2097152 | tf_op jit(solution)/shard_map/all_to_all | solution.py:457
  90.0 0.0 copy-start.2
  90.0 1.9 %fusion = (bf16[256,256]{1,0:T(8,128)(2,1)}, bf16[256,256]{1,0:T(8,128)(2,1)}, bf16[256,256]{1,0:T(8,128)(2,1)}, bf16[256,256]{1,0:T(8,128)(2,1)}) fusion(bf16[256,1024]{1,0:T(8,128)(2,1)} %param.15), kind=kLoop, calls=%fused_computation.2 | loop fusion | bytes 1048576 | tf_op jit(solution)/shard_map/slice | solution.py:248
  92.0 1.0 copy.24
  93.0 13.3 %all-to-all-done.2.refs_0_ = bf16[32,32,512]{2,1,0:T(8,128)(2,1)} async-done(((bf16[32,32,512]{2,1,0:T(8,128)(2,1)}), bf16[32,32,512]{2,1,0:T(8,128)(2,1)}, u32[]{:S(2)}, u32[]{:S(2)}) %all-to-all-start.2) | async-done | bytes 1048608 | tf_op jit(solution)/shard_map/all_to_all | solution.py:457
  106.3 0.0 collective-permute-done.2.f1_ref.m3_ref
  106.3 0.0 collective-permute-done.1.f0_ref.m2_ref
  106.3 0.0 copy-done.2
  106.3 0.0 copy-start.3
  106.3 0.9 copy-done.3
  107.2 0.0 copy-start.4
  107.2 0.9 copy-done.4
  108.1 0.0 copy-start.5
  108.1 0.9 copy-done.5
  109.0 0.0 copy-start.7
  109.0 0.9 copy-done.7
  109.9 0.9 copy-done.8
  110.8 0.0 copy-start.12
  110.8 17.0 %row_attention.1.x0_ref = bf16[264,256]{1,0:T(8,128)(2,1)} custom-call(s32[1]{0:T(128)} %bitcast.1.core_ref, bf16[264,256]{1,0:T(8,128)(2,1)S(1)} %copy-done.7, bf16[264,256]{1,0:T(8,128)(2,1)S(1)} %copy-done.2, bf16[16,264,128]{2,1,0:T(8,128)(2,1)S(1)} %all_to_all.25.n0_ref.m0_ref, bf16[16,264,128]{2,1,0:T(8,128)(2,1)S(1)} %all-to-all-done.1.n1_ref.m1_ref, ...), custom_call_target="tpu_custom_call" | custom-call | flops 17179869184 | bytes 8388608 | tf_op jit(solution)/shard_map/row_attention/pallas_call | solution.py:253
  127.8 1.8 collective-permute-start.5
  129.7 1.8 collective-permute-start.4
  131.5 2.0 %collective-permute-start.3 = (bf16[264,256]{1,0:T(8,128)(2,1)}, bf16[264,256]{1,0:T(8,128)(2,1)S(1)}, u32[]{:S(2)}, u32[]{:S(2)}) collective-permute-start(bf16[264,256]{1,0:T(8,128)(2,1)} %row_attention.1.x0_ref), channel_id=1, source_target_pairs={{0,8},{8,0},{16,24},{24,16},{1,9},{9,1},{17,25},{25,17},{2,10},{10... | collective-permute-start | bytes 405512 | tf_op jit(solution)/shard_map/ppermute | solution.py:461
  133.5 0.0 copy-done.12
  133.5 0.1 copy.22.right_ref
  133.7 0.1 copy.21.left_ref
  133.9 2.0 %collective-permute-done.5.x3_ref = bf16[264,256]{1,0:T(8,128)(2,1)S(1)} collective-permute-done((bf16[264,256]{1,0:T(8,128)(2,1)}, bf16[264,256]{1,0:T(8,128)(2,1)S(1)}, u32[]{:S(2)}, u32[]{:S(2)}) %collective-permute-start.5) | collective-permute-done | bytes 135200 | tf_op jit(solution)/shard_map/ppermute | solution.py:461
  135.8 0.0 collective-permute-done.4.x2_ref
  135.8 1.4 collective-permute-done.3.x1_ref
  137.3 0.0 copy-done.6
  137.3 0.0 copy-done.9
  137.3 9.2 %column_attention.1 = (bf16[256,256]{1,0:T(8,128)(2,1)S(1)}, bf16[8,64,640]{2,1,0:T(8,128)(2,1)}, bf16[1,64,640]{2,1,0:T(8,128)(2,1)S(1)}) custom-call(s32[1]{0:T(128)} %bitcast.mine_ref, bf16[264,256]{1,0:T(8,128)(2,1)} %row_attention.1.x0_ref, bf16[264,256]{1,0:T(8,128)(2,1)S(1)} %collective-permute-done.3.x1_ref, ...), custom_call_target="tpu_custom_call" | custom-call | flops 4294967296 | bytes 3145728 | tf_op jit(solution)/shard_map/column_attention/pallas_call | solution.py:346
  146.5 5.1 %all-to-all-start.4 = ((bf16[8,64,640]{2,1,0:T(8,128)(2,1)}), bf16[8,64,640]{2,1,0:T(8,128)(2,1)S(1)}, u32[]{:S(2)}, u32[]{:S(2)}) async-start(bf16[8,64,640]{2,1,0:T(8,128)(2,1)} %get-tuple-element.12), calls=%async_computation.4 | async-start | bytes 1310720 | tf_op jit(solution)/shard_map/all_to_all | solution.py:467
  151.6 6.7 %collective-permute-start.6 = (bf16[256,256]{1,0:T(8,128)(2,1)S(1)}, bf16[256,256]{1,0:T(8,128)(2,1)S(1)}, u32[]{:S(2)}, u32[]{:S(2)}) collective-permute-start(bf16[256,256]{1,0:T(8,128)(2,1)S(1)} %get-tuple-element.11), channel_id=1, source_target_pairs={{0,0},{8,32},{16,64},{24,96},{32,8},{40,40},{48,72},{56,104},{64,1... | collective-permute-start | bytes 393224 | tf_op jit(solution)/shard_map/ppermute | solution.py:50
  158.4 1.9 %collective-permute-start.7 = (bf16[64,640]{1,0:T(8,128)(2,1)S(1)}, bf16[64,640]{1,0:T(8,128)(2,1)S(1)}, u32[]{:S(2)}, u32[]{:S(2)}) collective-permute-start(bf16[64,640]{1,0:T(8,128)(2,1)S(1)} %bitcast.21), channel_id=1, source_target_pairs={{0,0},{8,32},{16,64},{24,96},{32,8},{40,40},{48,72},{56,104},{64,1... | collective-permute-start | bytes 245768 | tf_op jit(solution)/shard_map/ppermute | solution.py:50
  160.3 0.0 copy-done.11
  160.3 0.1 copy.23
  160.4 0.1 copy.27
  160.5 1.1 pad.4.w_ref
  161.6 3.2 %collective-permute-done.6 = bf16[256,256]{1,0:T(8,128)(2,1)S(1)} collective-permute-done((bf16[256,256]{1,0:T(8,128)(2,1)S(1)}, bf16[256,256]{1,0:T(8,128)(2,1)S(1)}, u32[]{:S(2)}, u32[]{:S(2)}) %collective-permute-start.6) | collective-permute-done | bytes 131104 | tf_op jit(solution)/shard_map/ppermute | solution.py:50
  164.8 0.9 collective-permute-done.7.b_ref
  165.6 0.0 all-to-all-done.4
  165.6 0.6 copy-done.13
  166.3 0.2 copy-done.10
  166.5 15.3 %pair_update.1 = bf16[512,64,128]{2,1,0:T(8,128)(2,1)} custom-call(bf16[512,640]{1,0:T(8,128)(2,1)} %bitcast.28, bf16[64,640]{1,0:T(8,128)(2,1)} %copy-done.13, bf16[128,4096]{1,0:T(8,128)(2,1)} %pad.4.w_ref, bf16[512,64,128]{2,1,0:T(8,128)(2,1)} %pair_ref.5), custom_call_target="tpu_custom_call" | custom-call | flops 8589934592 | bytes 18874368 | tf_op jit(solution)/shard_map/pair_update/pallas_call | solution.py:412
  181.9 0.7 copy.29
  (10 shorter events, 0.1 us)
Async XLA Ops:
  0.6 43.3 %copy-start = (bf16[128,8]{0,1:T(8,128)(2,1)S(1)}, bf16[128,8]{0,1:T(8,128)(2,1)}, u32[]{:S(2)}) copy-start(bf16[128,8]{0,1:T(8,128)(2,1)} %param.17) | copy-start | bytes 6148
  3.7 9.8 %collective-permute-start = (bf16[264,256]{1,0:T(8,128)(2,1)}, bf16[264,256]{1,0:T(8,128)(2,1)S(1)}, u32[]{:S(2)}, u32[]{:S(2)}) collective-permute-start(bf16[264,256]{1,0:T(8,128)(2,1)} %pack_lineup.1), channel_id=1, source_target_pairs={{0,0},{8,32},{16,64},{24,96},{32,8},{40,40},{48,72},{56,104},{64,1... | collective-permute-start | bytes 405512 | tf_op jit(solution)/shard_map/ppermute | solution.py:50
  13.5 0.6 copy-start.1
  40.2 23.5 %all-to-all-start.1 = ((bf16[16,264,128]{2,1,0:T(8,128)(2,1)}), bf16[16,264,128]{2,1,0:T(8,128)(2,1)S(1)}, u32[]{:S(2)}, u32[]{:S(2)}) async-start(bf16[16,264,128]{2,1,0:T(8,128)(2,1)} %get-tuple-element.10), calls=%async_computation.1 | async-start | bytes 2162688 | tf_op jit(solution)/shard_map/all_to_all | solution.py:451
  63.8 21.5 %all-to-all-start.3 = ((bf16[32,32,512]{2,1,0:T(8,128)(2,1)}), bf16[32,32,512]{2,1,0:T(8,128)(2,1)S(1)}, u32[]{:S(2)}, u32[]{:S(2)}) async-start(bf16[32,32,512]{2,1,0:T(8,128)(2,1)} %bitcast.24), calls=%async_computation.3 | async-start | bytes 2097152 | tf_op jit(solution)/shard_map/all_to_all | solution.py:457
  67.7 38.6 %collective-permute-start.2 = (bf16[16,264,128]{2,1,0:T(8,128)(2,1)S(1)}, bf16[16,264,128]{2,1,0:T(8,128)(2,1)}, u32[]{:S(2)}, u32[]{:S(2)}) collective-permute-start(bf16[16,264,128]{2,1,0:T(8,128)(2,1)S(1)} %all-to-all-done.1.n1_ref.m1_ref), channel_id=1, source_target_pairs={{0,32},{32,0},{1,33},{33,1},{2,34},{34,2},{3,35},{35,3},{4,36},{36... | collective-permute-start | bytes 3244040 | tf_op jit(solution)/shard_map/ppermute | solution.py:452
  68.2 38.1 %collective-permute-start.1 = (bf16[16,264,128]{2,1,0:T(8,128)(2,1)S(1)}, bf16[16,264,128]{2,1,0:T(8,128)(2,1)}, u32[]{:S(2)}, u32[]{:S(2)}) collective-permute-start(bf16[16,264,128]{2,1,0:T(8,128)(2,1)S(1)} %all_to_all.25.n0_ref.m0_ref), channel_id=1, source_target_pairs={{0,32},{32,0},{1,33},{33,1},{2,34},{34,2},{3,35},{35,3},{4,36},{36... | collective-permute-start | bytes 3244040 | tf_op jit(solution)/shard_map/ppermute | solution.py:452
  85.3 21.0 %all-to-all-start.2 = ((bf16[32,32,512]{2,1,0:T(8,128)(2,1)}), bf16[32,32,512]{2,1,0:T(8,128)(2,1)}, u32[]{:S(2)}, u32[]{:S(2)}) async-start(bf16[32,32,512]{2,1,0:T(8,128)(2,1)} %bitcast.23), calls=%async_computation.2 | async-start | bytes 2097152 | tf_op jit(solution)/shard_map/all_to_all | solution.py:457
  90.0 16.3 %copy-start.2 = (bf16[264,256]{1,0:T(8,128)(2,1)S(1)}, bf16[264,256]{1,0:T(8,128)(2,1)}, u32[]{:S(2)}) copy-start(bf16[264,256]{1,0:T(8,128)(2,1)} %copy-done.1) | copy-start | bytes 405508
  106.3 0.9 copy-start.3
  107.2 0.9 copy-start.4
  108.1 0.9 copy-start.5
  109.0 0.9 copy-start.7
  109.9 0.9 copy-start.8
  110.8 22.7 %copy-start.12 = (bf16[256,64]{0,1:T(8,128)(2,1)S(1)}, bf16[256,64]{0,1:T(8,128)(2,1)}, u32[]{:S(2)}) copy-start(bf16[256,64]{0,1:T(8,128)(2,1)} %param.20) | copy-start | bytes 98308
  127.8 9.4 %copy-start.6 = (bf16[256,1024]{1,0:T(8,128)(2,1)S(1)}, bf16[256,1024]{1,0:T(8,128)(2,1)}, u32[]{:S(2)}) copy-start(bf16[256,1024]{1,0:T(8,128)(2,1)} %w_ref.1) | copy-start | bytes 1572868
  127.8 9.4 %copy-start.9 = (bf16[256,256]{1,0:T(8,128)(2,1)S(1)}, bf16[256,256]{1,0:T(8,128)(2,1)}, u32[]{:S(2)}) copy-start(bf16[256,256]{1,0:T(8,128)(2,1)} %wo_ref.1) | copy-start | bytes 393220
  127.8 8.0 %collective-permute-start.5 = (bf16[264,256]{1,0:T(8,128)(2,1)}, bf16[264,256]{1,0:T(8,128)(2,1)S(1)}, u32[]{:S(2)}, u32[]{:S(2)}) collective-permute-start(bf16[264,256]{1,0:T(8,128)(2,1)} %row_attention.1.x0_ref), channel_id=1, source_target_pairs={{0,24},{8,16},{16,8},{24,0},{1,25},{9,17},{17,9},{25,1},{2,26},{10... | collective-permute-start | bytes 405512 | tf_op jit(solution)/shard_map/ppermute | solution.py:461
  129.7 6.2 %collective-permute-start.4 = (bf16[264,256]{1,0:T(8,128)(2,1)}, bf16[264,256]{1,0:T(8,128)(2,1)S(1)}, u32[]{:S(2)}, u32[]{:S(2)}) collective-permute-start(bf16[264,256]{1,0:T(8,128)(2,1)} %row_attention.1.x0_ref), channel_id=1, source_target_pairs={{0,16},{8,24},{16,0},{24,8},{1,17},{9,25},{17,1},{25,9},{2,18},{10... | collective-permute-start | bytes 405512 | tf_op jit(solution)/shard_map/ppermute | solution.py:461
  131.5 5.8 %collective-permute-start.3 = (bf16[264,256]{1,0:T(8,128)(2,1)}, bf16[264,256]{1,0:T(8,128)(2,1)S(1)}, u32[]{:S(2)}, u32[]{:S(2)}) collective-permute-start(bf16[264,256]{1,0:T(8,128)(2,1)} %row_attention.1.x0_ref), channel_id=1, source_target_pairs={{0,8},{8,0},{16,24},{24,16},{1,9},{9,1},{17,25},{25,17},{2,10},{10... | collective-permute-start | bytes 405512 | tf_op jit(solution)/shard_map/ppermute | solution.py:461
  146.5 13.8 %copy-start.11 = (bf16[1024,128]{1,0:T(8,128)(2,1)S(1)}, bf16[1024,128]{1,0:T(8,128)(2,1)}, u32[]{:S(2)}) copy-start(bf16[1024,128]{1,0:T(8,128)(2,1)} %param.21) | copy-start | bytes 786436
  146.5 19.1 %all-to-all-start.4 = ((bf16[8,64,640]{2,1,0:T(8,128)(2,1)}), bf16[8,64,640]{2,1,0:T(8,128)(2,1)S(1)}, u32[]{:S(2)}, u32[]{:S(2)}) async-start(bf16[8,64,640]{2,1,0:T(8,128)(2,1)} %get-tuple-element.12), calls=%async_computation.4 | async-start | bytes 1310720 | tf_op jit(solution)/shard_map/all_to_all | solution.py:467
  151.6 13.1 %collective-permute-start.6 = (bf16[256,256]{1,0:T(8,128)(2,1)S(1)}, bf16[256,256]{1,0:T(8,128)(2,1)S(1)}, u32[]{:S(2)}, u32[]{:S(2)}) collective-permute-start(bf16[256,256]{1,0:T(8,128)(2,1)S(1)} %get-tuple-element.11), channel_id=1, source_target_pairs={{0,0},{8,32},{16,64},{24,96},{32,8},{40,40},{48,72},{56,104},{64,1... | collective-permute-start | bytes 393224 | tf_op jit(solution)/shard_map/ppermute | solution.py:50
  158.4 7.3 %collective-permute-start.7 = (bf16[64,640]{1,0:T(8,128)(2,1)S(1)}, bf16[64,640]{1,0:T(8,128)(2,1)S(1)}, u32[]{:S(2)}, u32[]{:S(2)}) collective-permute-start(bf16[64,640]{1,0:T(8,128)(2,1)S(1)} %bitcast.21), channel_id=1, source_target_pairs={{0,0},{8,32},{16,64},{24,96},{32,8},{40,40},{48,72},{56,104},{64,1... | collective-permute-start | bytes 245768 | tf_op jit(solution)/shard_map/ppermute | solution.py:50
  165.6 0.6 copy-start.13
  165.6 0.9 copy-start.10

commit v2 on v1

v2 whole, which is shorter than its diff:
```python
import itertools
import math

import jax
import jax.numpy as jnp
import numpy as np
from jax import lax
from jax.experimental import pallas as pl
from jax.experimental.pallas import tpu as pltpu
from jax.sharding import Mesh, PartitionSpec as P

F32 = jnp.float32
BF16 = jnp.bfloat16

AXES = ("yl", "co", "yh", "zh", "zl", "x")
SIZES = (2, 2, 2, 2, 2, 4)
SEQ = ("yl", "co")
RES = ("yh", "zh", "zl", "x")
SWAPPED = ("yl", "co", "yh", "zh")
COLUMN = ("yh", "zh")
NEAR = ("zl", "x")

SEQS = 4
BLOCK = 64
ROWS = 512
WIDTH = 256
HEADS = 8
HEAD_DIM = 32
ALL_SEQS = 16
OUTER = 32
PAIR = 128
LEFT = ALL_SEQS * OUTER
CHUNK = SEQS * BLOCK + 8
MASKED = -1000000000.0
OTHER = -2000000000.0

FLIP = [(0, 1), (1, 0)]
NT = (((1,), (1,)), ((), ()))


def swap_pairs(flip):
    pairs = []
    for spot in np.ndindex(2, 2, 2, 2):
        target = (spot[2] ^ flip, spot[3], spot[0], spot[1])
        pairs.append(
            (int(np.ravel_multi_index(spot, (2, 2, 2, 2))), int(np.ravel_multi_index(target, (2, 2, 2, 2))))
        )
    return pairs


def swap(array, flip=0):
    return lax.ppermute(array, SWAPPED, swap_pairs(flip))


def shift(array, step, flip=0):
    return lax.ppermute(array, NEAR, [(z * 4 + i, (z ^ flip) * 4 + (i + step) % 4) for z in (0, 1) for i in range(4)])


def tie_body(*refs):
    pass


def tie(array, *first):
    anywhere = pl.BlockSpec(memory_space=pl.ANY)
    return pl.pallas_call(
        tie_body,
        in_specs=[anywhere] * (1 + len(first)),
        out_specs=anywhere,
        out_shape=jax.ShapeDtypeStruct(array.shape, array.dtype),
        input_output_aliases={0: 0},
        name="tie",
    )(array, *first)


def dot(a, b, dims=(((1,), (0,)), ((), ()))):
    return lax.dot_general(a, b, dims, preferred_element_type=F32)


def norm(data):
    centered = data - jnp.mean(data, axis=-1, keepdims=True)
    variance = jnp.mean(centered * centered, axis=-1, keepdims=True)
    return centered * lax.rsqrt(variance + 1e-05)


def iota(shape, dim):
    return lax.broadcasted_iota(jnp.int32, shape, dim)


def pack_body(block_ref, x_ref, filled_ref, flag_ref, out_ref):
    rows = SEQS * BLOCK
    out_ref[:rows, :] = x_ref[...]
    filled = filled_ref[...].astype(F32)
    block = block_ref[0]
    flags = flag_ref[pl.ds(block // 2, 1), :].astype(F32)
    live = filled * jnp.where(block % 2 == 0, flags[:, :BLOCK], flags[:, BLOCK:])
    lines = [jnp.concatenate([part[i : i + 1] for i in range(SEQS)], axis=1) for part in (filled, live)]
    lines.append(jnp.zeros((6, WIDTH), F32))
    out_ref[rows:, :] = jnp.concatenate(lines, axis=0).astype(BF16)


def pack_chunk(block, lineup_state, lineup_filled, flags):
    vmem = pl.BlockSpec(memory_space=pltpu.VMEM)
    return pl.pallas_call(
        pack_body,
        in_specs=[pl.BlockSpec(memory_space=pltpu.SMEM), vmem, vmem, vmem],
        out_specs=vmem,
        out_shape=jax.ShapeDtypeStruct((CHUNK, WIDTH), BF16),
        name="pack_lineup",
    )(block, lineup_state.reshape(SEQS * BLOCK, WIDTH), lineup_filled, flags.reshape(-1, 2 * BLOCK))


def norm_body(x_ref, flipped_ref, after_ref, out_ref):
    rows = SEQS * BLOCK
    for slot, ref in enumerate((x_ref, flipped_ref)):
        out_ref[slot, :rows, :] = norm(ref[:rows, :].astype(F32)).astype(BF16)
        out_ref[slot, rows:, :] = ref[rows:, :]


def norm_chunks(chunk, flipped, after):
    vmem = pl.BlockSpec(memory_space=pltpu.VMEM)
    return pl.pallas_call(
        norm_body,
        in_specs=[vmem, vmem, pl.BlockSpec(memory_space=pl.ANY)],
        out_shape=jax.ShapeDtypeStruct((2, CHUNK, WIDTH), BF16),
        name="norm_lineup",
    )(chunk, flipped, after)


BIAS_STEP = 128
BIAS_PARTS = 1
GROUP = 32
COPIES = 4


def bias_body(pair_ref, weight_ref, *refs):
    out_ref, spread, normed = refs[-3:]

    @pl.when(pl.program_id(0) == 0)
    def _():
        wide = weight_ref[...]
        owner = iota((PAIR, WIDTH), 1) // HEADS

        def place(i, carry):
            spread[pl.ds(pl.multiple_of(i * PAIR, PAIR), PAIR), :] = jnp.where(
                owner == i, wide, jnp.zeros_like(wide)
            )
            return carry

        lax.fori_loop(0, GROUP, place, 0)

    groups = BIAS_STEP // GROUP
    cols = BLOCK // BIAS_PARTS
    ones = jnp.ones((PAIR, PAIR), BF16)

    def one(i, carry):
        for g in range(groups):
            raw = pair_ref[g * GROUP + i]
            centered = raw.astype(F32) - dot(raw, ones) * (1.0 / PAIR)
            variance = jnp.mean(centered * centered, axis=-1, keepdims=True)
            normed[g * cols : (g + 1) * cols, pl.ds(pl.multiple_of(i * PAIR, PAIR), PAIR)] = (
                centered * lax.rsqrt(variance + 1e-05)
            ).astype(BF16)
        return carry

    lax.fori_loop(0, GROUP, one, 0, unroll=8)
    result = dot(normed[...], spread[...]).astype(BF16)
    for g in range(groups):
        for c in range(COPIES):
            out_ref[c, g // 2, :, (g % 2) * WIDTH : (g % 2 + 1) * WIDTH] = result[g * cols : (g + 1) * cols]


def bias_blocks(couple_state, couple_offset_matrix, start, steps, *after):
    wide = jnp.tile(couple_offset_matrix, (1, GROUP))
    per_step = BIAS_STEP // BLOCK
    cols = BLOCK // BIAS_PARTS
    return pl.pallas_call(
        bias_body,
        grid=(steps,),
        in_specs=[
            pl.BlockSpec((BIAS_STEP, cols, PAIR), lambda i: (i + start, 0, 0)),
            pl.BlockSpec((PAIR, WIDTH), lambda i: (0, 0)),
        ]
        + [pl.BlockSpec(memory_space=pl.ANY)] * len(after),
        out_specs=pl.BlockSpec((COPIES, per_step, cols, BLOCK * HEADS), lambda i: (0, i + start, 0, 0)),
        out_shape=jax.ShapeDtypeStruct((COPIES, ROWS // BLOCK, cols, BLOCK * HEADS), BF16),
        scratch_shapes=[
            pltpu.VMEM((GROUP * PAIR, WIDTH), BF16),
            pltpu.VMEM((BIAS_STEP // GROUP * cols, GROUP * PAIR), BF16),
        ],
        compiler_params=pltpu.CompilerParams(vmem_limit_bytes=53 << 20),
        cost_estimate=pl.CostEstimate(flops=8 << 30, bytes_accessed=6 << 20, transcendentals=0),
        input_output_aliases={2: 0} if start else {},
        name="pair_bias",
    )(couple_state, wide, *after)


KEY_TILE = 512
KEYS = 2048
QH = BLOCK * HEADS
PER_TILE = KEY_TILE // BLOCK
SPOTS = [(zl, x, co) for co in (0, 1) for zl in (0, 1) for x in (0, 1, 3, 2)]


def key_body(*refs):
    parts, flags = refs[: len(SPOTS)], refs[len(SPOTS) : 2 * len(SPOTS)]
    wk_ref, wvt_ref, key_ref, value_ref, live_ref = refs[2 * len(SPOTS) :]

    @pl.when(pl.program_id(0) == 0)
    def _():
        lanes = jnp.concatenate([ref[...].astype(F32)[:, 1, :] for ref in flags], axis=0)
        live_ref[...] = jnp.concatenate([lanes, jnp.zeros((128 - 2 * len(SPOTS), WIDTH), F32)], axis=0).T

    for t in range(KEYS // KEY_TILE):
        blocks = [(b // 2, b % 2) for b in range(t * PER_TILE, (t + 1) * PER_TILE)]
        tile = jnp.concatenate([parts[i][slot] for i, slot in blocks], axis=0)
        lanes = slice(t * KEY_TILE, (t + 1) * KEY_TILE)
        key_ref[0, lanes, :] = dot(tile, wk_ref[...]).astype(BF16)
        value_ref[0, :, lanes] = dot(wvt_ref[...], tile, NT).astype(BF16)


def row_keys(parts, wk, wv):
    gathered = pl.BlockSpec((2, BLOCK, WIDTH), lambda s: (0, s, 0))
    masks = pl.BlockSpec((2, 8, WIDTH), lambda s: (0, SEQS * BLOCK // 8, 0))
    square = pl.BlockSpec((WIDTH, WIDTH), lambda s: (0, 0))
    return pl.pallas_call(
        key_body,
        grid=(SEQS,),
        in_specs=[*([gathered] * len(SPOTS)), *([masks] * len(SPOTS)), square, square],
        out_specs=[
            pl.BlockSpec((1, KEYS, WIDTH), lambda s: (s, 0, 0)),
            pl.BlockSpec((1, WIDTH, KEYS), lambda s: (s, 0, 0)),
            pl.BlockSpec((WIDTH, 128), lambda s: (0, 0)),
        ],
        out_shape=[
            jax.ShapeDtypeStruct((SEQS, KEYS, WIDTH), BF16),
            jax.ShapeDtypeStruct((SEQS, WIDTH, KEYS), BF16),
            jax.ShapeDtypeStruct((WIDTH, 128), F32),
        ],
        compiler_params=pltpu.CompilerParams(vmem_limit_bytes=57 << 20),
        cost_estimate=pl.CostEstimate(flops=4 << 30, bytes_accessed=12 << 20, transcendentals=0),
        name="row_keys",
    )(*parts, *parts, wk, wv.T)


def row_body(spot_ref, own_ref, x_ref, key_ref, value_ref, live, *refs):
    bias_refs = refs[:BIAS_PARTS]
    wq_ref, wg_ref, wo_ref, out_ref, *scratch = refs[BIAS_PARTS:]
    weights = scratch[-1]
    even, odd = scratch[0:2], scratch[2:4]
    step = pl.program_id(0)
    yl, core, zl, x = (spot_ref[i] for i in range(4))
    head_rows = (iota((BLOCK, HEADS, WIDTH), 2) // HEAD_DIM) == iota((BLOCK, HEADS, WIDTH), 1)

    def rows_of(s):
        return pl.ds(pl.multiple_of(s * BLOCK, BLOCK), BLOCK)

    def score(buffers):
        scores, highest = buffers
        rows = rows_of(step)
        queries = (dot(own_ref[0, rows, :], wq_ref[...]) * (1.0 / math.sqrt(HEAD_DIM))).astype(BF16).astype(F32)
        spread = (
            jnp.where(head_rows, jnp.broadcast_to(queries[:, None, :], (BLOCK, HEADS, WIDTH)), 0.0)
            .reshape(QH, WIDTH)
            .astype(BF16)
        )
        top = jnp.full((8, QH), -3e38, F32)
        mask_rows = live[rows, : 2 * len(SPOTS)]
        for t in range(KEYS // KEY_TILE):
            blocks = [(b // 2, b % 2) for b in range(t * PER_TILE, (t + 1) * PER_TILE)]
            lanes = slice(t * KEY_TILE, (t + 1) * KEY_TILE)
            bias = []
            for i, slot in blocks:
                flip, back, side = SPOTS[i]
                block = (yl ^ slot) * 16 + (core ^ side) * 8 + (zl ^ flip) * 4 + (x + 4 - back) % 4
                bias += [part[block] for part in bias_refs]
            product = dot(key_ref[0, lanes, :], spread, NT) + jnp.concatenate(bias, axis=0).astype(F32)
            alive = jnp.concatenate([mask_rows[:, 2 * i + slot : 2 * i + slot + 1] for i, slot in blocks], axis=0)
            product = jnp.where(alive > 0.0, product, MASKED)
            scores[lanes, :] = product
            top = jnp.maximum(top, jnp.max(product.reshape(KEY_TILE // 8, 8, QH), axis=0))
            yield
        highest[...] = jnp.broadcast_to(jnp.max(top, axis=0, keepdims=True), (8, QH))

    def attend(buffers):
        scores, highest = buffers
        rows = rows_of(step - 1)
        largest = highest[0:1, :]
        total = jnp.zeros((8, QH), F32)
        for t in range(KEYS // KEY_TILE):
            lanes = slice(t * KEY_TILE, (t + 1) * KEY_TILE)
            expo = jnp.exp(scores[lanes, :] - largest)
            total = total + jnp.sum(expo.reshape(KEY_TILE // 8, 8, QH), axis=0)
            weights[lanes, :] = expo.astype(BF16)
            yield
        mixed = dot(value_ref[0], weights[...])
        mixed = mixed / jnp.sum(total, axis=0, keepdims=True)
        picked = jnp.where(head_rows, mixed.T.reshape(BLOCK, HEADS, WIDTH), 0.0)
        attended = jnp.sum(picked, axis=1)
        gate = jax.nn.sigmoid(dot(own_ref[0, rows, :], wg_ref[...]))
        added = dot((gate * attended).astype(BF16), wo_ref[...])
        out_ref[rows, :] = (x_ref[rows, :].astype(F32) + added).astype(BF16)

    def run(*work):
        for _ in itertools.zip_longest(*work):
            pass

    @pl.when(step == 0)
    def _():
        out_ref[SEQS * BLOCK :, :] = x_ref[SEQS * BLOCK :, :]
        run(score(even))

    @pl.when(step % 2 == 1)
    def _():
        run(score(odd), attend(even))

    @pl.when(step == 2)
    def _():
        run(score(even), attend(odd))

    @pl.when(step == SEQS)
    def _():
        run(attend(odd))


def row_attention(spot, own, x, keys, values, live, biases, wq, wg, wo):
    whole = lambda shape: pl.BlockSpec(shape, lambda s: (0,) * len(shape))
    square = whole((WIDTH, WIDTH))
    return pl.pallas_call(
        row_body,
        grid=(SEQS + 1,),
        in_specs=[
            pl.BlockSpec(memory_space=pltpu.SMEM),
            whole((2, CHUNK, WIDTH)),
            whole((CHUNK, WIDTH)),
            pl.BlockSpec((1, KEYS, WIDTH), lambda s: (jnp.minimum(s, SEQS - 1), 0, 0)),
            pl.BlockSpec((1, WIDTH, KEYS), lambda s: (jnp.maximum(s - 1, 0), 0, 0)),
            whole((WIDTH, 128)),
            *([whole((KEYS // BLOCK, BLOCK // BIAS_PARTS, QH))] * BIAS_PARTS),
            square,
            square,
            square,
        ],
        out_specs=whole((CHUNK, WIDTH)),
        out_shape=jax.ShapeDtypeStruct((CHUNK, WIDTH), BF16),
        scratch_shapes=[
            *([pltpu.VMEM((KEYS, QH), F32), pltpu.VMEM((8, QH), F32)] * 2),
            pltpu.VMEM((KEYS, QH), BF16),
        ],
        compiler_params=pltpu.CompilerParams(vmem_limit_bytes=57 << 20),
        cost_estimate=pl.CostEstimate(flops=12 << 30, bytes_accessed=12 << 20, transcendentals=4 << 20),
        name="row_attention",
    )(spot, own, x, keys, values, live, *biases, wq, wg, wo)


PART = 16
PART_ROWS = ALL_SEQS * PART
BACK = SEQS * BLOCK + 3 * BLOCK
SIDE = LEFT + 128


def column_body(
    mine_ref, x0_ref, x1_ref, x2_ref, x3_ref, w_ref, wo_ref, left_ref, right_ref, out_ref, a_ref, masks,
):
    x_refs = (x0_ref, x1_ref, x2_ref, x3_ref)
    mine = mine_ref[0]
    for b in range(4):
        lanes = x_refs[b][SEQS * BLOCK :, :].astype(F32)
        masks[:, b * 128 : b * 128 + 8] = lanes.T
    one_row = iota((PART_ROWS, PART_ROWS), 0)
    one_col = iota((PART_ROWS, PART_ROWS), 1)
    same = (one_row % PART) == (one_col % PART)

    def sequence(shape):
        slot = iota(shape, 0) // PART
        return ((slot // SEQS) ^ mine) * SEQS + slot % SEQS

    keep = iota((PART_ROWS, LEFT), 1) % ALL_SEQS == sequence((PART_ROWS, LEFT))
    keep_flag = iota((PART_ROWS, 128), 1) == sequence((PART_ROWS, 128))
    lane_head = iota((PART_ROWS, WIDTH), 1) // HEAD_DIM
    for g in range(BLOCK // PART):
        spots = [(s // SEQS, (s % SEQS) * BLOCK + g * PART) for s in range(ALL_SEQS)]
        data = jnp.concatenate([x_refs[b][r : r + PART, :] for b, r in spots], axis=0).astype(F32)
        filled = jnp.concatenate([masks[r : r + PART, b * 128 : b * 128 + 1] for b, r in spots], axis=0)
        live = jnp.concatenate([masks[r : r + PART, b * 128 + 1 : b * 128 + 2] for b, r in spots], axis=0)
        filled_lane = jnp.broadcast_to(filled, (PART_ROWS, 128)).T[0:1, :]
        fill = jnp.where(same, MASKED, OTHER)
        use = jnp.logical_and(same, jnp.broadcast_to(filled_lane, (PART_ROWS, PART_ROWS)) > 0.0)
        line = dot(norm(data).astype(BF16), w_ref[...])
        queries = (line[:, :WIDTH] * (1.0 / math.sqrt(HEAD_DIM))).astype(BF16)
        keys = line[:, WIDTH : 2 * WIDTH].astype(BF16)
        value = line[:, 2 * WIDTH : 3 * WIDTH].astype(BF16)
        gate = jax.nn.sigmoid(line[:, 3 * WIDTH :])
        mixed = jnp.zeros((PART_ROWS, WIDTH), F32)
        for h in range(HEADS):
            head = lane_head == h
            product = dot(jnp.where(head, queries, jnp.zeros_like(queries)), keys, NT)
            product = jnp.where(use, product, fill)
            expo = jnp.exp(product - jnp.max(product, axis=1, keepdims=True))
            total = jnp.sum(expo, axis=1, keepdims=True)
            mixed = mixed + jnp.where(head, dot(expo.astype(BF16), value) / total, 0.0)
        result = (data + dot((gate * mixed).astype(BF16), wo_ref[...])).astype(BF16)
        for s in range(SEQS):
            out_ref[s * BLOCK + g * PART : s * BLOCK + (g + 1) * PART, :] = result[s * PART : (s + 1) * PART]
        normed = norm(result.astype(F32)).astype(BF16)
        flags = jnp.where(keep_flag, jnp.broadcast_to(live, (PART_ROWS, 128)), 0.0)
        flags = jnp.sum(flags.reshape(ALL_SEQS, PART, 128), axis=0).astype(BF16)
        for weight_ref, out in ((right_ref, out_ref), (left_ref, a_ref)):
            wide = (dot(normed, weight_ref[...]) * live).astype(BF16).astype(F32)
            wide = jnp.where(keep, wide, 0.0)
            wide = jnp.sum(wide.reshape(ALL_SEQS, PART, LEFT), axis=0).astype(BF16)
            rows = slice(g * PART, (g + 1) * PART)
            if out is out_ref:
                first = SEQS * BLOCK + g * PART
                out[first : first + PART, :] = wide[:, :WIDTH]
                out[first + BLOCK : first + BLOCK + PART, :] = wide[:, WIDTH:]
                out[first + 2 * BLOCK : first + 2 * BLOCK + PART, :128] = flags
                out[first + 2 * BLOCK : first + 2 * BLOCK + PART, 128:] = flags
            else:
                for k in range(out.shape[0]):
                    out[k, rows, :LEFT] = wide
                    out[k, rows, LEFT:] = flags


def column_attention(mine, rows, query_matrix, final_matrix, side_matrix):
    left = jnp.repeat(side_matrix[:, :OUTER], ALL_SEQS, axis=1)
    right = jnp.repeat(side_matrix[:, OUTER:], ALL_SEQS, axis=1)
    vmem = pl.BlockSpec(memory_space=pltpu.VMEM)
    return pl.pallas_call(
        column_body,
        in_specs=[pl.BlockSpec(memory_space=pltpu.SMEM)] + [vmem] * 8,
        out_specs=[vmem] * 2,
        out_shape=[
            jax.ShapeDtypeStruct((BACK, WIDTH), BF16),
            jax.ShapeDtypeStruct((8, BLOCK, SIDE), BF16),
        ],
        scratch_shapes=[pltpu.VMEM((WIDTH, 512), F32)],
        compiler_params=pltpu.CompilerParams(vmem_limit_bytes=24 << 20),
        cost_estimate=pl.CostEstimate(flops=4 << 30, bytes_accessed=3 << 20, transcendentals=2 << 20),
        name="column_attention",
    )(mine, *rows, query_matrix, final_matrix, left, right)


PAIR_STEP = 128
WIDE = BLOCK * PAIR
STRIDE = BLOCK + 8


def pair_body(a_ref, b_ref, w_ref, pair_ref, out_ref, table, update):
    @pl.when(pl.program_id(0) == 0)
    def _():
        keep = (iota((16 * ALL_SEQS, LEFT), 1) % ALL_SEQS) == (iota((16 * ALL_SEQS, LEFT), 0) % ALL_SEQS)
        fold = (iota((LEFT, 128), 0) // ALL_SEQS == iota((LEFT, 128), 1)).astype(BF16)

        def build(q, carry):
            first = pl.multiple_of(SEQS * BLOCK + q * 16, 16)
            rows = jnp.concatenate(
                [b_ref[pl.ds(first, 16), :], b_ref[pl.ds(pl.multiple_of(first + BLOCK, 16), 16), :]], axis=1
            ).astype(F32)
            rows = jnp.broadcast_to(rows[:, None, :], (16, ALL_SEQS, LEFT)).reshape(16 * ALL_SEQS, LEFT)
            right = dot(jnp.where(keep, rows, 0.0).astype(BF16), fold).astype(BF16)
            for c in range(OUTER // 2):
                part = dot(right, w_ref[:, c * 256 : (c + 1) * 256]).astype(BF16)
                for j in range(16):
                    lanes = pl.ds(pl.multiple_of((q * 16 + j) * PAIR, PAIR), PAIR)
                    for d in range(2):
                        table[(2 * c + d) * 16 : (2 * c + d + 1) * 16, lanes] = part[
                            j * 16 : (j + 1) * 16, d * PAIR : (d + 1) * PAIR
                        ]
            return carry

        lax.fori_loop(0, BLOCK // 16, build, 0)

    left = a_ref[:, :LEFT]
    count = dot(a_ref[:, LEFT:], b_ref[BACK - BLOCK :, :128], NT)
    scale = 1.0 / jnp.maximum(count, 1.0)
    per_dot = 4
    for j in range(0, BLOCK, per_dot):
        part = dot(left, table[:, j * PAIR : (j + per_dot) * PAIR])
        for d in range(per_dot):
            update[pl.ds(j + d, PAIR_STEP, stride=STRIDE), :] = (
                part[:, d * PAIR : (d + 1) * PAIR] * scale[:, j + d : j + d + 1]
            )

    def finish(i, carry):
        rows = update[pl.ds(pl.multiple_of(i * STRIDE, 8), BLOCK), :]
        out_ref[i] = (pair_ref[i].astype(F32) + rows).astype(BF16)
        return carry

    lax.fori_loop(0, PAIR_STEP, finish, 0, unroll=4)


def pair_update(left, right, final_matrix, couple_state):
    wide = final_matrix.reshape(OUTER, OUTER, PAIR).transpose(1, 0, 2).reshape(OUTER, OUTER * PAIR)
    wide = jnp.pad(wide, ((0, 128 - OUTER), (0, 0)))
    block = pl.BlockSpec((PAIR_STEP, BLOCK, PAIR), lambda i: (i, 0, 0))
    return pl.pallas_call(
        pair_body,
        grid=(ROWS // PAIR_STEP,),
        in_specs=[
            pl.BlockSpec((PAIR_STEP, SIDE), lambda i: (i, 0)),
            pl.BlockSpec((BACK, WIDTH), lambda i: (0, 0)),
            pl.BlockSpec((128, OUTER * PAIR), lambda i: (0, 0)),
            block,
        ],
        out_specs=block,
        out_shape=jax.ShapeDtypeStruct(couple_state.shape, BF16),
        scratch_shapes=[
            pltpu.VMEM((LEFT, WIDE), BF16),
            pltpu.VMEM((STRIDE * PAIR_STEP, PAIR), F32),
        ],
        compiler_params=pltpu.CompilerParams(vmem_limit_bytes=53 << 20),
        cost_estimate=pl.CostEstimate(flops=8 << 30, bytes_accessed=18 << 20, transcendentals=0),
        name="pair_update",
    )(left, right, wide, couple_state)


def per_device(
    lineup_state,
    couple_state,
    lineup_filled,
    observed_amino_flag,
    horizontal_query_matrix,
    horizontal_final_matrix,
    couple_offset_matrix,
    vertical_query_matrix,
    vertical_final_matrix,
    tensor_mean_side_matrix,
    tensor_mean_final_matrix,
):
    spot = jnp.stack([lax.axis_index(axis) for axis in ("yl", "co", "zl", "x")]).astype(jnp.int32)
    block = lax.axis_index(RES).astype(jnp.int32).reshape(1)
    mine = (lax.axis_index("yh") * 2 + lax.axis_index("zh")).astype(jnp.int32).reshape(1)
    packed = pack_chunk(block, lineup_state, lineup_filled, observed_amino_flag)
    chunk = swap(packed)
    send = bias_blocks(couple_state, couple_offset_matrix, 0, 1)
    kept = norm_chunks(chunk, swap(packed, 1), send)
    parts = []
    for flip in (0, 1):
        part = shift(kept, 0, 1) if flip else kept
        parts += [part, shift(kept, 1, flip), shift(kept, -1, flip)]
    send = bias_blocks(couple_state, couple_offset_matrix, 1, 2, send, kept)
    send = bias_blocks(couple_state, couple_offset_matrix, 3, 1, send, *parts[1:])
    parts = parts[:3] + [shift(parts[1], 1)] + parts[3:] + [shift(parts[5], -1)]
    send = tie(send, parts[3], parts[7])
    parts += [lax.ppermute(part, "co", FLIP) for part in parts]
    biases = [lax.all_to_all(send.reshape((32,) + send.shape[2:]), RES, 0, 0)]
    wq, wk, wv, wg = (horizontal_query_matrix[:, i * WIDTH : (i + 1) * WIDTH] for i in range(4))
    keys, values, live = row_keys(parts, wk, wv)
    rows = row_attention(spot, kept, chunk, keys, values, live, biases, wq, wg, horizontal_final_matrix)
    rows = [rows] + [lax.ppermute(rows, COLUMN, [(i, i ^ k) for i in range(4)]) for k in (1, 2, 3)]
    back, left = column_attention(
        mine, rows, vertical_query_matrix, vertical_final_matrix, tensor_mean_side_matrix
    )
    back = swap(back)
    left = lax.all_to_all(left, NEAR, 0, 0)
    pair = pair_update(left.reshape(ROWS, SIDE), back, tensor_mean_final_matrix, couple_state)
    return back[: SEQS * BLOCK].reshape(SEQS, BLOCK, WIDTH), pair


def solution(mesh):
    fine = Mesh(mesh.devices.reshape(SIZES), AXES)
    return jax.shard_map(
        per_device,
        mesh=fine,
        in_specs=(
            P(SEQ, RES, None),
            P(SEQ, RES, None),
            P(SEQ, RES),
            P(),
            P(),
            P(),
            P(),
            P(),
            P(),
            P(),
            P(),
        ),
        out_specs=(P(SEQ, RES, None), P(SEQ, RES, None)),
        check_vma=False,
    )
```

time: 183 us -> 151 us (0.83)
  blocking collectives: 23.5 us -> 0 us
  waiting for transfers between devices: 39.4 us -> 28.6 us
  starting transfers between devices: 39.3 us -> 41.5 us
    all_to_all x1 -> x0, blocking collectives: 23.5 us -> none  [per_device(): near = [lax.all_to_all(send, ('yl', 'zl', 'x'), 0, 0) for send in sends]]
    all_to_all x3 -> x1, waiting for transfers between devices: 29.1 us -> 12.4 us  [per_device(): biases = [lax.all_to_all(send.reshape((32,) + send.shape[2:]), RES, 0, 0)]]
    ppermute x5 -> x18, starting transfers between devices: 16.1 us -> 26.1 us  [the longest x3 14.7 us: swap(): return lax.ppermute(array, SWAPPED, swap_pairs(flip))]
    all_to_all x3 -> x1, starting transfers between devices: 12.4 us -> 5.95 us  [per_device(): biases = [lax.all_to_all(send.reshape((32,) + send.shape[2:]), RES, 0, 0)]]
    ppermute x5 -> x18, waiting for transfers between devices: 6.93 us -> 11.3 us  [the longest x3 7.78 us: swap(): return lax.ppermute(array, SWAPPED, swap_pairs(flip))]
    pallas_call x4 -> x7, Pallas kernels: 39.9 us -> 41.1 us  [the longest x3 19.3 us: bias_blocks(): pl.pallas_call(bias_body, grid=(steps,), in_specs=[pl.BlockSpec((BIAS_STE...]
    unnamed x31 -> x48, local copies, waits for them, and re-layouts: 7.81 us -> 8.48 us
  transfers between devices with their start and end apart: 12 -> 23, of which waited for: 8 -> 8; matrix products, arithmetic and copies ran while one was open for 3% -> 4% of each run, Pallas kernels for 11% -> 18%
where the time goes in v2:
time: 151 us
  Pallas kernels  66.5 us (44%)
  starting transfers between devices  41.5 us (27%)
  waiting for transfers between devices  28.6 us (19%)
  local copies, waits for them, and re-layouts  12.6 us (8%)
    pallas_call x3, Pallas kernels, bias_blocks(): pl.pallas_call(bias_body, grid=(steps,), in_specs=[pl.BlockSpec((BIAS_STE...  19.3 us
    pallas_call x1, Pallas kernels, pair_update(): pl.pallas_call(pair_body, grid=(ROWS // PAIR_STEP,), in_specs=[pl.BlockSp...  15.4 us
    ppermute x3, starting transfers between devices, swap(): return lax.ppermute(array, SWAPPED, swap_pairs(flip))  14.7 us
    all_to_all x1, waiting for transfers between devices, per_device(): biases = [lax.all_to_all(send.reshape((32,) + send.shape[2:]), RES, 0, 0)]  12.4 us
    pallas_call x1, Pallas kernels, row_attention(): pl.pallas_call(row_body, grid=(SEQS + 1,), in_specs=[pl.BlockSpec(memory_...  12.3 us
    unnamed x48, local copies, waits for them, and re-layouts  8.48 us
    ppermute x7, starting transfers between devices, shift(): lax.ppermute(array, NEAR, [(z * 4 + i, (z ^ flip) * 4 + (i + step) % 4) f...  8.44 us
    pallas_call x1, Pallas kernels, column_attention(): pl.pallas_call(column_body, in_specs=[pl.BlockSpec(memory_space=pltpu.SME...  8.32 us
  transfers between devices with their start and end apart: 23, of which 8 were waited for; matrix products, arithmetic and copies ran while one was open for 4% of the time, Pallas kernels for 18%

profile of v2, /device:TPU:1, one launch (start us, length us, event | category | flops | bytes accessed | tf_op | source)
XLA Modules:
  0.0 150.6 jit_solution(15413633467662288309)
XLA Ops:
  0.6 0.0 copy-start
  0.7 1.7 %pack_lineup.1 = bf16[264,256]{1,0:T(8,128)(2,1)} custom-call(s32[1]{0:T(128)} %bitcast.5.block_ref, bf16[256,256]{1,0:T(8,128)(2,1)} %bitcast.29, s32[4,64]{1,0:T(4,128)} %filled_ref.1, s32[16,128]{1,0:T(8,128)} %bitcast.32), custom_call_target="tpu_custom_call" | custom-call | tf_op jit(solution)/shard_map/pack_lineup/pallas_call | solution.py:103
  2.4 6.9 %collective-permute-start = (bf16[264,256]{1,0:T(8,128)(2,1)}, bf16[264,256]{1,0:T(8,128)(2,1)S(1)}, u32[]{:S(2)}, u32[]{:S(2)}) collective-permute-start(bf16[264,256]{1,0:T(8,128)(2,1)} %pack_lineup.1), channel_id=1, source_target_pairs={{0,0},{8,32},{16,64},{24,96},{32,8},{40,40},{48,72},{56,104},{64,1... | collective-permute-start | bytes 405512 | tf_op jit(solution)/shard_map/ppermute | solution.py:52
  9.3 1.2 collective-permute-start.1
  10.5 0.1 copy.21.weight_ref
  10.6 5.5 %pair_bias.3.after_ref.refs_0_ = bf16[4,8,64,512]{3,2,1,0:T(8,128)(2,1)} custom-call(bf16[512,64,128]{2,1,0:T(8,128)(2,1)} %pair_ref.7, bf16[128,256]{1,0:T(8,128)(2,1)S(1)} %copy.21.weight_ref), custom_call_target="tpu_custom_call" | custom-call | flops 8589934592 | bytes 6291456 | tf_op jit(solution)/shard_map/pair_bias/pallas_call | solution.py:176
  16.1 0.0 collective-permute-done.x_ref
  16.1 1.8 %collective-permute-done.1.flipped_ref = bf16[264,256]{1,0:T(8,128)(2,1)S(1)} collective-permute-done((bf16[264,256]{1,0:T(8,128)(2,1)}, bf16[264,256]{1,0:T(8,128)(2,1)S(1)}, u32[]{:S(2)}, u32[]{:S(2)}) %collective-permute-start.1) | collective-permute-done | bytes 135200 | tf_op jit(solution)/shard_map/ppermute | solution.py:52
  17.9 0.7 copy-done.15
  18.6 1.9 %norm_lineup.1.refs_0_.refs_16_.refs_1_.own_ref = bf16[2,264,256]{2,1,0:T(8,128)(2,1)} custom-call(bf16[264,256]{1,0:T(8,128)(2,1)} %copy-done.14, bf16[264,256]{1,0:T(8,128)(2,1)} %copy-done.15, bf16[4,8,64,512]{3,2,1,0:T(8,128)(2,1)} %pair_bias.3.after_ref.refs_0_), custom_call_target="tpu_custom_call" | custom-call | tf_op jit(solution)/shard_map/norm_lineup/pallas_call | solution.py:121
  20.5 1.2 collective-permute-start.2
  21.7 1.9 %collective-permute-start.7 = (bf16[2,264,256]{2,1,0:T(8,128)(2,1)}, bf16[2,264,256]{2,1,0:T(8,128)(2,1)S(1)}, u32[]{:S(2)}, u32[]{:S(2)}) collective-permute-start(bf16[2,264,256]{2,1,0:T(8,128)(2,1)} %norm_lineup.1.refs_0_.refs_16_.refs_1_.own_ref), channel_id=1, source_target_pairs={{0,7},{1,4},{2,5},{3,6},{4,3},{5,0},{6,1},{7,2},{8,15},{9,12},{10,... | collective-permute-start | bytes 811016 | tf_op jit(solution)/shard_map/ppermute | solution.py:56
  23.6 1.3 collective-permute-start.3
  24.9 0.7 collective-permute-start.5
  25.6 0.7 collective-permute-start.6
  26.3 1.0 copy-done.1
  27.3 8.3 %pair_bias.4.refs_0_ = bf16[4,8,64,512]{3,2,1,0:T(8,128)(2,1)} custom-call(bf16[512,64,128]{2,1,0:T(8,128)(2,1)} %pair_ref.7, bf16[128,256]{1,0:T(8,128)(2,1)S(1)} %copy.21.weight_ref, bf16[4,8,64,512]{3,2,1,0:T(8,128)(2,1)} %pair_bias.3.after_ref.refs_0_, bf16[2,264,256]{2,1,0:T(8,128)(2,1)S(1)} %copy-done.1), custom_call_target="tpu_custom_call", output_to_operand_aliasing={{}: (2, {})} | custom-call | flops 8589934592 | bytes 6291456 | tf_op jit(solution)/shard_map/pair_bias/pallas_call | solution.py:176
  35.6 0.0 collective-permute-start.4
  35.6 0.0 collective-permute-done.7.refs_6_.refs_22_.refs_5_
  35.6 2.7 %collective-permute-start.8 = (bf16[2,264,256]{2,1,0:T(8,128)(2,1)S(1)}, bf16[2,264,256]{2,1,0:T(8,128)(2,1)S(1)}, u32[]{:S(2)}, u32[]{:S(2)}) collective-permute-start(bf16[2,264,256]{2,1,0:T(8,128)(2,1)S(1)} %collective-permute-done.7.refs_6_.refs_22_.refs_5_), channel_id=1, source_target_pairs={{0,3},{1,0},{2,1},{3,2},{4,7},{5,4},{6,5},{7,6},{8,11},{9,8},{10,9... | collective-permute-start | bytes 811016 | tf_op jit(solution)/shard_map/ppermute | solution.py:56
  38.3 0.0 collective-permute-done.3.refs_2_.refs_18_
  38.3 2.7 %collective-permute-done.5.refs_4_.refs_20_.refs_3_ = bf16[2,264,256]{2,1,0:T(8,128)(2,1)S(1)} collective-permute-done((bf16[2,264,256]{2,1,0:T(8,128)(2,1)}, bf16[2,264,256]{2,1,0:T(8,128)(2,1)S(1)}, u32[]{:S(2)}, u32[]{:S(2)}) %collective-permute-start.5) | collective-permute-done | bytes 270368 | tf_op jit(solution)/shard_map/ppermute | solution.py:56
  41.0 0.8 copy-done.18
  41.8 5.5 %pair_bias.5.refs_0_ = bf16[4,8,64,512]{3,2,1,0:T(8,128)(2,1)} custom-call(bf16[512,64,128]{2,1,0:T(8,128)(2,1)} %pair_ref.7, bf16[128,256]{1,0:T(8,128)(2,1)S(1)} %copy.21.weight_ref, bf16[4,8,64,512]{3,2,1,0:T(8,128)(2,1)} %pair_bias.4.refs_0_, bf16[2,264,256]{2,1,0:T(8,128)(2,1)S(1)} %collective-permute-done.2.refs_1_.refs_17_, ...), custom_call_target="tpu_custom_call", output_to_operand_aliasing={{}: (2, {})} | custom-call | flops 8589934592 | bytes 6291456 | tf_op jit(solution)/shard_map/pair_bias/pallas_call | solution.py:176
  47.3 0.7 copy-done.10
  48.0 0.7 copy-done.12
  48.7 5.9 %all-to-all-start = ((bf16[32,64,512]{2,1,0:T(8,128)(2,1)}), bf16[32,64,512]{2,1,0:T(8,128)(2,1)S(1)}, u32[]{:S(2)}, u32[]{:S(2)}) async-start(bf16[32,64,512]{2,1,0:T(8,128)(2,1)} %bitcast.23), calls=%async_computation | async-start | bytes 4194304 | tf_op jit(solution)/shard_map/all_to_all | solution.py:546
  54.7 0.8 collective-permute-start.9
  55.6 0.1 collective-permute-start.10
  55.7 0.4 collective-permute-start.15
  56.1 0.1 collective-permute-start.11
  56.2 0.4 collective-permute-start.13
  56.6 0.1 collective-permute-done.9.refs_8_.refs_24_
  56.7 0.4 collective-permute-start.14
  57.1 0.0 collective-permute-done.10.refs_9_.refs_25_
  57.1 0.4 collective-permute-start.12
  57.5 0.6 collective-permute-done.15.refs_14_.refs_30_
  58.1 0.7 copy-done.21
  58.8 0.4 collective-permute-start.16
  59.2 1.8 %fusion = (bf16[256,256]{1,0:T(8,128)(2,1)}, bf16[256,256]{1,0:T(8,128)(2,1)S(1)}, bf16[256,256]{1,0:T(8,128)(2,1)}, bf16[256,256]{1,0:T(8,128)(2,1)}) fusion(bf16[256,1024]{1,0:T(8,128)(2,1)} %param.15), kind=kLoop, calls=%fused_computation.3 | loop fusion | bytes 1048576 | tf_op jit(solution)/shard_map/slice | solution.py:547
  61.1 0.8 copy.28
  61.8 0.6 pad_add_fusion.spot_ref
  62.4 0.7 copy-done.22
  63.1 7.6 %row_keys.1 = (bf16[4,2048,256]{2,1,0:T(8,128)(2,1)}, bf16[4,256,2048]{2,1,0:T(8,128)(2,1)}, f32[256,128]{1,0:T(8,128)}) custom-call(bf16[2,264,256]{2,1,0:T(8,128)(2,1)} %norm_lineup.1.refs_0_.refs_16_.refs_1_.own_ref, bf16[2,264,256]{2,1,0:T(8,128)(2,1)} %copy-done.4, bf16[2,264,256]{2,1,0:T(8,128)(2,1)} %copy-done.5, bf16[2,264,256]{2,1,0:T(8,128)(2,1)} %copy-done.10, ...), custom_call_target="tpu_custom_call" | custom-call | flops 4294967296 | bytes 12582912 | tf_op jit(solution)/shard_map/row_keys/pallas_call | solution.py:225
  70.7 12.4 %all-to-all-done.refs_0_ = bf16[32,64,512]{2,1,0:T(8,128)(2,1)S(1)} async-done(((bf16[32,64,512]{2,1,0:T(8,128)(2,1)}), bf16[32,64,512]{2,1,0:T(8,128)(2,1)S(1)}, u32[]{:S(2)}, u32[]{:S(2)}) %all-to-all-start) | async-done | bytes 2097184 | tf_op jit(solution)/shard_map/all_to_all | solution.py:546
  83.1 1.4 copy-done.9
  84.5 12.3 %row_attention.1.x0_ref = bf16[264,256]{1,0:T(8,128)(2,1)} custom-call(s32[4]{0:T(128)} %pad_add_fusion.spot_ref, bf16[2,264,256]{2,1,0:T(8,128)(2,1)} %norm_lineup.1.refs_0_.refs_16_.refs_1_.own_ref, bf16[264,256]{1,0:T(8,128)(2,1)} %copy-done.14, bf16[4,2048,256]{2,1,0:T(8,128)(2,1)} %get-tuple-element.7.key_ref, ...), custom_call_target="tpu_custom_call" | custom-call | flops 12884901888 | bytes 12582912 | tf_op jit(solution)/shard_map/row_attention/pallas_call | solution.py:328
  96.8 0.9 collective-permute-start.17
  97.6 1.5 collective-permute-start.18
  99.1 3.3 %collective-permute-start.19 = (bf16[264,256]{1,0:T(8,128)(2,1)}, bf16[264,256]{1,0:T(8,128)(2,1)S(1)}, u32[]{:S(2)}, u32[]{:S(2)}) collective-permute-start(bf16[264,256]{1,0:T(8,128)(2,1)} %row_attention.1.x0_ref), channel_id=1, source_target_pairs={{0,24},{8,16},{16,8},{24,0},{1,25},{9,17},{17,9},{25,1},{2,26},{10... | collective-permute-start | bytes 405512 | tf_op jit(solution)/shard_map/ppermute | solution.py:550
  102.5 0.1 copy.25.left_ref
  102.7 0.1 copy.26.right_ref
  102.8 0.4 collective-permute-done.18.x2_ref
  103.2 4.5 %collective-permute-done.19.x3_ref = bf16[264,256]{1,0:T(8,128)(2,1)S(1)} collective-permute-done((bf16[264,256]{1,0:T(8,128)(2,1)}, bf16[264,256]{1,0:T(8,128)(2,1)S(1)}, u32[]{:S(2)}, u32[]{:S(2)}) %collective-permute-start.19) | collective-permute-done | bytes 135200 | tf_op jit(solution)/shard_map/ppermute | solution.py:550
  107.7 0.9 copy-done.7
  108.6 8.3 %column_attention.1 = (bf16[448,256]{1,0:T(8,128)(2,1)S(1)}, bf16[8,64,640]{2,1,0:T(8,128)(2,1)}) custom-call(s32[1]{0:T(128)} %bitcast.mine_ref, bf16[264,256]{1,0:T(8,128)(2,1)S(1)} %copy-done.7, bf16[264,256]{1,0:T(8,128)(2,1)S(1)} %collective-permute-done.17.x1_ref, bf16[264,256]{1,0:T(8,128)(2,1)S(1)} %collective-permute-done.18.x2_ref, ...), custom_call_target="tpu_custom_call" | custom-call | flops 4294967296 | bytes 3145728 | tf_op jit(solution)/shard_map/column_attention/pallas_call | solution.py:428
  116.9 3.8 %all-to-all-start.1 = ((bf16[8,64,640]{2,1,0:T(8,128)(2,1)}), bf16[8,64,640]{2,1,0:T(8,128)(2,1)S(1)}, u32[]{:S(2)}, u32[]{:S(2)}) async-start(bf16[8,64,640]{2,1,0:T(8,128)(2,1)} %get-tuple-element.11), calls=%async_computation.1 | async-start | bytes 1310720 | tf_op jit(solution)/shard_map/all_to_all | solution.py:555
  120.7 6.6 %collective-permute-start.20 = (bf16[448,256]{1,0:T(8,128)(2,1)S(1)}, bf16[448,256]{1,0:T(8,128)(2,1)S(1)}, u32[]{:S(2)}, u32[]{:S(2)}) collective-permute-start(bf16[448,256]{1,0:T(8,128)(2,1)S(1)} %get-tuple-element.10), channel_id=1, source_target_pairs={{0,0},{8,32},{16,64},{24,96},{32,8},{40,40},{48,72},{56,104},{64,1... | collective-permute-start | bytes 688136 | tf_op jit(solution)/shard_map/ppermute | solution.py:52
  127.3 0.1 copy.27
  127.4 0.1 copy.31
  127.5 1.1 pad.4.w_ref
  128.6 6.0 %collective-permute-done.20.b_ref = bf16[448,256]{1,0:T(8,128)(2,1)S(1)} collective-permute-done((bf16[448,256]{1,0:T(8,128)(2,1)S(1)}, bf16[448,256]{1,0:T(8,128)(2,1)S(1)}, u32[]{:S(2)}, u32[]{:S(2)}) %collective-permute-start.20) | collective-permute-done | bytes 229408 | tf_op jit(solution)/shard_map/ppermute | solution.py:52
  134.6 0.7 slice.28
  135.2 15.4 %pair_update.1 = bf16[512,64,128]{2,1,0:T(8,128)(2,1)} custom-call(bf16[512,640]{1,0:T(8,128)(2,1)S(1)} %bitcast.22, bf16[448,256]{1,0:T(8,128)(2,1)S(1)} %collective-permute-done.20.b_ref, bf16[128,4096]{1,0:T(8,128)(2,1)} %pad.4.w_ref, bf16[512,64,128]{2,1,0:T(8,128)(2,1)} %pair_ref.7), custom_call_target="tpu_custom_call" | custom-call | flops 8589934592 | bytes 18874368 | tf_op jit(solution)/shard_map/pair_update/pallas_call | solution.py:496
  (52 shorter events, 0.2 us)
Async XLA Ops:
  0.6 9.8 %copy-start = (bf16[128,8]{0,1:T(8,128)(2,1)S(1)}, bf16[128,8]{0,1:T(8,128)(2,1)}, u32[]{:S(2)}) copy-start(bf16[128,8]{0,1:T(8,128)(2,1)} %param.17) | copy-start | bytes 6148
  2.4 13.7 %collective-permute-start = (bf16[264,256]{1,0:T(8,128)(2,1)}, bf16[264,256]{1,0:T(8,128)(2,1)S(1)}, u32[]{:S(2)}, u32[]{:S(2)}) collective-permute-start(bf16[264,256]{1,0:T(8,128)(2,1)} %pack_lineup.1), channel_id=1, source_target_pairs={{0,0},{8,32},{16,64},{24,96},{32,8},{40,40},{48,72},{56,104},{64,1... | collective-permute-start | bytes 405512 | tf_op jit(solution)/shard_map/ppermute | solution.py:52
  9.3 8.6 %collective-permute-start.1 = (bf16[264,256]{1,0:T(8,128)(2,1)}, bf16[264,256]{1,0:T(8,128)(2,1)S(1)}, u32[]{:S(2)}, u32[]{:S(2)}) collective-permute-start(bf16[264,256]{1,0:T(8,128)(2,1)} %pack_lineup.1), channel_id=1, source_target_pairs={{0,64},{8,96},{16,0},{24,32},{32,72},{40,104},{48,8},{56,40},{64,8... | collective-permute-start | bytes 405512 | tf_op jit(solution)/shard_map/ppermute | solution.py:52
  16.1 1.8 %copy-start.14 = (bf16[264,256]{1,0:T(8,128)(2,1)}, bf16[264,256]{1,0:T(8,128)(2,1)S(1)}, u32[]{:S(2)}) copy-start(bf16[264,256]{1,0:T(8,128)(2,1)S(1)} %collective-permute-done.x_ref) | copy-start | bytes 405508
  17.9 0.7 copy-start.15
  20.5 15.1 %collective-permute-start.2 = (bf16[2,264,256]{2,1,0:T(8,128)(2,1)}, bf16[2,264,256]{2,1,0:T(8,128)(2,1)S(1)}, u32[]{:S(2)}, u32[]{:S(2)}) collective-permute-start(bf16[2,264,256]{2,1,0:T(8,128)(2,1)} %norm_lineup.1.refs_0_.refs_16_.refs_1_.own_ref), channel_id=1, source_target_pairs={{0,1},{1,2},{2,3},{3,0},{4,5},{5,6},{6,7},{7,4},{8,9},{9,10},{10,1... | collective-permute-start | bytes 811016 | tf_op jit(solution)/shard_map/ppermute | solution.py:56
  21.7 13.9 %collective-permute-start.7 = (bf16[2,264,256]{2,1,0:T(8,128)(2,1)}, bf16[2,264,256]{2,1,0:T(8,128)(2,1)S(1)}, u32[]{:S(2)}, u32[]{:S(2)}) collective-permute-start(bf16[2,264,256]{2,1,0:T(8,128)(2,1)} %norm_lineup.1.refs_0_.refs_16_.refs_1_.own_ref), channel_id=1, source_target_pairs={{0,7},{1,4},{2,5},{3,6},{4,3},{5,0},{6,1},{7,2},{8,15},{9,12},{10,... | collective-permute-start | bytes 811016 | tf_op jit(solution)/shard_map/ppermute | solution.py:56
  23.6 14.7 %collective-permute-start.3 = (bf16[2,264,256]{2,1,0:T(8,128)(2,1)}, bf16[2,264,256]{2,1,0:T(8,128)(2,1)S(1)}, u32[]{:S(2)}, u32[]{:S(2)}) collective-permute-start(bf16[2,264,256]{2,1,0:T(8,128)(2,1)} %norm_lineup.1.refs_0_.refs_16_.refs_1_.own_ref), channel_id=1, source_target_pairs={{0,3},{1,0},{2,1},{3,2},{4,7},{5,4},{6,5},{7,6},{8,11},{9,8},{10,9... | collective-permute-start | bytes 811016 | tf_op jit(solution)/shard_map/ppermute | solution.py:56
  24.9 16.1 %collective-permute-start.5 = (bf16[2,264,256]{2,1,0:T(8,128)(2,1)}, bf16[2,264,256]{2,1,0:T(8,128)(2,1)S(1)}, u32[]{:S(2)}, u32[]{:S(2)}) collective-permute-start(bf16[2,264,256]{2,1,0:T(8,128)(2,1)} %norm_lineup.1.refs_0_.refs_16_.refs_1_.own_ref), channel_id=1, source_target_pairs={{0,4},{1,5},{2,6},{3,7},{4,0},{5,1},{6,2},{7,3},{8,12},{9,13},{10,... | collective-permute-start | bytes 811016 | tf_op jit(solution)/shard_map/ppermute | solution.py:56
  25.6 15.4 %collective-permute-start.6 = (bf16[2,264,256]{2,1,0:T(8,128)(2,1)}, bf16[2,264,256]{2,1,0:T(8,128)(2,1)S(1)}, u32[]{:S(2)}, u32[]{:S(2)}) collective-permute-start(bf16[2,264,256]{2,1,0:T(8,128)(2,1)} %norm_lineup.1.refs_0_.refs_16_.refs_1_.own_ref), channel_id=1, source_target_pairs={{0,5},{1,6},{2,7},{3,4},{4,1},{5,2},{6,3},{7,0},{8,13},{9,14},{10,... | collective-permute-start | bytes 811016 | tf_op jit(solution)/shard_map/ppermute | solution.py:56
  26.3 1.0 copy-start.1
  35.6 20.0 %copy-start.4 = (bf16[2,264,256]{2,1,0:T(8,128)(2,1)}, bf16[2,264,256]{2,1,0:T(8,128)(2,1)S(1)}, u32[]{:S(2)}) copy-start(bf16[2,264,256]{2,1,0:T(8,128)(2,1)S(1)} %collective-permute-done.2.refs_1_.refs_17_) | copy-start | bytes 811012
  35.6 11.7 %collective-permute-start.4 = (bf16[2,264,256]{2,1,0:T(8,128)(2,1)S(1)}, bf16[2,264,256]{2,1,0:T(8,128)(2,1)S(1)}, u32[]{:S(2)}, u32[]{:S(2)}) collective-permute-start(bf16[2,264,256]{2,1,0:T(8,128)(2,1)S(1)} %collective-permute-done.2.refs_1_.refs_17_), channel_id=1, source_target_pairs={{0,1},{1,2},{2,3},{3,0},{4,5},{5,6},{6,7},{7,4},{8,9},{9,10},{10,1... | collective-permute-start | bytes 811016 | tf_op jit(solution)/shard_map/ppermute | solution.py:56
  35.6 5.4 %copy-start.17 = (bf16[2,264,256]{2,1,0:T(8,128)(2,1)}, bf16[2,264,256]{2,1,0:T(8,128)(2,1)S(1)}, u32[]{:S(2)}) copy-start(bf16[2,264,256]{2,1,0:T(8,128)(2,1)S(1)} %collective-permute-done.7.refs_6_.refs_22_.refs_5_) | copy-start | bytes 811012
  35.6 11.7 %collective-permute-start.8 = (bf16[2,264,256]{2,1,0:T(8,128)(2,1)S(1)}, bf16[2,264,256]{2,1,0:T(8,128)(2,1)S(1)}, u32[]{:S(2)}, u32[]{:S(2)}) collective-permute-start(bf16[2,264,256]{2,1,0:T(8,128)(2,1)S(1)} %collective-permute-done.7.refs_6_.refs_22_.refs_5_), channel_id=1, source_target_pairs={{0,3},{1,0},{2,1},{3,2},{4,7},{5,4},{6,5},{7,6},{8,11},{9,8},{10,9... | collective-permute-start | bytes 811016 | tf_op jit(solution)/shard_map/ppermute | solution.py:56
  38.3 17.8 %copy-start.5 = (bf16[2,264,256]{2,1,0:T(8,128)(2,1)}, bf16[2,264,256]{2,1,0:T(8,128)(2,1)S(1)}, u32[]{:S(2)}) copy-start(bf16[2,264,256]{2,1,0:T(8,128)(2,1)S(1)} %collective-permute-done.3.refs_2_.refs_18_) | copy-start | bytes 811012
  41.0 15.2 %copy-start.6 = (bf16[2,264,256]{2,1,0:T(8,128)(2,1)}, bf16[2,264,256]{2,1,0:T(8,128)(2,1)S(1)}, u32[]{:S(2)}) copy-start(bf16[2,264,256]{2,1,0:T(8,128)(2,1)S(1)} %collective-permute-done.5.refs_4_.refs_20_.refs_3_) | copy-start | bytes 811012
  41.0 0.8 copy-start.18
  47.3 0.7 copy-start.10
  48.0 0.7 copy-start.12
  48.7 6.0 %copy-start.2 = (bf16[2,264,256]{2,1,0:T(8,128)(2,1)S(1)}, bf16[2,264,256]{2,1,0:T(8,128)(2,1)}, u32[]{:S(2)}) copy-start(bf16[2,264,256]{2,1,0:T(8,128)(2,1)} %norm_lineup.1.refs_0_.refs_16_.refs_1_.own_ref) | copy-start | bytes 811012
  48.7 8.4 %copy-start.11 = (bf16[2,264,256]{2,1,0:T(8,128)(2,1)S(1)}, bf16[2,264,256]{2,1,0:T(8,128)(2,1)}, u32[]{:S(2)}) copy-start(bf16[2,264,256]{2,1,0:T(8,128)(2,1)} %copy-done.10) | copy-start | bytes 811012
  48.7 34.3 %all-to-all-start = ((bf16[32,64,512]{2,1,0:T(8,128)(2,1)}), bf16[32,64,512]{2,1,0:T(8,128)(2,1)S(1)}, u32[]{:S(2)}, u32[]{:S(2)}) async-start(bf16[32,64,512]{2,1,0:T(8,128)(2,1)} %bitcast.23), calls=%async_computation | async-start | bytes 4194304 | tf_op jit(solution)/shard_map/all_to_all | solution.py:546
  54.7 2.0 %collective-permute-start.9 = (bf16[2,264,256]{2,1,0:T(8,128)(2,1)S(1)}, bf16[2,264,256]{2,1,0:T(8,128)(2,1)S(1)}, u32[]{:S(2)}, u32[]{:S(2)}) collective-permute-start(bf16[2,264,256]{2,1,0:T(8,128)(2,1)S(1)} %copy-done.2), channel_id=1, source_target_pairs={{0,32},{32,0},{1,33},{33,1},{2,34},{34,2},{3,35},{35,3},{4,36},{36... | collective-permute-start | bytes 811016 | tf_op jit(solution)/shard_map/ppermute | solution.py:545
  55.6 1.6 %collective-permute-start.10 = (bf16[2,264,256]{2,1,0:T(8,128)(2,1)S(1)}, bf16[2,264,256]{2,1,0:T(8,128)(2,1)S(1)}, u32[]{:S(2)}, u32[]{:S(2)}) collective-permute-start(bf16[2,264,256]{2,1,0:T(8,128)(2,1)S(1)} %collective-permute-done.2.refs_1_.refs_17_), channel_id=1, source_target_pairs={{0,32},{32,0},{1,33},{33,1},{2,34},{34,2},{3,35},{35,3},{4,36},{36... | collective-permute-start | bytes 811016 | tf_op jit(solution)/shard_map/ppermute | solution.py:545
  55.7 2.4 %collective-permute-start.15 = (bf16[2,264,256]{2,1,0:T(8,128)(2,1)}, bf16[2,264,256]{2,1,0:T(8,128)(2,1)S(1)}, u32[]{:S(2)}, u32[]{:S(2)}) collective-permute-start(bf16[2,264,256]{2,1,0:T(8,128)(2,1)} %copy-done.17), channel_id=1, source_target_pairs={{0,32},{32,0},{1,33},{33,1},{2,34},{34,2},{3,35},{35,3},{4,36},{36... | collective-permute-start | bytes 811016 | tf_op jit(solution)/shard_map/ppermute | solution.py:545
  56.1 6.3 %collective-permute-start.11 = (bf16[2,264,256]{2,1,0:T(8,128)(2,1)S(1)}, bf16[2,264,256]{2,1,0:T(8,128)(2,1)}, u32[]{:S(2)}, u32[]{:S(2)}) collective-permute-start(bf16[2,264,256]{2,1,0:T(8,128)(2,1)S(1)} %collective-permute-done.3.refs_2_.refs_18_), channel_id=1, source_target_pairs={{0,32},{32,0},{1,33},{33,1},{2,34},{34,2},{3,35},{35,3},{4,36},{36... | collective-permute-start | bytes 811016 | tf_op jit(solution)/shard_map/ppermute | solution.py:545
  56.2 6.2 %collective-permute-start.13 = (bf16[2,264,256]{2,1,0:T(8,128)(2,1)S(1)}, bf16[2,264,256]{2,1,0:T(8,128)(2,1)}, u32[]{:S(2)}, u32[]{:S(2)}) collective-permute-start(bf16[2,264,256]{2,1,0:T(8,128)(2,1)S(1)} %collective-permute-done.5.refs_4_.refs_20_.refs_3_), channel_id=1, source_target_pairs={{0,32},{32,0},{1,33},{33,1},{2,34},{34,2},{3,35},{35,3},{4,36},{36... | collective-permute-start | bytes 811016 | tf_op jit(solution)/shard_map/ppermute | solution.py:545
  56.7 1.4 copy-start.19
  56.7 5.7 %collective-permute-start.14 = (bf16[2,264,256]{2,1,0:T(8,128)(2,1)}, bf16[2,264,256]{2,1,0:T(8,128)(2,1)S(1)}, u32[]{:S(2)}, u32[]{:S(2)}) collective-permute-start(bf16[2,264,256]{2,1,0:T(8,128)(2,1)} %copy-done.18), channel_id=1, source_target_pairs={{0,32},{32,0},{1,33},{33,1},{2,34},{34,2},{3,35},{35,3},{4,36},{36... | collective-permute-start | bytes 811016 | tf_op jit(solution)/shard_map/ppermute | solution.py:545
  57.1 1.0 copy-start.20
  57.1 5.3 %collective-permute-start.12 = (bf16[2,264,256]{2,1,0:T(8,128)(2,1)S(1)}, bf16[2,264,256]{2,1,0:T(8,128)(2,1)}, u32[]{:S(2)}, u32[]{:S(2)}) collective-permute-start(bf16[2,264,256]{2,1,0:T(8,128)(2,1)S(1)} %copy-done.11), channel_id=1, source_target_pairs={{0,32},{32,0},{1,33},{33,1},{2,34},{34,2},{3,35},{35,3},{4,36},{36... | collective-permute-start | bytes 811016 | tf_op jit(solution)/shard_map/ppermute | solution.py:545
  58.1 0.7 copy-start.21
  58.8 3.6 %collective-permute-start.16 = (bf16[2,264,256]{2,1,0:T(8,128)(2,1)}, bf16[2,264,256]{2,1,0:T(8,128)(2,1)}, u32[]{:S(2)}, u32[]{:S(2)}) collective-permute-start(bf16[2,264,256]{2,1,0:T(8,128)(2,1)} %copy-done.12), channel_id=1, source_target_pairs={{0,32},{32,0},{1,33},{33,1},{2,34},{34,2},{3,35},{35,3},{4,36},{36... | collective-permute-start | bytes 811016 | tf_op jit(solution)/shard_map/ppermute | solution.py:545
  62.4 0.7 copy-start.22
  83.1 1.4 copy-start.9
  84.5 18.0 %copy-start.16 = (bf16[256,64]{0,1:T(8,128)(2,1)S(1)}, bf16[256,64]{0,1:T(8,128)(2,1)}, u32[]{:S(2)}) copy-start(bf16[256,64]{0,1:T(8,128)(2,1)} %param.20) | copy-start | bytes 98308
  84.5 23.3 %copy-start.3 = (bf16[256,1024]{1,0:T(8,128)(2,1)S(1)}, bf16[256,1024]{1,0:T(8,128)(2,1)}, u32[]{:S(2)}) copy-start(bf16[256,1024]{1,0:T(8,128)(2,1)} %w_ref.1) | copy-start | bytes 1572868
  84.5 23.3 %copy-start.8 = (bf16[256,256]{1,0:T(8,128)(2,1)S(1)}, bf16[256,256]{1,0:T(8,128)(2,1)}, u32[]{:S(2)}) copy-start(bf16[256,256]{1,0:T(8,128)(2,1)} %wo_ref.1) | copy-start | bytes 393220
  96.8 6.0 %collective-permute-start.17 = (bf16[264,256]{1,0:T(8,128)(2,1)}, bf16[264,256]{1,0:T(8,128)(2,1)S(1)}, u32[]{:S(2)}, u32[]{:S(2)}) collective-permute-start(bf16[264,256]{1,0:T(8,128)(2,1)} %row_attention.1.x0_ref), channel_id=1, source_target_pairs={{0,8},{8,0},{16,24},{24,16},{1,9},{9,1},{17,25},{25,17},{2,10},{10... | collective-permute-start | bytes 405512 | tf_op jit(solution)/shard_map/ppermute | solution.py:550
  97.6 5.6 %collective-permute-start.18 = (bf16[264,256]{1,0:T(8,128)(2,1)}, bf16[264,256]{1,0:T(8,128)(2,1)S(1)}, u32[]{:S(2)}, u32[]{:S(2)}) collective-permute-start(bf16[264,256]{1,0:T(8,128)(2,1)} %row_attention.1.x0_ref), channel_id=1, source_target_pairs={{0,16},{8,24},{16,0},{24,8},{1,17},{9,25},{17,1},{25,9},{2,18},{10... | collective-permute-start | bytes 405512 | tf_op jit(solution)/shard_map/ppermute | solution.py:550
  99.1 8.6 %collective-permute-start.19 = (bf16[264,256]{1,0:T(8,128)(2,1)}, bf16[264,256]{1,0:T(8,128)(2,1)S(1)}, u32[]{:S(2)}, u32[]{:S(2)}) collective-permute-start(bf16[264,256]{1,0:T(8,128)(2,1)} %row_attention.1.x0_ref), channel_id=1, source_target_pairs={{0,24},{8,16},{16,8},{24,0},{1,25},{9,17},{17,9},{25,1},{2,26},{10... | collective-permute-start | bytes 405512 | tf_op jit(solution)/shard_map/ppermute | solution.py:550
  107.7 0.9 copy-start.7
  108.6 18.7 %copy-start.13 = (bf16[1024,128]{1,0:T(8,128)(2,1)S(1)}, bf16[1024,128]{1,0:T(8,128)(2,1)}, u32[]{:S(2)}) copy-start(bf16[1024,128]{1,0:T(8,128)(2,1)} %param.21) | copy-start | bytes 786436
  116.9 18.3 %all-to-all-start.1 = ((bf16[8,64,640]{2,1,0:T(8,128)(2,1)}), bf16[8,64,640]{2,1,0:T(8,128)(2,1)S(1)}, u32[]{:S(2)}, u32[]{:S(2)}) async-start(bf16[8,64,640]{2,1,0:T(8,128)(2,1)} %get-tuple-element.11), calls=%async_computation.1 | async-start | bytes 1310720 | tf_op jit(solution)/shard_map/all_to_all | solution.py:555
  120.7 13.9 %collective-permute-start.20 = (bf16[448,256]{1,0:T(8,128)(2,1)S(1)}, bf16[448,256]{1,0:T(8,128)(2,1)S(1)}, u32[]{:S(2)}, u32[]{:S(2)}) collective-permute-start(bf16[448,256]{1,0:T(8,128)(2,1)S(1)} %get-tuple-element.10), channel_id=1, source_target_pairs={{0,0},{8,32},{16,64},{24,96},{32,8},{40,40},{48,72},{56,104},{64,1... | collective-permute-start | bytes 688136 | tf_op jit(solution)/shard_map/ppermute | solution.py:52

commit v3 on v2

--- a/solution.py
+++ b/solution.py
@@ -359,7 +359,7 @@
 
 
 def column_body(
-    mine_ref, x0_ref, x1_ref, x2_ref, x3_ref, w_ref, wo_ref, left_ref, right_ref, out_ref, a_ref, masks,
+    mine_ref, x0_ref, x3_ref, x2_ref, x1_ref, w_ref, wo_ref, left_ref, right_ref, out_ref, a_ref, masks,
 ):
     x_refs = (x0_ref, x1_ref, x2_ref, x3_ref)
     mine = mine_ref[0]
@@ -445,9 +445,38 @@
 STRIDE = BLOCK + 8
 
 
-def pair_body(a_ref, b_ref, w_ref, pair_ref, out_ref, table, update):
-    @pl.when(pl.program_id(0) == 0)
-    def _():
+def pair_body(a_ref, b_ref, w_ref, pair_ref, out_ref, aligned_ref, table, even, odd):
+    step = pl.program_id(0)
+    steps = ROWS // PAIR_STEP
+    per_dot = 4
+
+    def multiply(update):
+        left = a_ref[:, :LEFT]
+        count = dot(a_ref[:, LEFT:], b_ref[BACK - BLOCK :, :128], NT)
+        scale = 1.0 / jnp.maximum(count, 1.0)
+        for j in range(0, BLOCK, per_dot):
+            part = dot(left, table[:, j * PAIR : (j + per_dot) * PAIR])
+            for d in range(per_dot):
+                update[pl.ds(j + d, PAIR_STEP, stride=STRIDE), :] = (
+                    part[:, d * PAIR : (d + 1) * PAIR] * scale[:, j + d : j + d + 1]
+                )
+            yield
+
+    def finish(update):
+        share = PAIR_STEP * per_dot // BLOCK
+        for first in range(0, PAIR_STEP, share):
+            for i in range(first, first + share):
+                rows = update[i * STRIDE : i * STRIDE + BLOCK, :]
+                out_ref[i] = (pair_ref[i].astype(F32) + rows).astype(BF16)
+            yield
+
+    def run(*work):
+        for _ in itertools.zip_longest(*work):
+            pass
+
+    @pl.when(step == 0)
+    def _():
+        aligned_ref[...] = b_ref[: SEQS * BLOCK, :]
         keep = (iota((16 * ALL_SEQS, LEFT), 1) % ALL_SEQS) == (iota((16 * ALL_SEQS, LEFT), 0) % ALL_SEQS)
         fold = (iota((LEFT, 128), 0) // ALL_SEQS == iota((LEFT, 128), 1)).astype(BF16)
 
@@ -469,46 +498,46 @@
             return carry
 
         lax.fori_loop(0, BLOCK // 16, build, 0)
-
-    left = a_ref[:, :LEFT]
-    count = dot(a_ref[:, LEFT:], b_ref[BACK - BLOCK :, :128], NT)
-    scale = 1.0 / jnp.maximum(count, 1.0)
-    per_dot = 4
-    for j in range(0, BLOCK, per_dot):
-        part = dot(left, table[:, j * PAIR : (j + per_dot) * PAIR])
-        for d in range(per_dot):
-            update[pl.ds(j + d, PAIR_STEP, stride=STRIDE), :] = (
-                part[:, d * PAIR : (d + 1) * PAIR] * scale[:, j + d : j + d + 1]
-            )
-
-    def finish(i, carry):
-        rows = update[pl.ds(pl.multiple_of(i * STRIDE, 8), BLOCK), :]
-        out_ref[i] = (pair_ref[i].astype(F32) + rows).astype(BF16)
-        return carry
-
-    lax.fori_loop(0, PAIR_STEP, finish, 0, unroll=4)
+        run(multiply(even))
+
+    @pl.when(step % 2 == 1)
+    def _():
+        run(multiply(odd), finish(even))
+
+    @pl.when(jnp.logical_and(step > 0, jnp.logical_and(step % 2 == 0, step < steps)))
+    def _():
+        run(multiply(even), finish(odd))
+
+    @pl.when(step == steps)
+    def _():
+        run(finish(odd))
 
 
 def pair_update(left, right, final_matrix, couple_state):
     wide = final_matrix.reshape(OUTER, OUTER, PAIR).transpose(1, 0, 2).reshape(OUTER, OUTER * PAIR)
     wide = jnp.pad(wide, ((0, 128 - OUTER), (0, 0)))
-    block = pl.BlockSpec((PAIR_STEP, BLOCK, PAIR), lambda i: (i, 0, 0))
+    steps = ROWS // PAIR_STEP
+    block = pl.BlockSpec((PAIR_STEP, BLOCK, PAIR), lambda i: (jnp.maximum(i - 1, 0), 0, 0))
     return pl.pallas_call(
         pair_body,
-        grid=(ROWS // PAIR_STEP,),
+        grid=(steps + 1,),
         in_specs=[
-            pl.BlockSpec((PAIR_STEP, SIDE), lambda i: (i, 0)),
+            pl.BlockSpec((PAIR_STEP, SIDE), lambda i: (jnp.minimum(i, steps - 1), 0)),
             pl.BlockSpec((BACK, WIDTH), lambda i: (0, 0)),
             pl.BlockSpec((128, OUTER * PAIR), lambda i: (0, 0)),
             block,
         ],
-        out_specs=block,
-        out_shape=jax.ShapeDtypeStruct(couple_state.shape, BF16),
+        out_specs=[block, pl.BlockSpec((SEQS * BLOCK, WIDTH), lambda i: (0, 0))],
+        out_shape=[
+            jax.ShapeDtypeStruct(couple_state.shape, BF16),
+            jax.ShapeDtypeStruct((SEQS * BLOCK, WIDTH), BF16),
+        ],
         scratch_shapes=[
             pltpu.VMEM((LEFT, WIDE), BF16),
             pltpu.VMEM((STRIDE * PAIR_STEP, PAIR), F32),
-        ],
-        compiler_params=pltpu.CompilerParams(vmem_limit_bytes=53 << 20),
+            pltpu.VMEM((STRIDE * PAIR_STEP, PAIR), F32),
+        ],
+        compiler_params=pltpu.CompilerParams(vmem_limit_bytes=57 << 20),
         cost_estimate=pl.CostEstimate(flops=8 << 30, bytes_accessed=18 << 20, transcendentals=0),
         name="pair_update",
     )(left, right, wide, couple_state)
@@ -547,14 +576,14 @@
     wq, wk, wv, wg = (horizontal_query_matrix[:, i * WIDTH : (i + 1) * WIDTH] for i in range(4))
     keys, values, live = row_keys(parts, wk, wv)
     rows = row_attention(spot, kept, chunk, keys, values, live, biases, wq, wg, horizontal_final_matrix)
-    rows = [rows] + [lax.ppermute(rows, COLUMN, [(i, i ^ k) for i in range(4)]) for k in (1, 2, 3)]
+    rows = [rows] + [lax.ppermute(rows, COLUMN, [(i, i ^ k) for i in range(4)]) for k in (3, 2, 1)]
     back, left = column_attention(
         mine, rows, vertical_query_matrix, vertical_final_matrix, tensor_mean_side_matrix
     )
     back = swap(back)
     left = lax.all_to_all(left, NEAR, 0, 0)
-    pair = pair_update(left.reshape(ROWS, SIDE), back, tensor_mean_final_matrix, couple_state)
-    return back[: SEQS * BLOCK].reshape(SEQS, BLOCK, WIDTH), pair
+    pair, aligned = pair_update(left.reshape(ROWS, SIDE), back, tensor_mean_final_matrix, couple_state)
+    return aligned.reshape(SEQS, BLOCK, WIDTH), pair
 
 
 def solution(mesh):

time: 151 us -> 151 us (level)
    unnamed x48 -> x52, local copies, waits for them, and re-layouts: 8.48 us -> 9.36 us
  transfers between devices with their start and end apart: 23 -> 23, of which waited for: 8 -> 9; matrix products, arithmetic and copies ran while one was open for 4% -> 3% of each run, Pallas kernels for 18% -> 18%
where the time goes in v3:
time: 151 us; the launch traced here: 150 us
  Pallas kernels  66.3 us (44%)
  starting transfers between devices  42 us (28%)
  waiting for transfers between devices  27.7 us (18%)
  local copies, waits for them, and re-layouts  12.8 us (8%)
    pallas_call x3, Pallas kernels, bias_blocks(): pl.pallas_call(bias_body, grid=(steps,), in_specs=[pl.BlockSpec((BIAS_STE...  19.3 us
    pallas_call x1, Pallas kernels, pair_update(): pl.pallas_call(pair_body, grid=(steps + 1,), in_specs=[pl.BlockSpec((PAIR...  15.2 us
    ppermute x3, starting transfers between devices, swap(): return lax.ppermute(array, SWAPPED, swap_pairs(flip))  14.4 us
    all_to_all x1, waiting for transfers between devices, per_device(): biases = [lax.all_to_all(send.reshape((32,) + send.shape[2:]), RES, 0, 0)]  12.4 us
    pallas_call x1, Pallas kernels, row_attention(): pl.pallas_call(row_body, grid=(SEQS + 1,), in_specs=[pl.BlockSpec(memory_...  12.3 us
    unnamed x52, local copies, waits for them, and re-layouts  9.36 us
    ppermute x7, starting transfers between devices, shift(): lax.ppermute(array, NEAR, [(z * 4 + i, (z ^ flip) * 4 + (i + step) % 4) f...  8.44 us
    pallas_call x1, Pallas kernels, column_attention(): pl.pallas_call(column_body, in_specs=[pl.BlockSpec(memory_space=pltpu.SME...  8.31 us
  transfers between devices with their start and end apart: 23, of which 9 were waited for; matrix products, arithmetic and copies ran while one was open for 3% of the time, Pallas kernels for 18%

profile of v3, /device:TPU:1, one launch (start us, length us, event | category | flops | bytes accessed | tf_op | source)
XLA Modules:
  0.0 150.4 jit_solution(16105920472412122832)
XLA Ops:
  0.6 0.0 copy-start
  0.7 1.7 %pack_lineup.1 = bf16[264,256]{1,0:T(8,128)(2,1)} custom-call(s32[1]{0:T(128)} %bitcast.5.block_ref, bf16[256,256]{1,0:T(8,128)(2,1)} %bitcast.29, s32[4,64]{1,0:T(4,128)} %filled_ref.1, s32[16,128]{1,0:T(8,128)} %bitcast.31), custom_call_target="tpu_custom_call" | custom-call | tf_op jit(solution)/shard_map/pack_lineup/pallas_call | solution.py:103
  2.4 6.9 %collective-permute-start = (bf16[264,256]{1,0:T(8,128)(2,1)}, bf16[264,256]{1,0:T(8,128)(2,1)S(1)}, u32[]{:S(2)}, u32[]{:S(2)}) collective-permute-start(bf16[264,256]{1,0:T(8,128)(2,1)} %pack_lineup.1), channel_id=1, source_target_pairs={{0,0},{8,32},{16,64},{24,96},{32,8},{40,40},{48,72},{56,104},{64,1... | collective-permute-start | bytes 405512 | tf_op jit(solution)/shard_map/ppermute | solution.py:52
  9.3 1.2 collective-permute-start.1
  10.5 0.1 copy.21.weight_ref
  10.6 5.5 %pair_bias.3.after_ref.refs_0_ = bf16[4,8,64,512]{3,2,1,0:T(8,128)(2,1)} custom-call(bf16[512,64,128]{2,1,0:T(8,128)(2,1)} %pair_ref.7, bf16[128,256]{1,0:T(8,128)(2,1)S(1)} %copy.21.weight_ref), custom_call_target="tpu_custom_call" | custom-call | flops 8589934592 | bytes 6291456 | tf_op jit(solution)/shard_map/pair_bias/pallas_call | solution.py:176
  16.1 1.8 %collective-permute-done.1.flipped_ref = bf16[264,256]{1,0:T(8,128)(2,1)S(1)} collective-permute-done((bf16[264,256]{1,0:T(8,128)(2,1)}, bf16[264,256]{1,0:T(8,128)(2,1)S(1)}, u32[]{:S(2)}, u32[]{:S(2)}) %collective-permute-start.1) | collective-permute-done | bytes 135200 | tf_op jit(solution)/shard_map/ppermute | solution.py:52
  17.9 0.7 copy-done.16
  18.6 1.9 %norm_lineup.1.refs_0_.refs_16_.refs_1_.own_ref = bf16[2,264,256]{2,1,0:T(8,128)(2,1)} custom-call(bf16[264,256]{1,0:T(8,128)(2,1)} %copy-done.15, bf16[264,256]{1,0:T(8,128)(2,1)} %copy-done.16, bf16[4,8,64,512]{3,2,1,0:T(8,128)(2,1)} %pair_bias.3.after_ref.refs_0_), custom_call_target="tpu_custom_call" | custom-call | tf_op jit(solution)/shard_map/norm_lineup/pallas_call | solution.py:121
  20.5 1.2 collective-permute-start.2
  21.7 1.9 %collective-permute-start.7 = (bf16[2,264,256]{2,1,0:T(8,128)(2,1)}, bf16[2,264,256]{2,1,0:T(8,128)(2,1)S(1)}, u32[]{:S(2)}, u32[]{:S(2)}) collective-permute-start(bf16[2,264,256]{2,1,0:T(8,128)(2,1)} %norm_lineup.1.refs_0_.refs_16_.refs_1_.own_ref), channel_id=1, source_target_pairs={{0,7},{1,4},{2,5},{3,6},{4,3},{5,0},{6,1},{7,2},{8,15},{9,12},{10,... | collective-permute-start | bytes 811016 | tf_op jit(solution)/shard_map/ppermute | solution.py:56
  23.6 1.3 collective-permute-start.3
  24.9 0.7 collective-permute-start.5
  25.6 0.7 collective-permute-start.6
  26.3 1.0 copy-done.1
  27.3 8.3 %pair_bias.4.refs_0_ = bf16[4,8,64,512]{3,2,1,0:T(8,128)(2,1)} custom-call(bf16[512,64,128]{2,1,0:T(8,128)(2,1)} %pair_ref.7, bf16[128,256]{1,0:T(8,128)(2,1)S(1)} %copy.21.weight_ref, bf16[4,8,64,512]{3,2,1,0:T(8,128)(2,1)} %pair_bias.3.after_ref.refs_0_, bf16[2,264,256]{2,1,0:T(8,128)(2,1)S(1)} %copy-done.1), custom_call_target="tpu_custom_call", output_to_operand_aliasing={{}: (2, {})} | custom-call | flops 8589934592 | bytes 6291456 | tf_op jit(solution)/shard_map/pair_bias/pallas_call | solution.py:176
  35.6 0.0 collective-permute-done.2.refs_1_.refs_17_
  35.6 0.0 collective-permute-start.4
  35.6 2.7 %collective-permute-start.8 = (bf16[2,264,256]{2,1,0:T(8,128)(2,1)S(1)}, bf16[2,264,256]{2,1,0:T(8,128)(2,1)S(1)}, u32[]{:S(2)}, u32[]{:S(2)}) collective-permute-start(bf16[2,264,256]{2,1,0:T(8,128)(2,1)S(1)} %collective-permute-done.7.refs_6_.refs_22_.refs_5_), channel_id=1, source_target_pairs={{0,3},{1,0},{2,1},{3,2},{4,7},{5,4},{6,5},{7,6},{8,11},{9,8},{10,9... | collective-permute-start | bytes 811016 | tf_op jit(solution)/shard_map/ppermute | solution.py:56
  38.3 2.8 %collective-permute-done.5.refs_4_.refs_20_.refs_3_ = bf16[2,264,256]{2,1,0:T(8,128)(2,1)S(1)} collective-permute-done((bf16[2,264,256]{2,1,0:T(8,128)(2,1)}, bf16[2,264,256]{2,1,0:T(8,128)(2,1)S(1)}, u32[]{:S(2)}, u32[]{:S(2)}) %collective-permute-start.5) | collective-permute-done | bytes 270368 | tf_op jit(solution)/shard_map/ppermute | solution.py:56
  41.1 0.8 copy-done.19
  41.9 5.5 %pair_bias.5.refs_0_ = bf16[4,8,64,512]{3,2,1,0:T(8,128)(2,1)} custom-call(bf16[512,64,128]{2,1,0:T(8,128)(2,1)} %pair_ref.7, bf16[128,256]{1,0:T(8,128)(2,1)S(1)} %copy.21.weight_ref, bf16[4,8,64,512]{3,2,1,0:T(8,128)(2,1)} %pair_bias.4.refs_0_, bf16[2,264,256]{2,1,0:T(8,128)(2,1)S(1)} %collective-permute-done.2.refs_1_.refs_17_, ...), custom_call_target="tpu_custom_call", output_to_operand_aliasing={{}: (2, {})} | custom-call | flops 8589934592 | bytes 6291456 | tf_op jit(solution)/shard_map/pair_bias/pallas_call | solution.py:176
  47.3 0.7 copy-done.11
  48.1 0.7 copy-done.13
  48.8 5.9 %all-to-all-start = ((bf16[32,64,512]{2,1,0:T(8,128)(2,1)}), bf16[32,64,512]{2,1,0:T(8,128)(2,1)S(1)}, u32[]{:S(2)}, u32[]{:S(2)}) async-start(bf16[32,64,512]{2,1,0:T(8,128)(2,1)} %bitcast.22), calls=%async_computation | async-start | bytes 4194304 | tf_op jit(solution)/shard_map/all_to_all | solution.py:575
  54.7 0.9 collective-permute-start.9
  55.6 0.1 collective-permute-start.10
  55.7 0.4 collective-permute-start.15
  56.1 0.1 collective-permute-start.11
  56.2 0.4 collective-permute-start.13
  56.6 0.1 collective-permute-done.9.refs_8_.refs_24_
  56.8 0.4 collective-permute-start.14
  57.1 0.0 collective-permute-done.10.refs_9_.refs_25_
  57.2 0.4 collective-permute-start.12
  57.5 0.6 collective-permute-done.15.refs_14_.refs_30_
  58.2 0.7 copy-done.22
  58.8 0.4 collective-permute-start.16
  59.2 1.8 %fusion = (bf16[256,256]{1,0:T(8,128)(2,1)}, bf16[256,256]{1,0:T(8,128)(2,1)S(1)}, bf16[256,256]{1,0:T(8,128)(2,1)}, bf16[256,256]{1,0:T(8,128)(2,1)}) fusion(bf16[256,1024]{1,0:T(8,128)(2,1)} %param.15), kind=kLoop, calls=%fused_computation.3 | loop fusion | bytes 1048576 | tf_op jit(solution)/shard_map/slice | solution.py:576
  61.1 0.7 copy.28
  61.8 0.7 pad_add_fusion.spot_ref
  62.5 0.7 copy-done.23
  63.2 7.5 %row_keys.1 = (bf16[4,2048,256]{2,1,0:T(8,128)(2,1)}, bf16[4,256,2048]{2,1,0:T(8,128)(2,1)}, f32[256,128]{1,0:T(8,128)}) custom-call(bf16[2,264,256]{2,1,0:T(8,128)(2,1)} %norm_lineup.1.refs_0_.refs_16_.refs_1_.own_ref, bf16[2,264,256]{2,1,0:T(8,128)(2,1)} %copy-done.4, bf16[2,264,256]{2,1,0:T(8,128)(2,1)} %copy-done.5, bf16[2,264,256]{2,1,0:T(8,128)(2,1)} %copy-done.11, ...), custom_call_target="tpu_custom_call" | custom-call | flops 4294967296 | bytes 12582912 | tf_op jit(solution)/shard_map/row_keys/pallas_call | solution.py:225
  70.7 12.4 %all-to-all-done.refs_0_ = bf16[32,64,512]{2,1,0:T(8,128)(2,1)S(1)} async-done(((bf16[32,64,512]{2,1,0:T(8,128)(2,1)}), bf16[32,64,512]{2,1,0:T(8,128)(2,1)S(1)}, u32[]{:S(2)}, u32[]{:S(2)}) %all-to-all-start) | async-done | bytes 2097184 | tf_op jit(solution)/shard_map/all_to_all | solution.py:575
  83.1 1.4 copy-done.9
  84.5 12.3 %row_attention.1.x0_ref = bf16[264,256]{1,0:T(8,128)(2,1)} custom-call(s32[4]{0:T(128)} %pad_add_fusion.spot_ref, bf16[2,264,256]{2,1,0:T(8,128)(2,1)} %norm_lineup.1.refs_0_.refs_16_.refs_1_.own_ref, bf16[264,256]{1,0:T(8,128)(2,1)} %copy-done.15, bf16[4,2048,256]{2,1,0:T(8,128)(2,1)} %get-tuple-element.9.key_ref, ...), custom_call_target="tpu_custom_call" | custom-call | flops 12884901888 | bytes 12582912 | tf_op jit(solution)/shard_map/row_attention/pallas_call | solution.py:328
  96.8 2.0 %collective-permute-start.17 = (bf16[264,256]{1,0:T(8,128)(2,1)}, bf16[264,256]{1,0:T(8,128)(2,1)S(1)}, u32[]{:S(2)}, u32[]{:S(2)}) collective-permute-start(bf16[264,256]{1,0:T(8,128)(2,1)} %row_attention.1.x0_ref), channel_id=1, source_target_pairs={{0,24},{8,16},{16,8},{24,0},{1,25},{9,17},{17,9},{25,1},{2,26},{10... | collective-permute-start | bytes 405512 | tf_op jit(solution)/shard_map/ppermute | solution.py:579
  98.8 1.5 %collective-permute-start.18 = (bf16[264,256]{1,0:T(8,128)(2,1)}, bf16[264,256]{1,0:T(8,128)(2,1)S(1)}, u32[]{:S(2)}, u32[]{:S(2)}) collective-permute-start(bf16[264,256]{1,0:T(8,128)(2,1)} %row_attention.1.x0_ref), channel_id=1, source_target_pairs={{0,16},{8,24},{16,0},{24,8},{1,17},{9,25},{17,1},{25,9},{2,18},{10... | collective-permute-start | bytes 405512 | tf_op jit(solution)/shard_map/ppermute | solution.py:579
  100.3 2.1 %collective-permute-start.19 = (bf16[264,256]{1,0:T(8,128)(2,1)}, bf16[264,256]{1,0:T(8,128)(2,1)S(1)}, u32[]{:S(2)}, u32[]{:S(2)}) collective-permute-start(bf16[264,256]{1,0:T(8,128)(2,1)} %row_attention.1.x0_ref), channel_id=1, source_target_pairs={{0,8},{8,0},{16,24},{24,16},{1,9},{9,1},{17,25},{25,17},{2,10},{10... | collective-permute-start | bytes 405512 | tf_op jit(solution)/shard_map/ppermute | solution.py:579
  102.5 0.1 copy.25.left_ref
  102.7 0.1 copy.26.right_ref
  102.8 2.0 %collective-permute-done.17.x3_ref = bf16[264,256]{1,0:T(8,128)(2,1)S(1)} collective-permute-done((bf16[264,256]{1,0:T(8,128)(2,1)}, bf16[264,256]{1,0:T(8,128)(2,1)S(1)}, u32[]{:S(2)}, u32[]{:S(2)}) %collective-permute-start.17) | collective-permute-done | bytes 135200 | tf_op jit(solution)/shard_map/ppermute | solution.py:579
  104.8 0.1 collective-permute-done.18.x2_ref
  104.9 1.8 %collective-permute-done.19.x1_ref = bf16[264,256]{1,0:T(8,128)(2,1)S(1)} collective-permute-done((bf16[264,256]{1,0:T(8,128)(2,1)}, bf16[264,256]{1,0:T(8,128)(2,1)S(1)}, u32[]{:S(2)}, u32[]{:S(2)}) %collective-permute-start.19) | collective-permute-done | bytes 135200 | tf_op jit(solution)/shard_map/ppermute | solution.py:579
  106.7 0.9 copy-done.7
  107.6 8.3 %column_attention.1 = (bf16[448,256]{1,0:T(8,128)(2,1)S(1)}, bf16[8,64,640]{2,1,0:T(8,128)(2,1)}) custom-call(s32[1]{0:T(128)} %bitcast.mine_ref, bf16[264,256]{1,0:T(8,128)(2,1)S(1)} %copy-done.7, bf16[264,256]{1,0:T(8,128)(2,1)S(1)} %collective-permute-done.17.x3_ref, bf16[264,256]{1,0:T(8,128)(2,1)S(1)} %collective-permute-done.18.x2_ref, ...), custom_call_target="tpu_custom_call" | custom-call | flops 4294967296 | bytes 3145728 | tf_op jit(solution)/shard_map/column_attention/pallas_call | solution.py:428
  116.0 4.5 %all-to-all-start.1 = ((bf16[8,64,640]{2,1,0:T(8,128)(2,1)}), bf16[8,64,640]{2,1,0:T(8,128)(2,1)S(1)}, u32[]{:S(2)}, u32[]{:S(2)}) async-start(bf16[8,64,640]{2,1,0:T(8,128)(2,1)} %get-tuple-element.12), calls=%async_computation.1 | async-start | bytes 1310720 | tf_op jit(solution)/shard_map/all_to_all | solution.py:584
  120.5 6.4 %collective-permute-start.20 = (bf16[448,256]{1,0:T(8,128)(2,1)S(1)}, bf16[448,256]{1,0:T(8,128)(2,1)S(1)}, u32[]{:S(2)}, u32[]{:S(2)}) collective-permute-start(bf16[448,256]{1,0:T(8,128)(2,1)S(1)} %get-tuple-element.13), channel_id=1, source_target_pairs={{0,0},{8,32},{16,64},{24,96},{32,8},{40,40},{48,72},{56,104},{64,1... | collective-permute-start | bytes 688136 | tf_op jit(solution)/shard_map/ppermute | solution.py:52
  126.9 0.1 copy.27
  127.0 0.1 copy.31
  127.1 1.1 pad.4.w_ref
  128.2 6.1 %collective-permute-done.20.b_ref = bf16[448,256]{1,0:T(8,128)(2,1)S(1)} collective-permute-done((bf16[448,256]{1,0:T(8,128)(2,1)S(1)}, bf16[448,256]{1,0:T(8,128)(2,1)S(1)}, u32[]{:S(2)}, u32[]{:S(2)}) %collective-permute-start.20) | collective-permute-done | bytes 229408 | tf_op jit(solution)/shard_map/ppermute | solution.py:52
  134.2 0.7 copy-done.24
  134.9 0.3 copy-done.10
  135.2 15.2 %pair_update.1 = (bf16[512,64,128]{2,1,0:T(8,128)(2,1)}, bf16[256,256]{1,0:T(8,128)(2,1)}) custom-call(bf16[512,640]{1,0:T(8,128)(2,1)} %bitcast.27, bf16[448,256]{1,0:T(8,128)(2,1)} %copy-done.24, bf16[128,4096]{1,0:T(8,128)(2,1)} %pad.4.w_ref, bf16[512,64,128]{2,1,0:T(8,128)(2,1)} %pair_ref.7), custom_call_target="tpu_custom_call" | custom-call | flops 8589934592 | bytes 18874368 | tf_op jit(solution)/shard_map/pair_update/pallas_call | solution.py:521
  (55 shorter events, 0.2 us)
Async XLA Ops:
  0.6 9.8 %copy-start = (bf16[128,8]{0,1:T(8,128)(2,1)S(1)}, bf16[128,8]{0,1:T(8,128)(2,1)}, u32[]{:S(2)}) copy-start(bf16[128,8]{0,1:T(8,128)(2,1)} %param.17) | copy-start | bytes 6148
  2.4 13.7 %collective-permute-start = (bf16[264,256]{1,0:T(8,128)(2,1)}, bf16[264,256]{1,0:T(8,128)(2,1)S(1)}, u32[]{:S(2)}, u32[]{:S(2)}) collective-permute-start(bf16[264,256]{1,0:T(8,128)(2,1)} %pack_lineup.1), channel_id=1, source_target_pairs={{0,0},{8,32},{16,64},{24,96},{32,8},{40,40},{48,72},{56,104},{64,1... | collective-permute-start | bytes 405512 | tf_op jit(solution)/shard_map/ppermute | solution.py:52
  9.3 8.6 %collective-permute-start.1 = (bf16[264,256]{1,0:T(8,128)(2,1)}, bf16[264,256]{1,0:T(8,128)(2,1)S(1)}, u32[]{:S(2)}, u32[]{:S(2)}) collective-permute-start(bf16[264,256]{1,0:T(8,128)(2,1)} %pack_lineup.1), channel_id=1, source_target_pairs={{0,64},{8,96},{16,0},{24,32},{32,72},{40,104},{48,8},{56,40},{64,8... | collective-permute-start | bytes 405512 | tf_op jit(solution)/shard_map/ppermute | solution.py:52
  16.1 1.8 %copy-start.15 = (bf16[264,256]{1,0:T(8,128)(2,1)}, bf16[264,256]{1,0:T(8,128)(2,1)S(1)}, u32[]{:S(2)}) copy-start(bf16[264,256]{1,0:T(8,128)(2,1)S(1)} %collective-permute-done.x_ref) | copy-start | bytes 405508
  17.9 0.7 copy-start.16
  20.5 15.1 %collective-permute-start.2 = (bf16[2,264,256]{2,1,0:T(8,128)(2,1)}, bf16[2,264,256]{2,1,0:T(8,128)(2,1)S(1)}, u32[]{:S(2)}, u32[]{:S(2)}) collective-permute-start(bf16[2,264,256]{2,1,0:T(8,128)(2,1)} %norm_lineup.1.refs_0_.refs_16_.refs_1_.own_ref), channel_id=1, source_target_pairs={{0,1},{1,2},{2,3},{3,0},{4,5},{5,6},{6,7},{7,4},{8,9},{9,10},{10,1... | collective-permute-start | bytes 811016 | tf_op jit(solution)/shard_map/ppermute | solution.py:56
  21.7 13.9 %collective-permute-start.7 = (bf16[2,264,256]{2,1,0:T(8,128)(2,1)}, bf16[2,264,256]{2,1,0:T(8,128)(2,1)S(1)}, u32[]{:S(2)}, u32[]{:S(2)}) collective-permute-start(bf16[2,264,256]{2,1,0:T(8,128)(2,1)} %norm_lineup.1.refs_0_.refs_16_.refs_1_.own_ref), channel_id=1, source_target_pairs={{0,7},{1,4},{2,5},{3,6},{4,3},{5,0},{6,1},{7,2},{8,15},{9,12},{10,... | collective-permute-start | bytes 811016 | tf_op jit(solution)/shard_map/ppermute | solution.py:56
  23.6 14.6 %collective-permute-start.3 = (bf16[2,264,256]{2,1,0:T(8,128)(2,1)}, bf16[2,264,256]{2,1,0:T(8,128)(2,1)S(1)}, u32[]{:S(2)}, u32[]{:S(2)}) collective-permute-start(bf16[2,264,256]{2,1,0:T(8,128)(2,1)} %norm_lineup.1.refs_0_.refs_16_.refs_1_.own_ref), channel_id=1, source_target_pairs={{0,3},{1,0},{2,1},{3,2},{4,7},{5,4},{6,5},{7,6},{8,11},{9,8},{10,9... | collective-permute-start | bytes 811016 | tf_op jit(solution)/shard_map/ppermute | solution.py:56
  24.9 16.2 %collective-permute-start.5 = (bf16[2,264,256]{2,1,0:T(8,128)(2,1)}, bf16[2,264,256]{2,1,0:T(8,128)(2,1)S(1)}, u32[]{:S(2)}, u32[]{:S(2)}) collective-permute-start(bf16[2,264,256]{2,1,0:T(8,128)(2,1)} %norm_lineup.1.refs_0_.refs_16_.refs_1_.own_ref), channel_id=1, source_target_pairs={{0,4},{1,5},{2,6},{3,7},{4,0},{5,1},{6,2},{7,3},{8,12},{9,13},{10,... | collective-permute-start | bytes 811016 | tf_op jit(solution)/shard_map/ppermute | solution.py:56
  25.6 15.4 %collective-permute-start.6 = (bf16[2,264,256]{2,1,0:T(8,128)(2,1)}, bf16[2,264,256]{2,1,0:T(8,128)(2,1)S(1)}, u32[]{:S(2)}, u32[]{:S(2)}) collective-permute-start(bf16[2,264,256]{2,1,0:T(8,128)(2,1)} %norm_lineup.1.refs_0_.refs_16_.refs_1_.own_ref), channel_id=1, source_target_pairs={{0,5},{1,6},{2,7},{3,4},{4,1},{5,2},{6,3},{7,0},{8,13},{9,14},{10,... | collective-permute-start | bytes 811016 | tf_op jit(solution)/shard_map/ppermute | solution.py:56
  26.3 1.0 copy-start.1
  35.6 20.0 %copy-start.4 = (bf16[2,264,256]{2,1,0:T(8,128)(2,1)}, bf16[2,264,256]{2,1,0:T(8,128)(2,1)S(1)}, u32[]{:S(2)}) copy-start(bf16[2,264,256]{2,1,0:T(8,128)(2,1)S(1)} %collective-permute-done.2.refs_1_.refs_17_) | copy-start | bytes 811012
  35.6 11.7 %collective-permute-start.4 = (bf16[2,264,256]{2,1,0:T(8,128)(2,1)S(1)}, bf16[2,264,256]{2,1,0:T(8,128)(2,1)S(1)}, u32[]{:S(2)}, u32[]{:S(2)}) collective-permute-start(bf16[2,264,256]{2,1,0:T(8,128)(2,1)S(1)} %collective-permute-done.2.refs_1_.refs_17_), channel_id=1, source_target_pairs={{0,1},{1,2},{2,3},{3,0},{4,5},{5,6},{6,7},{7,4},{8,9},{9,10},{10,1... | collective-permute-start | bytes 811016 | tf_op jit(solution)/shard_map/ppermute | solution.py:56
  35.6 5.5 %copy-start.18 = (bf16[2,264,256]{2,1,0:T(8,128)(2,1)}, bf16[2,264,256]{2,1,0:T(8,128)(2,1)S(1)}, u32[]{:S(2)}) copy-start(bf16[2,264,256]{2,1,0:T(8,128)(2,1)S(1)} %collective-permute-done.7.refs_6_.refs_22_.refs_5_) | copy-start | bytes 811012
  35.6 11.7 %collective-permute-start.8 = (bf16[2,264,256]{2,1,0:T(8,128)(2,1)S(1)}, bf16[2,264,256]{2,1,0:T(8,128)(2,1)S(1)}, u32[]{:S(2)}, u32[]{:S(2)}) collective-permute-start(bf16[2,264,256]{2,1,0:T(8,128)(2,1)S(1)} %collective-permute-done.7.refs_6_.refs_22_.refs_5_), channel_id=1, source_target_pairs={{0,3},{1,0},{2,1},{3,2},{4,7},{5,4},{6,5},{7,6},{8,11},{9,8},{10,9... | collective-permute-start | bytes 811016 | tf_op jit(solution)/shard_map/ppermute | solution.py:56
  38.3 17.9 %copy-start.5 = (bf16[2,264,256]{2,1,0:T(8,128)(2,1)}, bf16[2,264,256]{2,1,0:T(8,128)(2,1)S(1)}, u32[]{:S(2)}) copy-start(bf16[2,264,256]{2,1,0:T(8,128)(2,1)S(1)} %collective-permute-done.3.refs_2_.refs_18_) | copy-start | bytes 811012
  41.0 15.2 %copy-start.6 = (bf16[2,264,256]{2,1,0:T(8,128)(2,1)}, bf16[2,264,256]{2,1,0:T(8,128)(2,1)S(1)}, u32[]{:S(2)}) copy-start(bf16[2,264,256]{2,1,0:T(8,128)(2,1)S(1)} %collective-permute-done.5.refs_4_.refs_20_.refs_3_) | copy-start | bytes 811012
  41.1 0.8 copy-start.19
  47.3 0.7 copy-start.11
  48.1 0.7 copy-start.13
  48.8 6.0 %copy-start.2 = (bf16[2,264,256]{2,1,0:T(8,128)(2,1)S(1)}, bf16[2,264,256]{2,1,0:T(8,128)(2,1)}, u32[]{:S(2)}) copy-start(bf16[2,264,256]{2,1,0:T(8,128)(2,1)} %norm_lineup.1.refs_0_.refs_16_.refs_1_.own_ref) | copy-start | bytes 811012
  48.8 8.4 %copy-start.12 = (bf16[2,264,256]{2,1,0:T(8,128)(2,1)S(1)}, bf16[2,264,256]{2,1,0:T(8,128)(2,1)}, u32[]{:S(2)}) copy-start(bf16[2,264,256]{2,1,0:T(8,128)(2,1)} %copy-done.11) | copy-start | bytes 811012
  48.8 34.3 %all-to-all-start = ((bf16[32,64,512]{2,1,0:T(8,128)(2,1)}), bf16[32,64,512]{2,1,0:T(8,128)(2,1)S(1)}, u32[]{:S(2)}, u32[]{:S(2)}) async-start(bf16[32,64,512]{2,1,0:T(8,128)(2,1)} %bitcast.22), calls=%async_computation | async-start | bytes 4194304 | tf_op jit(solution)/shard_map/all_to_all | solution.py:575
  54.7 2.0 %collective-permute-start.9 = (bf16[2,264,256]{2,1,0:T(8,128)(2,1)S(1)}, bf16[2,264,256]{2,1,0:T(8,128)(2,1)S(1)}, u32[]{:S(2)}, u32[]{:S(2)}) collective-permute-start(bf16[2,264,256]{2,1,0:T(8,128)(2,1)S(1)} %copy-done.2), channel_id=1, source_target_pairs={{0,32},{32,0},{1,33},{33,1},{2,34},{34,2},{3,35},{35,3},{4,36},{36... | collective-permute-start | bytes 811016 | tf_op jit(solution)/shard_map/ppermute | solution.py:574
  55.6 1.6 %collective-permute-start.10 = (bf16[2,264,256]{2,1,0:T(8,128)(2,1)S(1)}, bf16[2,264,256]{2,1,0:T(8,128)(2,1)S(1)}, u32[]{:S(2)}, u32[]{:S(2)}) collective-permute-start(bf16[2,264,256]{2,1,0:T(8,128)(2,1)S(1)} %collective-permute-done.2.refs_1_.refs_17_), channel_id=1, source_target_pairs={{0,32},{32,0},{1,33},{33,1},{2,34},{34,2},{3,35},{35,3},{4,36},{36... | collective-permute-start | bytes 811016 | tf_op jit(solution)/shard_map/ppermute | solution.py:574
  55.7 2.4 %collective-permute-start.15 = (bf16[2,264,256]{2,1,0:T(8,128)(2,1)}, bf16[2,264,256]{2,1,0:T(8,128)(2,1)S(1)}, u32[]{:S(2)}, u32[]{:S(2)}) collective-permute-start(bf16[2,264,256]{2,1,0:T(8,128)(2,1)} %copy-done.18), channel_id=1, source_target_pairs={{0,32},{32,0},{1,33},{33,1},{2,34},{34,2},{3,35},{35,3},{4,36},{36... | collective-permute-start | bytes 811016 | tf_op jit(solution)/shard_map/ppermute | solution.py:574
  56.1 6.3 %collective-permute-start.11 = (bf16[2,264,256]{2,1,0:T(8,128)(2,1)S(1)}, bf16[2,264,256]{2,1,0:T(8,128)(2,1)}, u32[]{:S(2)}, u32[]{:S(2)}) collective-permute-start(bf16[2,264,256]{2,1,0:T(8,128)(2,1)S(1)} %collective-permute-done.3.refs_2_.refs_18_), channel_id=1, source_target_pairs={{0,32},{32,0},{1,33},{33,1},{2,34},{34,2},{3,35},{35,3},{4,36},{36... | collective-permute-start | bytes 811016 | tf_op jit(solution)/shard_map/ppermute | solution.py:574
  56.2 6.2 %collective-permute-start.13 = (bf16[2,264,256]{2,1,0:T(8,128)(2,1)S(1)}, bf16[2,264,256]{2,1,0:T(8,128)(2,1)}, u32[]{:S(2)}, u32[]{:S(2)}) collective-permute-start(bf16[2,264,256]{2,1,0:T(8,128)(2,1)S(1)} %collective-permute-done.5.refs_4_.refs_20_.refs_3_), channel_id=1, source_target_pairs={{0,32},{32,0},{1,33},{33,1},{2,34},{34,2},{3,35},{35,3},{4,36},{36... | collective-permute-start | bytes 811016 | tf_op jit(solution)/shard_map/ppermute | solution.py:574
  56.8 1.4 copy-start.20
  56.8 5.7 %collective-permute-start.14 = (bf16[2,264,256]{2,1,0:T(8,128)(2,1)}, bf16[2,264,256]{2,1,0:T(8,128)(2,1)S(1)}, u32[]{:S(2)}, u32[]{:S(2)}) collective-permute-start(bf16[2,264,256]{2,1,0:T(8,128)(2,1)} %copy-done.19), channel_id=1, source_target_pairs={{0,32},{32,0},{1,33},{33,1},{2,34},{34,2},{3,35},{35,3},{4,36},{36... | collective-permute-start | bytes 811016 | tf_op jit(solution)/shard_map/ppermute | solution.py:574
  57.2 1.0 copy-start.21
  57.2 5.3 %collective-permute-start.12 = (bf16[2,264,256]{2,1,0:T(8,128)(2,1)S(1)}, bf16[2,264,256]{2,1,0:T(8,128)(2,1)}, u32[]{:S(2)}, u32[]{:S(2)}) collective-permute-start(bf16[2,264,256]{2,1,0:T(8,128)(2,1)S(1)} %copy-done.12), channel_id=1, source_target_pairs={{0,32},{32,0},{1,33},{33,1},{2,34},{34,2},{3,35},{35,3},{4,36},{36... | collective-permute-start | bytes 811016 | tf_op jit(solution)/shard_map/ppermute | solution.py:574
  58.1 0.7 copy-start.22
  58.8 3.6 %collective-permute-start.16 = (bf16[2,264,256]{2,1,0:T(8,128)(2,1)}, bf16[2,264,256]{2,1,0:T(8,128)(2,1)}, u32[]{:S(2)}, u32[]{:S(2)}) collective-permute-start(bf16[2,264,256]{2,1,0:T(8,128)(2,1)} %copy-done.13), channel_id=1, source_target_pairs={{0,32},{32,0},{1,33},{33,1},{2,34},{34,2},{3,35},{35,3},{4,36},{36... | collective-permute-start | bytes 811016 | tf_op jit(solution)/shard_map/ppermute | solution.py:574
  62.5 0.7 copy-start.23
  83.1 1.4 copy-start.9
  84.5 18.0 %copy-start.17 = (bf16[256,64]{0,1:T(8,128)(2,1)S(1)}, bf16[256,64]{0,1:T(8,128)(2,1)}, u32[]{:S(2)}) copy-start(bf16[256,64]{0,1:T(8,128)(2,1)} %param.20) | copy-start | bytes 98308
  84.5 22.3 %copy-start.3 = (bf16[256,1024]{1,0:T(8,128)(2,1)S(1)}, bf16[256,1024]{1,0:T(8,128)(2,1)}, u32[]{:S(2)}) copy-start(bf16[256,1024]{1,0:T(8,128)(2,1)} %w_ref.1) | copy-start | bytes 1572868
  84.5 22.3 %copy-start.8 = (bf16[256,256]{1,0:T(8,128)(2,1)S(1)}, bf16[256,256]{1,0:T(8,128)(2,1)}, u32[]{:S(2)}) copy-start(bf16[256,256]{1,0:T(8,128)(2,1)} %wo_ref.1) | copy-start | bytes 393220
  96.8 8.0 %collective-permute-start.17 = (bf16[264,256]{1,0:T(8,128)(2,1)}, bf16[264,256]{1,0:T(8,128)(2,1)S(1)}, u32[]{:S(2)}, u32[]{:S(2)}) collective-permute-start(bf16[264,256]{1,0:T(8,128)(2,1)} %row_attention.1.x0_ref), channel_id=1, source_target_pairs={{0,24},{8,16},{16,8},{24,0},{1,25},{9,17},{17,9},{25,1},{2,26},{10... | collective-permute-start | bytes 405512 | tf_op jit(solution)/shard_map/ppermute | solution.py:579
  98.8 6.1 %collective-permute-start.18 = (bf16[264,256]{1,0:T(8,128)(2,1)}, bf16[264,256]{1,0:T(8,128)(2,1)S(1)}, u32[]{:S(2)}, u32[]{:S(2)}) collective-permute-start(bf16[264,256]{1,0:T(8,128)(2,1)} %row_attention.1.x0_ref), channel_id=1, source_target_pairs={{0,16},{8,24},{16,0},{24,8},{1,17},{9,25},{17,1},{25,9},{2,18},{10... | collective-permute-start | bytes 405512 | tf_op jit(solution)/shard_map/ppermute | solution.py:579
  100.3 6.4 %collective-permute-start.19 = (bf16[264,256]{1,0:T(8,128)(2,1)}, bf16[264,256]{1,0:T(8,128)(2,1)S(1)}, u32[]{:S(2)}, u32[]{:S(2)}) collective-permute-start(bf16[264,256]{1,0:T(8,128)(2,1)} %row_attention.1.x0_ref), channel_id=1, source_target_pairs={{0,8},{8,0},{16,24},{24,16},{1,9},{9,1},{17,25},{25,17},{2,10},{10... | collective-permute-start | bytes 405512 | tf_op jit(solution)/shard_map/ppermute | solution.py:579
  106.7 0.9 copy-start.7
  107.6 19.2 %copy-start.14 = (bf16[1024,128]{1,0:T(8,128)(2,1)S(1)}, bf16[1024,128]{1,0:T(8,128)(2,1)}, u32[]{:S(2)}) copy-start(bf16[1024,128]{1,0:T(8,128)(2,1)} %param.21) | copy-start | bytes 786436
  116.0 18.3 %all-to-all-start.1 = ((bf16[8,64,640]{2,1,0:T(8,128)(2,1)}), bf16[8,64,640]{2,1,0:T(8,128)(2,1)S(1)}, u32[]{:S(2)}, u32[]{:S(2)}) async-start(bf16[8,64,640]{2,1,0:T(8,128)(2,1)} %get-tuple-element.12), calls=%async_computation.1 | async-start | bytes 1310720 | tf_op jit(solution)/shard_map/all_to_all | solution.py:584
  120.5 13.8 %collective-permute-start.20 = (bf16[448,256]{1,0:T(8,128)(2,1)S(1)}, bf16[448,256]{1,0:T(8,128)(2,1)S(1)}, u32[]{:S(2)}, u32[]{:S(2)}) collective-permute-start(bf16[448,256]{1,0:T(8,128)(2,1)S(1)} %get-tuple-element.13), channel_id=1, source_target_pairs={{0,0},{8,32},{16,64},{24,96},{32,8},{40,40},{48,72},{56,104},{64,1... | collective-permute-start | bytes 688136 | tf_op jit(solution)/shard_map/ppermute | solution.py:52
  134.2 0.7 copy-start.24
  134.2 0.9 copy-start.10

commit v4 on v3

--- a/solution.py
+++ b/solution.py
@@ -30,7 +30,8 @@
 OUTER = 32
 PAIR = 128
 LEFT = ALL_SEQS * OUTER
-CHUNK = SEQS * BLOCK + 8
+FLAG_ROWS = 16
+CHUNK = SEQS * BLOCK + FLAG_ROWS
 MASKED = -1000000000.0
 OTHER = -2000000000.0
 
@@ -94,7 +95,7 @@
     flags = flag_ref[pl.ds(block // 2, 1), :].astype(F32)
     live = filled * jnp.where(block % 2 == 0, flags[:, :BLOCK], flags[:, BLOCK:])
     lines = [jnp.concatenate([part[i : i + 1] for i in range(SEQS)], axis=1) for part in (filled, live)]
-    lines.append(jnp.zeros((6, WIDTH), F32))
+    lines.append(jnp.zeros((FLAG_ROWS - 2, WIDTH), F32))
     out_ref[rows:, :] = jnp.concatenate(lines, axis=0).astype(BF16)
 
 
@@ -220,7 +221,7 @@
 
 def row_keys(parts, wk, wv):
     gathered = pl.BlockSpec((2, BLOCK, WIDTH), lambda s: (0, s, 0))
-    masks = pl.BlockSpec((2, 8, WIDTH), lambda s: (0, SEQS * BLOCK // 8, 0))
+    masks = pl.BlockSpec((2, FLAG_ROWS, WIDTH), lambda s: (0, SEQS * BLOCK // FLAG_ROWS, 0))
     square = pl.BlockSpec((WIDTH, WIDTH), lambda s: (0, 0))
     return pl.pallas_call(
         key_body,
@@ -365,7 +366,7 @@
     mine = mine_ref[0]
     for b in range(4):
         lanes = x_refs[b][SEQS * BLOCK :, :].astype(F32)
-        masks[:, b * 128 : b * 128 + 8] = lanes.T
+        masks[:, b * 128 : b * 128 + FLAG_ROWS] = lanes.T
     one_row = iota((PART_ROWS, PART_ROWS), 0)
     one_col = iota((PART_ROWS, PART_ROWS), 1)
     same = (one_row % PART) == (one_col % PART)

time: 151 us -> 152 us (level)
  no operation moved by 1% of the time
where the time goes in v4:
time: 152 us; the launch traced here: 151 us
  Pallas kernels  66.5 us (44%)
  starting transfers between devices  41.9 us (28%)
  waiting for transfers between devices  28.5 us (19%)
  local copies, waits for them, and re-layouts  12.9 us (8%)
    pallas_call x3, Pallas kernels, bias_blocks(): pl.pallas_call(bias_body, grid=(steps,), in_specs=[pl.BlockSpec((BIAS_STE...  19.3 us
    pallas_call x1, Pallas kernels, pair_update(): pl.pallas_call(pair_body, grid=(steps + 1,), in_specs=[pl.BlockSpec((PAIR...  15.2 us
    ppermute x3, starting transfers between devices, swap(): return lax.ppermute(array, SWAPPED, swap_pairs(flip))  14.4 us
    pallas_call x1, Pallas kernels, row_attention(): pl.pallas_call(row_body, grid=(SEQS + 1,), in_specs=[pl.BlockSpec(memory_...  12.5 us
    all_to_all x1, waiting for transfers between devices, per_device(): biases = [lax.all_to_all(send.reshape((32,) + send.shape[2:]), RES, 0, 0)]  12.3 us
    unnamed x52, local copies, waits for them, and re-layouts  9.39 us
    ppermute x7, starting transfers between devices, shift(): lax.ppermute(array, NEAR, [(z * 4 + i, (z ^ flip) * 4 + (i + step) % 4) f...  8.44 us
    pallas_call x1, Pallas kernels, column_attention(): pl.pallas_call(column_body, in_specs=[pl.BlockSpec(memory_space=pltpu.SME...  8.32 us
  transfers between devices with their start and end apart: 23, of which 9 were waited for; matrix products, arithmetic and copies ran while one was open for 3% of the time, Pallas kernels for 18%

profile of v4, /device:TPU:1, one launch (start us, length us, event | category | flops | bytes accessed | tf_op | source)
XLA Modules:
  0.0 151.2 jit_solution(3548179276345756717)
XLA Ops:
  0.6 0.0 copy-start
  0.7 1.7 %pack_lineup.1 = bf16[272,256]{1,0:T(8,128)(2,1)} custom-call(s32[1]{0:T(128)} %bitcast.5.block_ref, bf16[256,256]{1,0:T(8,128)(2,1)} %bitcast.29, s32[4,64]{1,0:T(4,128)} %filled_ref.1, s32[16,128]{1,0:T(8,128)} %bitcast.31), custom_call_target="tpu_custom_call" | custom-call | tf_op jit(solution)/shard_map/pack_lineup/pallas_call | solution.py:104
  2.4 6.9 %collective-permute-start = (bf16[272,256]{1,0:T(8,128)(2,1)}, bf16[272,256]{1,0:T(8,128)(2,1)S(1)}, u32[]{:S(2)}, u32[]{:S(2)}) collective-permute-start(bf16[272,256]{1,0:T(8,128)(2,1)} %pack_lineup.1), channel_id=1, source_target_pairs={{0,0},{8,32},{16,64},{24,96},{32,8},{40,40},{48,72},{56,104},{64,1... | collective-permute-start | bytes 417800 | tf_op jit(solution)/shard_map/ppermute | solution.py:53
  9.3 1.2 collective-permute-start.1
  10.5 0.1 copy.21.weight_ref
  10.6 5.5 %pair_bias.3.after_ref.refs_0_ = bf16[4,8,64,512]{3,2,1,0:T(8,128)(2,1)} custom-call(bf16[512,64,128]{2,1,0:T(8,128)(2,1)} %pair_ref.7, bf16[128,256]{1,0:T(8,128)(2,1)S(1)} %copy.21.weight_ref), custom_call_target="tpu_custom_call" | custom-call | flops 8589934592 | bytes 6291456 | tf_op jit(solution)/shard_map/pair_bias/pallas_call | solution.py:177
  16.1 0.0 collective-permute-done.x_ref
  16.1 1.8 %collective-permute-done.1.flipped_ref = bf16[272,256]{1,0:T(8,128)(2,1)S(1)} collective-permute-done((bf16[272,256]{1,0:T(8,128)(2,1)}, bf16[272,256]{1,0:T(8,128)(2,1)S(1)}, u32[]{:S(2)}, u32[]{:S(2)}) %collective-permute-start.1) | collective-permute-done | bytes 139296 | tf_op jit(solution)/shard_map/ppermute | solution.py:53
  18.0 0.7 copy-done.16
  18.6 1.9 %norm_lineup.1.refs_0_.refs_16_.refs_1_.own_ref = bf16[2,272,256]{2,1,0:T(8,128)(2,1)} custom-call(bf16[272,256]{1,0:T(8,128)(2,1)} %copy-done.15, bf16[272,256]{1,0:T(8,128)(2,1)} %copy-done.16, bf16[4,8,64,512]{3,2,1,0:T(8,128)(2,1)} %pair_bias.3.after_ref.refs_0_), custom_call_target="tpu_custom_call" | custom-call | tf_op jit(solution)/shard_map/norm_lineup/pallas_call | solution.py:122
  20.5 1.2 collective-permute-start.2
  21.8 1.9 %collective-permute-start.7 = (bf16[2,272,256]{2,1,0:T(8,128)(2,1)}, bf16[2,272,256]{2,1,0:T(8,128)(2,1)S(1)}, u32[]{:S(2)}, u32[]{:S(2)}) collective-permute-start(bf16[2,272,256]{2,1,0:T(8,128)(2,1)} %norm_lineup.1.refs_0_.refs_16_.refs_1_.own_ref), channel_id=1, source_target_pairs={{0,7},{1,4},{2,5},{3,6},{4,3},{5,0},{6,1},{7,2},{8,15},{9,12},{10,... | collective-permute-start | bytes 835592 | tf_op jit(solution)/shard_map/ppermute | solution.py:57
  23.7 1.3 collective-permute-start.3
  24.9 0.7 collective-permute-start.5
  25.7 0.7 collective-permute-start.6
  26.3 1.0 copy-done.1
  27.3 8.3 %pair_bias.4.refs_0_ = bf16[4,8,64,512]{3,2,1,0:T(8,128)(2,1)} custom-call(bf16[512,64,128]{2,1,0:T(8,128)(2,1)} %pair_ref.7, bf16[128,256]{1,0:T(8,128)(2,1)S(1)} %copy.21.weight_ref, bf16[4,8,64,512]{3,2,1,0:T(8,128)(2,1)} %pair_bias.3.after_ref.refs_0_, bf16[2,272,256]{2,1,0:T(8,128)(2,1)S(1)} %copy-done.1), custom_call_target="tpu_custom_call", output_to_operand_aliasing={{}: (2, {})} | custom-call | flops 8589934592 | bytes 6291456 | tf_op jit(solution)/shard_map/pair_bias/pallas_call | solution.py:177
  35.6 0.0 collective-permute-start.4
  35.7 2.7 %collective-permute-start.8 = (bf16[2,272,256]{2,1,0:T(8,128)(2,1)S(1)}, bf16[2,272,256]{2,1,0:T(8,128)(2,1)S(1)}, u32[]{:S(2)}, u32[]{:S(2)}) collective-permute-start(bf16[2,272,256]{2,1,0:T(8,128)(2,1)S(1)} %collective-permute-done.7.refs_6_.refs_22_.refs_5_), channel_id=1, source_target_pairs={{0,3},{1,0},{2,1},{3,2},{4,7},{5,4},{6,5},{7,6},{8,11},{9,8},{10,9... | collective-permute-start | bytes 835592 | tf_op jit(solution)/shard_map/ppermute | solution.py:57
  38.3 3.3 %collective-permute-done.5.refs_4_.refs_20_.refs_3_ = bf16[2,272,256]{2,1,0:T(8,128)(2,1)S(1)} collective-permute-done((bf16[2,272,256]{2,1,0:T(8,128)(2,1)}, bf16[2,272,256]{2,1,0:T(8,128)(2,1)S(1)}, u32[]{:S(2)}, u32[]{:S(2)}) %collective-permute-start.5) | collective-permute-done | bytes 278560 | tf_op jit(solution)/shard_map/ppermute | solution.py:57
  41.6 0.8 copy-done.19
  42.4 5.5 %pair_bias.5.refs_0_ = bf16[4,8,64,512]{3,2,1,0:T(8,128)(2,1)} custom-call(bf16[512,64,128]{2,1,0:T(8,128)(2,1)} %pair_ref.7, bf16[128,256]{1,0:T(8,128)(2,1)S(1)} %copy.21.weight_ref, bf16[4,8,64,512]{3,2,1,0:T(8,128)(2,1)} %pair_bias.4.refs_0_, bf16[2,272,256]{2,1,0:T(8,128)(2,1)S(1)} %collective-permute-done.2.refs_1_.refs_17_, ...), custom_call_target="tpu_custom_call", output_to_operand_aliasing={{}: (2, {})} | custom-call | flops 8589934592 | bytes 6291456 | tf_op jit(solution)/shard_map/pair_bias/pallas_call | solution.py:177
  47.9 0.7 copy-done.11
  48.6 0.7 copy-done.13
  49.3 5.9 %all-to-all-start = ((bf16[32,64,512]{2,1,0:T(8,128)(2,1)}), bf16[32,64,512]{2,1,0:T(8,128)(2,1)S(1)}, u32[]{:S(2)}, u32[]{:S(2)}) async-start(bf16[32,64,512]{2,1,0:T(8,128)(2,1)} %bitcast.22), calls=%async_computation | async-start | bytes 4194304 | tf_op jit(solution)/shard_map/all_to_all | solution.py:576
  55.3 0.9 collective-permute-start.9
  56.1 0.1 collective-permute-start.10
  56.2 0.4 collective-permute-start.15
  56.7 0.1 collective-permute-start.11
  56.8 0.4 collective-permute-start.13
  57.2 0.2 collective-permute-done.9.refs_8_.refs_24_
  57.3 0.4 collective-permute-start.14
  57.7 0.0 collective-permute-done.10.refs_9_.refs_25_
  57.7 0.4 collective-permute-start.12
  58.1 0.6 collective-permute-done.15.refs_14_.refs_30_
  58.7 0.7 copy-done.22
  59.4 0.4 collective-permute-start.16
  59.8 1.8 %fusion = (bf16[256,256]{1,0:T(8,128)(2,1)}, bf16[256,256]{1,0:T(8,128)(2,1)S(1)}, bf16[256,256]{1,0:T(8,128)(2,1)}, bf16[256,256]{1,0:T(8,128)(2,1)}) fusion(bf16[256,1024]{1,0:T(8,128)(2,1)} %param.15), kind=kLoop, calls=%fused_computation.3 | loop fusion | bytes 1048576 | tf_op jit(solution)/shard_map/slice | solution.py:577
  61.7 0.7 copy.28
  62.4 0.7 pad_add_fusion.spot_ref
  63.1 0.7 copy-done.23
  63.8 7.6 %row_keys.1 = (bf16[4,2048,256]{2,1,0:T(8,128)(2,1)}, bf16[4,256,2048]{2,1,0:T(8,128)(2,1)}, f32[256,128]{1,0:T(8,128)}) custom-call(bf16[2,272,256]{2,1,0:T(8,128)(2,1)} %norm_lineup.1.refs_0_.refs_16_.refs_1_.own_ref, bf16[2,272,256]{2,1,0:T(8,128)(2,1)} %copy-done.4, bf16[2,272,256]{2,1,0:T(8,128)(2,1)} %copy-done.5, bf16[2,272,256]{2,1,0:T(8,128)(2,1)} %copy-done.11, ...), custom_call_target="tpu_custom_call" | custom-call | flops 4294967296 | bytes 12582912 | tf_op jit(solution)/shard_map/row_keys/pallas_call | solution.py:226
  71.3 12.3 %all-to-all-done.refs_0_ = bf16[32,64,512]{2,1,0:T(8,128)(2,1)S(1)} async-done(((bf16[32,64,512]{2,1,0:T(8,128)(2,1)}), bf16[32,64,512]{2,1,0:T(8,128)(2,1)S(1)}, u32[]{:S(2)}, u32[]{:S(2)}) %all-to-all-start) | async-done | bytes 2097184 | tf_op jit(solution)/shard_map/all_to_all | solution.py:576
  83.7 1.4 copy-done.9
  85.0 12.5 %row_attention.1.x0_ref = bf16[272,256]{1,0:T(8,128)(2,1)} custom-call(s32[4]{0:T(128)} %pad_add_fusion.spot_ref, bf16[2,272,256]{2,1,0:T(8,128)(2,1)} %norm_lineup.1.refs_0_.refs_16_.refs_1_.own_ref, bf16[272,256]{1,0:T(8,128)(2,1)} %copy-done.15, bf16[4,2048,256]{2,1,0:T(8,128)(2,1)} %get-tuple-element.9.key_ref, ...), custom_call_target="tpu_custom_call" | custom-call | flops 12884901888 | bytes 12582912 | tf_op jit(solution)/shard_map/row_attention/pallas_call | solution.py:329
  97.5 2.0 %collective-permute-start.17 = (bf16[272,256]{1,0:T(8,128)(2,1)}, bf16[272,256]{1,0:T(8,128)(2,1)S(1)}, u32[]{:S(2)}, u32[]{:S(2)}) collective-permute-start(bf16[272,256]{1,0:T(8,128)(2,1)} %row_attention.1.x0_ref), channel_id=1, source_target_pairs={{0,24},{8,16},{16,8},{24,0},{1,25},{9,17},{17,9},{25,1},{2,26},{10... | collective-permute-start | bytes 417800 | tf_op jit(solution)/shard_map/ppermute | solution.py:580
  99.5 1.5 collective-permute-start.18
  101.0 2.1 %collective-permute-start.19 = (bf16[272,256]{1,0:T(8,128)(2,1)}, bf16[272,256]{1,0:T(8,128)(2,1)S(1)}, u32[]{:S(2)}, u32[]{:S(2)}) collective-permute-start(bf16[272,256]{1,0:T(8,128)(2,1)} %row_attention.1.x0_ref), channel_id=1, source_target_pairs={{0,8},{8,0},{16,24},{24,16},{1,9},{9,1},{17,25},{25,17},{2,10},{10... | collective-permute-start | bytes 417800 | tf_op jit(solution)/shard_map/ppermute | solution.py:580
  103.2 0.1 copy.25.left_ref
  103.4 0.1 copy.26.right_ref
  103.5 2.0 %collective-permute-done.17.x3_ref = bf16[272,256]{1,0:T(8,128)(2,1)S(1)} collective-permute-done((bf16[272,256]{1,0:T(8,128)(2,1)}, bf16[272,256]{1,0:T(8,128)(2,1)S(1)}, u32[]{:S(2)}, u32[]{:S(2)}) %collective-permute-start.17) | collective-permute-done | bytes 139296 | tf_op jit(solution)/shard_map/ppermute | solution.py:580
  105.5 0.1 collective-permute-done.18.x2_ref
  105.7 1.9 %collective-permute-done.19.x1_ref = bf16[272,256]{1,0:T(8,128)(2,1)S(1)} collective-permute-done((bf16[272,256]{1,0:T(8,128)(2,1)}, bf16[272,256]{1,0:T(8,128)(2,1)S(1)}, u32[]{:S(2)}, u32[]{:S(2)}) %collective-permute-start.19) | collective-permute-done | bytes 139296 | tf_op jit(solution)/shard_map/ppermute | solution.py:580
  107.6 0.9 copy-done.7
  108.5 8.3 %column_attention.1 = (bf16[448,256]{1,0:T(8,128)(2,1)S(1)}, bf16[8,64,640]{2,1,0:T(8,128)(2,1)}) custom-call(s32[1]{0:T(128)} %bitcast.mine_ref, bf16[272,256]{1,0:T(8,128)(2,1)S(1)} %copy-done.7, bf16[272,256]{1,0:T(8,128)(2,1)S(1)} %collective-permute-done.17.x3_ref, bf16[272,256]{1,0:T(8,128)(2,1)S(1)} %collective-permute-done.18.x2_ref, ...), custom_call_target="tpu_custom_call" | custom-call | flops 4294967296 | bytes 3145728 | tf_op jit(solution)/shard_map/column_attention/pallas_call | solution.py:429
  116.8 4.5 %all-to-all-start.1 = ((bf16[8,64,640]{2,1,0:T(8,128)(2,1)}), bf16[8,64,640]{2,1,0:T(8,128)(2,1)S(1)}, u32[]{:S(2)}, u32[]{:S(2)}) async-start(bf16[8,64,640]{2,1,0:T(8,128)(2,1)} %get-tuple-element.12), calls=%async_computation.1 | async-start | bytes 1310720 | tf_op jit(solution)/shard_map/all_to_all | solution.py:585
  121.3 6.3 %collective-permute-start.20 = (bf16[448,256]{1,0:T(8,128)(2,1)S(1)}, bf16[448,256]{1,0:T(8,128)(2,1)S(1)}, u32[]{:S(2)}, u32[]{:S(2)}) collective-permute-start(bf16[448,256]{1,0:T(8,128)(2,1)S(1)} %get-tuple-element.13), channel_id=1, source_target_pairs={{0,0},{8,32},{16,64},{24,96},{32,8},{40,40},{48,72},{56,104},{64,1... | collective-permute-start | bytes 688136 | tf_op jit(solution)/shard_map/ppermute | solution.py:53
  127.6 0.1 copy.27
  127.7 0.1 copy.31
  127.8 1.1 pad.4.w_ref
  128.9 6.1 %collective-permute-done.20.b_ref = bf16[448,256]{1,0:T(8,128)(2,1)S(1)} collective-permute-done((bf16[448,256]{1,0:T(8,128)(2,1)S(1)}, bf16[448,256]{1,0:T(8,128)(2,1)S(1)}, u32[]{:S(2)}, u32[]{:S(2)}) %collective-permute-start.20) | collective-permute-done | bytes 229408 | tf_op jit(solution)/shard_map/ppermute | solution.py:53
  135.0 0.7 copy-done.24
  135.7 0.3 copy-done.10
  136.0 15.2 %pair_update.1 = (bf16[512,64,128]{2,1,0:T(8,128)(2,1)}, bf16[256,256]{1,0:T(8,128)(2,1)}) custom-call(bf16[512,640]{1,0:T(8,128)(2,1)} %bitcast.27, bf16[448,256]{1,0:T(8,128)(2,1)} %copy-done.24, bf16[128,4096]{1,0:T(8,128)(2,1)} %pad.4.w_ref, bf16[512,64,128]{2,1,0:T(8,128)(2,1)} %pair_ref.7), custom_call_target="tpu_custom_call" | custom-call | flops 8589934592 | bytes 18874368 | tf_op jit(solution)/shard_map/pair_update/pallas_call | solution.py:522
  (55 shorter events, 0.2 us)
Async XLA Ops:
  0.6 9.8 %copy-start = (bf16[128,8]{0,1:T(8,128)(2,1)S(1)}, bf16[128,8]{0,1:T(8,128)(2,1)}, u32[]{:S(2)}) copy-start(bf16[128,8]{0,1:T(8,128)(2,1)} %param.17) | copy-start | bytes 6148
  2.4 13.7 %collective-permute-start = (bf16[272,256]{1,0:T(8,128)(2,1)}, bf16[272,256]{1,0:T(8,128)(2,1)S(1)}, u32[]{:S(2)}, u32[]{:S(2)}) collective-permute-start(bf16[272,256]{1,0:T(8,128)(2,1)} %pack_lineup.1), channel_id=1, source_target_pairs={{0,0},{8,32},{16,64},{24,96},{32,8},{40,40},{48,72},{56,104},{64,1... | collective-permute-start | bytes 417800 | tf_op jit(solution)/shard_map/ppermute | solution.py:53
  9.3 8.7 %collective-permute-start.1 = (bf16[272,256]{1,0:T(8,128)(2,1)}, bf16[272,256]{1,0:T(8,128)(2,1)S(1)}, u32[]{:S(2)}, u32[]{:S(2)}) collective-permute-start(bf16[272,256]{1,0:T(8,128)(2,1)} %pack_lineup.1), channel_id=1, source_target_pairs={{0,64},{8,96},{16,0},{24,32},{32,72},{40,104},{48,8},{56,40},{64,8... | collective-permute-start | bytes 417800 | tf_op jit(solution)/shard_map/ppermute | solution.py:53
  16.1 1.8 %copy-start.15 = (bf16[272,256]{1,0:T(8,128)(2,1)}, bf16[272,256]{1,0:T(8,128)(2,1)S(1)}, u32[]{:S(2)}) copy-start(bf16[272,256]{1,0:T(8,128)(2,1)S(1)} %collective-permute-done.x_ref) | copy-start | bytes 417796
  18.0 0.7 copy-start.16
  20.5 15.1 %collective-permute-start.2 = (bf16[2,272,256]{2,1,0:T(8,128)(2,1)}, bf16[2,272,256]{2,1,0:T(8,128)(2,1)S(1)}, u32[]{:S(2)}, u32[]{:S(2)}) collective-permute-start(bf16[2,272,256]{2,1,0:T(8,128)(2,1)} %norm_lineup.1.refs_0_.refs_16_.refs_1_.own_ref), channel_id=1, source_target_pairs={{0,1},{1,2},{2,3},{3,0},{4,5},{5,6},{6,7},{7,4},{8,9},{9,10},{10,1... | collective-permute-start | bytes 835592 | tf_op jit(solution)/shard_map/ppermute | solution.py:57
  21.8 13.9 %collective-permute-start.7 = (bf16[2,272,256]{2,1,0:T(8,128)(2,1)}, bf16[2,272,256]{2,1,0:T(8,128)(2,1)S(1)}, u32[]{:S(2)}, u32[]{:S(2)}) collective-permute-start(bf16[2,272,256]{2,1,0:T(8,128)(2,1)} %norm_lineup.1.refs_0_.refs_16_.refs_1_.own_ref), channel_id=1, source_target_pairs={{0,7},{1,4},{2,5},{3,6},{4,3},{5,0},{6,1},{7,2},{8,15},{9,12},{10,... | collective-permute-start | bytes 835592 | tf_op jit(solution)/shard_map/ppermute | solution.py:57
  23.7 14.6 %collective-permute-start.3 = (bf16[2,272,256]{2,1,0:T(8,128)(2,1)}, bf16[2,272,256]{2,1,0:T(8,128)(2,1)S(1)}, u32[]{:S(2)}, u32[]{:S(2)}) collective-permute-start(bf16[2,272,256]{2,1,0:T(8,128)(2,1)} %norm_lineup.1.refs_0_.refs_16_.refs_1_.own_ref), channel_id=1, source_target_pairs={{0,3},{1,0},{2,1},{3,2},{4,7},{5,4},{6,5},{7,6},{8,11},{9,8},{10,9... | collective-permute-start | bytes 835592 | tf_op jit(solution)/shard_map/ppermute | solution.py:57
  24.9 16.6 %collective-permute-start.5 = (bf16[2,272,256]{2,1,0:T(8,128)(2,1)}, bf16[2,272,256]{2,1,0:T(8,128)(2,1)S(1)}, u32[]{:S(2)}, u32[]{:S(2)}) collective-permute-start(bf16[2,272,256]{2,1,0:T(8,128)(2,1)} %norm_lineup.1.refs_0_.refs_16_.refs_1_.own_ref), channel_id=1, source_target_pairs={{0,4},{1,5},{2,6},{3,7},{4,0},{5,1},{6,2},{7,3},{8,12},{9,13},{10,... | collective-permute-start | bytes 835592 | tf_op jit(solution)/shard_map/ppermute | solution.py:57
  25.7 15.9 %collective-permute-start.6 = (bf16[2,272,256]{2,1,0:T(8,128)(2,1)}, bf16[2,272,256]{2,1,0:T(8,128)(2,1)S(1)}, u32[]{:S(2)}, u32[]{:S(2)}) collective-permute-start(bf16[2,272,256]{2,1,0:T(8,128)(2,1)} %norm_lineup.1.refs_0_.refs_16_.refs_1_.own_ref), channel_id=1, source_target_pairs={{0,5},{1,6},{2,7},{3,4},{4,1},{5,2},{6,3},{7,0},{8,13},{9,14},{10,... | collective-permute-start | bytes 835592 | tf_op jit(solution)/shard_map/ppermute | solution.py:57
  26.3 1.0 copy-start.1
  35.6 20.5 %copy-start.4 = (bf16[2,272,256]{2,1,0:T(8,128)(2,1)}, bf16[2,272,256]{2,1,0:T(8,128)(2,1)S(1)}, u32[]{:S(2)}) copy-start(bf16[2,272,256]{2,1,0:T(8,128)(2,1)S(1)} %collective-permute-done.2.refs_1_.refs_17_) | copy-start | bytes 835588
  35.6 12.2 %collective-permute-start.4 = (bf16[2,272,256]{2,1,0:T(8,128)(2,1)S(1)}, bf16[2,272,256]{2,1,0:T(8,128)(2,1)S(1)}, u32[]{:S(2)}, u32[]{:S(2)}) collective-permute-start(bf16[2,272,256]{2,1,0:T(8,128)(2,1)S(1)} %collective-permute-done.2.refs_1_.refs_17_), channel_id=1, source_target_pairs={{0,1},{1,2},{2,3},{3,0},{4,5},{5,6},{6,7},{7,4},{8,9},{9,10},{10,1... | collective-permute-start | bytes 835592 | tf_op jit(solution)/shard_map/ppermute | solution.py:57
  35.6 5.9 %copy-start.18 = (bf16[2,272,256]{2,1,0:T(8,128)(2,1)}, bf16[2,272,256]{2,1,0:T(8,128)(2,1)S(1)}, u32[]{:S(2)}) copy-start(bf16[2,272,256]{2,1,0:T(8,128)(2,1)S(1)} %collective-permute-done.7.refs_6_.refs_22_.refs_5_) | copy-start | bytes 835588
  35.7 12.2 %collective-permute-start.8 = (bf16[2,272,256]{2,1,0:T(8,128)(2,1)S(1)}, bf16[2,272,256]{2,1,0:T(8,128)(2,1)S(1)}, u32[]{:S(2)}, u32[]{:S(2)}) collective-permute-start(bf16[2,272,256]{2,1,0:T(8,128)(2,1)S(1)} %collective-permute-done.7.refs_6_.refs_22_.refs_5_), channel_id=1, source_target_pairs={{0,3},{1,0},{2,1},{3,2},{4,7},{5,4},{6,5},{7,6},{8,11},{9,8},{10,9... | collective-permute-start | bytes 835592 | tf_op jit(solution)/shard_map/ppermute | solution.py:57
  38.3 18.3 %copy-start.5 = (bf16[2,272,256]{2,1,0:T(8,128)(2,1)}, bf16[2,272,256]{2,1,0:T(8,128)(2,1)S(1)}, u32[]{:S(2)}) copy-start(bf16[2,272,256]{2,1,0:T(8,128)(2,1)S(1)} %collective-permute-done.3.refs_2_.refs_18_) | copy-start | bytes 835588
  41.6 15.2 %copy-start.6 = (bf16[2,272,256]{2,1,0:T(8,128)(2,1)}, bf16[2,272,256]{2,1,0:T(8,128)(2,1)S(1)}, u32[]{:S(2)}) copy-start(bf16[2,272,256]{2,1,0:T(8,128)(2,1)S(1)} %collective-permute-done.5.refs_4_.refs_20_.refs_3_) | copy-start | bytes 835588
  41.6 0.8 copy-start.19
  47.9 0.7 copy-start.11
  48.6 0.7 copy-start.13
  49.3 6.0 %copy-start.2 = (bf16[2,272,256]{2,1,0:T(8,128)(2,1)S(1)}, bf16[2,272,256]{2,1,0:T(8,128)(2,1)}, u32[]{:S(2)}) copy-start(bf16[2,272,256]{2,1,0:T(8,128)(2,1)} %norm_lineup.1.refs_0_.refs_16_.refs_1_.own_ref) | copy-start | bytes 835588
  49.3 8.4 %copy-start.12 = (bf16[2,272,256]{2,1,0:T(8,128)(2,1)S(1)}, bf16[2,272,256]{2,1,0:T(8,128)(2,1)}, u32[]{:S(2)}) copy-start(bf16[2,272,256]{2,1,0:T(8,128)(2,1)} %copy-done.11) | copy-start | bytes 835588
  49.3 34.3 %all-to-all-start = ((bf16[32,64,512]{2,1,0:T(8,128)(2,1)}), bf16[32,64,512]{2,1,0:T(8,128)(2,1)S(1)}, u32[]{:S(2)}, u32[]{:S(2)}) async-start(bf16[32,64,512]{2,1,0:T(8,128)(2,1)} %bitcast.22), calls=%async_computation | async-start | bytes 4194304 | tf_op jit(solution)/shard_map/all_to_all | solution.py:576
  55.3 2.0 %collective-permute-start.9 = (bf16[2,272,256]{2,1,0:T(8,128)(2,1)S(1)}, bf16[2,272,256]{2,1,0:T(8,128)(2,1)S(1)}, u32[]{:S(2)}, u32[]{:S(2)}) collective-permute-start(bf16[2,272,256]{2,1,0:T(8,128)(2,1)S(1)} %copy-done.2), channel_id=1, source_target_pairs={{0,32},{32,0},{1,33},{33,1},{2,34},{34,2},{3,35},{35,3},{4,36},{36... | collective-permute-start | bytes 835592 | tf_op jit(solution)/shard_map/ppermute | solution.py:575
  56.1 1.6 %collective-permute-start.10 = (bf16[2,272,256]{2,1,0:T(8,128)(2,1)S(1)}, bf16[2,272,256]{2,1,0:T(8,128)(2,1)S(1)}, u32[]{:S(2)}, u32[]{:S(2)}) collective-permute-start(bf16[2,272,256]{2,1,0:T(8,128)(2,1)S(1)} %collective-permute-done.2.refs_1_.refs_17_), channel_id=1, source_target_pairs={{0,32},{32,0},{1,33},{33,1},{2,34},{34,2},{3,35},{35,3},{4,36},{36... | collective-permute-start | bytes 835592 | tf_op jit(solution)/shard_map/ppermute | solution.py:575
  56.2 2.5 %collective-permute-start.15 = (bf16[2,272,256]{2,1,0:T(8,128)(2,1)}, bf16[2,272,256]{2,1,0:T(8,128)(2,1)S(1)}, u32[]{:S(2)}, u32[]{:S(2)}) collective-permute-start(bf16[2,272,256]{2,1,0:T(8,128)(2,1)} %copy-done.18), channel_id=1, source_target_pairs={{0,32},{32,0},{1,33},{33,1},{2,34},{34,2},{3,35},{35,3},{4,36},{36... | collective-permute-start | bytes 835592 | tf_op jit(solution)/shard_map/ppermute | solution.py:575
  56.7 6.4 %collective-permute-start.11 = (bf16[2,272,256]{2,1,0:T(8,128)(2,1)S(1)}, bf16[2,272,256]{2,1,0:T(8,128)(2,1)}, u32[]{:S(2)}, u32[]{:S(2)}) collective-permute-start(bf16[2,272,256]{2,1,0:T(8,128)(2,1)S(1)} %collective-permute-done.3.refs_2_.refs_18_), channel_id=1, source_target_pairs={{0,32},{32,0},{1,33},{33,1},{2,34},{34,2},{3,35},{35,3},{4,36},{36... | collective-permute-start | bytes 835592 | tf_op jit(solution)/shard_map/ppermute | solution.py:575
  56.8 6.3 %collective-permute-start.13 = (bf16[2,272,256]{2,1,0:T(8,128)(2,1)S(1)}, bf16[2,272,256]{2,1,0:T(8,128)(2,1)}, u32[]{:S(2)}, u32[]{:S(2)}) collective-permute-start(bf16[2,272,256]{2,1,0:T(8,128)(2,1)S(1)} %collective-permute-done.5.refs_4_.refs_20_.refs_3_), channel_id=1, source_target_pairs={{0,32},{32,0},{1,33},{33,1},{2,34},{34,2},{3,35},{35,3},{4,36},{36... | collective-permute-start | bytes 835592 | tf_op jit(solution)/shard_map/ppermute | solution.py:575
  57.3 1.4 copy-start.20
  57.3 5.7 %collective-permute-start.14 = (bf16[2,272,256]{2,1,0:T(8,128)(2,1)}, bf16[2,272,256]{2,1,0:T(8,128)(2,1)S(1)}, u32[]{:S(2)}, u32[]{:S(2)}) collective-permute-start(bf16[2,272,256]{2,1,0:T(8,128)(2,1)} %copy-done.19), channel_id=1, source_target_pairs={{0,32},{32,0},{1,33},{33,1},{2,34},{34,2},{3,35},{35,3},{4,36},{36... | collective-permute-start | bytes 835592 | tf_op jit(solution)/shard_map/ppermute | solution.py:575
  57.7 1.0 copy-start.21
  57.7 5.3 %collective-permute-start.12 = (bf16[2,272,256]{2,1,0:T(8,128)(2,1)S(1)}, bf16[2,272,256]{2,1,0:T(8,128)(2,1)}, u32[]{:S(2)}, u32[]{:S(2)}) collective-permute-start(bf16[2,272,256]{2,1,0:T(8,128)(2,1)S(1)} %copy-done.12), channel_id=1, source_target_pairs={{0,32},{32,0},{1,33},{33,1},{2,34},{34,2},{3,35},{35,3},{4,36},{36... | collective-permute-start | bytes 835592 | tf_op jit(solution)/shard_map/ppermute | solution.py:575
  58.7 0.7 copy-start.22
  59.4 3.6 %collective-permute-start.16 = (bf16[2,272,256]{2,1,0:T(8,128)(2,1)}, bf16[2,272,256]{2,1,0:T(8,128)(2,1)}, u32[]{:S(2)}, u32[]{:S(2)}) collective-permute-start(bf16[2,272,256]{2,1,0:T(8,128)(2,1)} %copy-done.13), channel_id=1, source_target_pairs={{0,32},{32,0},{1,33},{33,1},{2,34},{34,2},{3,35},{35,3},{4,36},{36... | collective-permute-start | bytes 835592 | tf_op jit(solution)/shard_map/ppermute | solution.py:575
  63.1 0.7 copy-start.23
  83.7 1.4 copy-start.9
  85.0 18.1 %copy-start.17 = (bf16[256,64]{0,1:T(8,128)(2,1)S(1)}, bf16[256,64]{0,1:T(8,128)(2,1)}, u32[]{:S(2)}) copy-start(bf16[256,64]{0,1:T(8,128)(2,1)} %param.20) | copy-start | bytes 98308
  85.0 22.6 %copy-start.3 = (bf16[256,1024]{1,0:T(8,128)(2,1)S(1)}, bf16[256,1024]{1,0:T(8,128)(2,1)}, u32[]{:S(2)}) copy-start(bf16[256,1024]{1,0:T(8,128)(2,1)} %w_ref.1) | copy-start | bytes 1572868
  85.0 22.6 %copy-start.8 = (bf16[256,256]{1,0:T(8,128)(2,1)S(1)}, bf16[256,256]{1,0:T(8,128)(2,1)}, u32[]{:S(2)}) copy-start(bf16[256,256]{1,0:T(8,128)(2,1)} %wo_ref.1) | copy-start | bytes 393220
  97.5 8.1 %collective-permute-start.17 = (bf16[272,256]{1,0:T(8,128)(2,1)}, bf16[272,256]{1,0:T(8,128)(2,1)S(1)}, u32[]{:S(2)}, u32[]{:S(2)}) collective-permute-start(bf16[272,256]{1,0:T(8,128)(2,1)} %row_attention.1.x0_ref), channel_id=1, source_target_pairs={{0,24},{8,16},{16,8},{24,0},{1,25},{9,17},{17,9},{25,1},{2,26},{10... | collective-permute-start | bytes 417800 | tf_op jit(solution)/shard_map/ppermute | solution.py:580
  99.5 6.1 %collective-permute-start.18 = (bf16[272,256]{1,0:T(8,128)(2,1)}, bf16[272,256]{1,0:T(8,128)(2,1)S(1)}, u32[]{:S(2)}, u32[]{:S(2)}) collective-permute-start(bf16[272,256]{1,0:T(8,128)(2,1)} %row_attention.1.x0_ref), channel_id=1, source_target_pairs={{0,16},{8,24},{16,0},{24,8},{1,17},{9,25},{17,1},{25,9},{2,18},{10... | collective-permute-start | bytes 417800 | tf_op jit(solution)/shard_map/ppermute | solution.py:580
  101.0 6.6 %collective-permute-start.19 = (bf16[272,256]{1,0:T(8,128)(2,1)}, bf16[272,256]{1,0:T(8,128)(2,1)S(1)}, u32[]{:S(2)}, u32[]{:S(2)}) collective-permute-start(bf16[272,256]{1,0:T(8,128)(2,1)} %row_attention.1.x0_ref), channel_id=1, source_target_pairs={{0,8},{8,0},{16,24},{24,16},{1,9},{9,1},{17,25},{25,17},{2,10},{10... | collective-permute-start | bytes 417800 | tf_op jit(solution)/shard_map/ppermute | solution.py:580
  107.6 0.9 copy-start.7
  108.5 19.1 %copy-start.14 = (bf16[1024,128]{1,0:T(8,128)(2,1)S(1)}, bf16[1024,128]{1,0:T(8,128)(2,1)}, u32[]{:S(2)}) copy-start(bf16[1024,128]{1,0:T(8,128)(2,1)} %param.21) | copy-start | bytes 786436
  116.8 18.2 %all-to-all-start.1 = ((bf16[8,64,640]{2,1,0:T(8,128)(2,1)}), bf16[8,64,640]{2,1,0:T(8,128)(2,1)S(1)}, u32[]{:S(2)}, u32[]{:S(2)}) async-start(bf16[8,64,640]{2,1,0:T(8,128)(2,1)} %get-tuple-element.12), calls=%async_computation.1 | async-start | bytes 1310720 | tf_op jit(solution)/shard_map/all_to_all | solution.py:585
  121.3 13.7 %collective-permute-start.20 = (bf16[448,256]{1,0:T(8,128)(2,1)S(1)}, bf16[448,256]{1,0:T(8,128)(2,1)S(1)}, u32[]{:S(2)}, u32[]{:S(2)}) collective-permute-start(bf16[448,256]{1,0:T(8,128)(2,1)S(1)} %get-tuple-element.13), channel_id=1, source_target_pairs={{0,0},{8,32},{16,64},{24,96},{32,8},{40,40},{48,72},{56,104},{64,1... | collective-permute-start | bytes 688136 | tf_op jit(solution)/shard_map/ppermute | solution.py:53
  135.0 0.7 copy-start.24
  135.0 0.9 copy-start.10
